TPU v7x, 128 devices: a whole 4x4x4 slice. The times are simulated.
128 devices in a mesh: layer: 4 (over x_hi, core), example: 32 (over z, x_lo, y).
Axes of the slice: x: 4 (x_hi: 2, x_lo: 2; x = x_hi * 2 + x_lo), y: 4, z: 4, core: 2. Of those that a mesh axis runs over, the one named last changes fastest.
Arguments:
- train_features: bfloat16 [4, 49152, 4096], P('layer', 'example'), may hold values from -0.046875 to 0.046875
- query_codes: bfloat16 [4, 2048, 4096], P('layer', 'example'), may hold values from -512 to 512
- query_exponents: int32 [4, 2048], P('layer', 'example'), may hold values from 6 to 10
Outputs:
- scores: float32 [2048, 49152], P('layer', 'example')
All inputs are finite; a program needn't handle non-finite values.
Results may differ from a plain program's by a relative error of at most 0.0003.
Values may be sent and summed in bfloat16 or wider, within the bound.
No kernel may reach another device: no remote copies, remote signals or barrier semaphores. Data moves between devices by JAX's collectives and lax.ppermute only.
A program may use at most 128 MiB of HBM per device.

v0:
```python
import jax
import jax.numpy as jnp
from jax import lax
from jax.sharding import PartitionSpec as P


def shards(train_features, query_codes, query_exponents):
    row_scale = jnp.exp2(-query_exponents.astype(jnp.float32))
    dequant = (query_codes.astype(jnp.float32) * row_scale[:, :, None]).astype(jnp.bfloat16)
    partial_value = lax.dot_general(
        lax.all_gather(dequant, "example", axis=1, tiled=True),
        train_features,
        (((0, 2), (0, 2)), ((), ())),
        preferred_element_type=jnp.float32,
    )
    scores = lax.psum_scatter(partial_value, "layer", scatter_dimension=0, tiled=True)
    return scores


def solution(mesh):
    in_specs = (P("layer", "example", None), P("layer", "example", None), P("layer", "example"))
    out_specs = P("layer", "example")
    return jax.shard_map(shards, mesh=mesh, in_specs=in_specs, out_specs=out_specs, check_vma=False)
```

profile of v0, /device:TPU:2, one launch (start us, length us, event | category | flops | bytes accessed | tf_op | source)
XLA Modules:
  0.0 349.3 jit_solution(290350093720434316)
XLA Ops:
  6.5 0.0 all-gather.2.cloned.1.call-start
  6.5 0.7 exponential_bitcast_fusion
  7.2 2.0 multiply_convert_fusion
  9.2 0.0 all-gather.2.cloned.1.call-update
  9.2 0.0 reduce-scatter.2.cloned.1.call-start
  9.3 190.6 %all-gather.2.cloned.1.call-done = bf16[1,2048,4096]{2,1,0:T(8,128)(2,1)} async-done(((bf16[1,64,4096]{2,1,0:T(8,128)(2,1)}), bf16[1,2048,4096]{2,1,0:T(8,128)(2,1)}) %all-gather.2.cloned.1.call-update) | async-done | bytes 16777232 | tf_op jit(solution)/shard_map/all_gather | solution.py:11
  199.8 34.2 %fusion = f32[2048,1536]{1,0:T(8,128)} fusion(bf16[1,2048,4096]{2,1,0:T(8,128)(2,1)} %all-gather.2.cloned.1.call-done, bf16[1,1536,4096]{2,1,0:T(8,128)(2,1)} %param.3), kind=kOutput, calls=%fused_computation | convolution fusion | flops 25769803776 | bytes 41943040 | tf_op jit(solution)/shard_map/dot_general | solution.py:10
  234.1 0.0 reduce-scatter.2.cloned.1.call-update
  234.1 108.4 %reduce-scatter.2.cloned.1.call-done = f32[512,1536]{1,0:T(8,128)} async-done(((f32[2048,1536]{1,0:T(8,128)}), f32[512,1536]{1,0:T(8,128)}) %reduce-scatter.2.cloned.1.call-update) | async-done | bytes 3145744 | tf_op jit(solution)/shard_map/reduce_scatter | solution.py:16
Async XLA Ops:
  6.5 193.3 %all-gather.2.cloned.1.call-start = ((), (), s32[]{:S(2)}) async-start(), calls=%async_computation.1 | async-start | bytes 17301504 | tf_op jit(solution)/shard_map/all_gather | solution.py:11
  9.2 333.3 %reduce-scatter.2.cloned.1.call-start = ((), (), s32[]{:S(2)}) async-start(), calls=%async_computation.2 | async-start | bytes 15728640 | tf_op jit(solution)/shard_map/reduce_scatter | solution.py:16
Sparse Core Ops, SparseCore 0:
  9.3 190.4 all-gather.1
  234.2 108.2 reduce-scatter.1
where the time goes:
time: 351 us; the launch traced here: 349 us
  waiting for transfers between devices  299 us (85%)
  matrix products  34.2 us (10%)
  between operations  13.4 us (4%)
    all_gather x1, waiting for transfers between devices, shards(): lax.all_gather(dequant, 'example', axis=1, tiled=True)  191 us
    reduce_scatter x1, waiting for transfers between devices, shards(): lax.psum_scatter(partial_value, 'layer', scatter_dimension=0, tiled=True)  108 us
    dot_general x1, matrix products, shards(): lax.dot_general(lax.all_gather(dequant, 'example', axis=1, tiled=True), t...  34.2 us
  transfers between devices with their start and end apart: 2, of which 2 were waited for; matrix products, arithmetic and copies ran while one was open for 0% of the time, Pallas kernels for 0%

commit v1 on v0

v1 whole, which is shorter than its diff:
```python
import jax
import jax.numpy as jnp
from jax import lax
from jax.sharding import PartitionSpec as P

BOTH = ("layer", "example")


def moves(step):
    pairs = []
    for x in range(4):
        for core in range(2):
            for z in range(4):
                for y in range(4):
                    tx, tc, tz, ty = step(x, core, z, y)
                    pairs.append((place(x, core, z, y), place(tx % 4, tc % 2, tz % 4, ty % 4)))
    return pairs


def place(x, core, z, y):
    return (2 * (x // 2) + core) * 32 + (2 * z + x % 2) * 4 + y


FIRST_UP = moves(lambda x, c, z, y: (x, c, z + c, y + 1 - c))
FIRST_DOWN = moves(lambda x, c, z, y: (x, c, z - c, y - 1 + c))
SECOND_UP = moves(lambda x, c, z, y: (x, c, z + 1 - c, y + c))
SECOND_DOWN = moves(lambda x, c, z, y: (x, c, z - 1 + c, y - c))
PAIR = moves(lambda x, c, z, y: (x ^ 1, c, z, y))
CORE = moves(lambda x, c, z, y: (x, c + 1, z, y))
ACROSS = moves(lambda x, c, z, y: (x + 2, c, z, y))


def send(value, pairs):
    return lax.ppermute(value, BOTH, pairs)


def narrow(block):
    peak = jnp.maximum(jnp.max(jnp.abs(block), axis=0, keepdims=True), 1e-30)
    power = 13.0 - jnp.floor(jnp.log2(peak))
    scaled = (block * jnp.exp2(power)).astype(jnp.float16)
    return jnp.concatenate([scaled, jnp.broadcast_to(power, (8, block.shape[1])).astype(jnp.float16)], 0)


def widen(message):
    return message[:-8].astype(jnp.float32) * jnp.exp2(-message[-8:-7].astype(jnp.float32))


def shards(train_features, query_codes, query_exponents):
    layer, example = lax.axis_index("layer"), lax.axis_index("example")
    half, core = layer // 2, layer % 2
    z, low, y = example // 8, (example // 4) % 2, example % 4
    train = train_features[0]
    row_scale = jnp.exp2(-query_exponents[0].astype(jnp.float32))
    own = (query_codes[0].astype(jnp.float32) * row_scale[:, None]).astype(jnp.bfloat16)

    def by_core(zero, one):
        return jnp.where(core == 0, zero, one)

    def times(blocks):
        return lax.dot_general(
            jnp.concatenate(blocks, 0), train, (((1,), (1,)), ((), ())), preferred_element_type=jnp.float32
        ).reshape(len(blocks), 128, -1)

    q = {}
    pair = send(own, PAIR)
    below, above = send(own, FIRST_UP), send(own, FIRST_DOWN)
    q[0, 0] = jnp.concatenate([own, pair], 0)
    below_pair, above_pair = send(pair, FIRST_UP), send(pair, FIRST_DOWN)
    far, far_pair = send(below, FIRST_UP), send(above_pair, FIRST_DOWN)
    q[3, 0] = jnp.concatenate([below, below_pair], 0)
    q[1, 0] = jnp.concatenate([above, above_pair], 0)
    q[2, 0] = jnp.concatenate([far, far_pair], 0)
    q[0, 3], q[0, 1] = send(q[0, 0], SECOND_UP), send(q[0, 0], SECOND_DOWN)
    q[3, 3], q[1, 1] = send(q[3, 0], SECOND_UP), send(q[1, 0], SECOND_DOWN)
    third, q[3, 1] = send(by_core(q[0, 3], q[2, 0]), SECOND_UP), send(q[3, 0], SECOND_DOWN)
    q[1, 3], q[2, 1] = send(q[1, 0], SECOND_UP), send(q[2, 0], SECOND_DOWN)
    q[3, 2], q[1, 2] = send(q[3, 3], SECOND_UP), send(q[1, 1], SECOND_DOWN)
    sixth, q[2, 2] = send(by_core(q[2, 0], q[0, 3]), SECOND_UP), send(q[2, 1], SECOND_DOWN)

    out = jnp.zeros((2, 4, 64, train.shape[0]), jnp.float32)

    def reduce(out, dy, partial, spots):
        def plane(target):
            return lax.dynamic_index_in_dim(partial, spots((target - z) % 4), 0, keepdims=False)

        got = send(jnp.stack([plane(1 - core), plane(3 - core)]), CORE)
        other = plane(2 * (1 - half) + core) + lax.dynamic_index_in_dim(got, 1 - half, 0, keepdims=False)
        far_sum = send(narrow(other), ACROSS)
        mine = plane(2 * half + core) + lax.dynamic_index_in_dim(got, half, 0, keepdims=False)
        total = mine + widen(far_sum)
        column = (y + dy) % 4
        out = lax.dynamic_update_slice(out, total[None, None, :64], (low, column, 0, 0))
        return lax.dynamic_update_slice(out, total[None, None, 64:], (1 - low, column, 0, 0))

    straight = lambda spot: spot
    out = reduce(out, 0, times([q[0, 0], by_core(q[0, 1], q[1, 0]), by_core(third, q[2, 0]), by_core(q[0, 3], q[3, 0])]), straight)
    out = reduce(out, 1, times([by_core(q[1, 0], q[0, 1]), q[1, 1], by_core(q[1, 2], q[2, 1]), by_core(q[1, 3], q[3, 1])]), straight)
    out = reduce(out, 3, times([by_core(q[3, 0], q[0, 3]), by_core(q[3, 1], q[1, 3]), by_core(q[3, 2], third), q[3, 3]]), straight)
    early = times([by_core(q[2, 0], q[3, 2]), by_core(q[2, 1], q[1, 2])])
    late = times([q[2, 2], sixth])
    out = reduce(out, 2, jnp.concatenate([early, late], 0), lambda spot: by_core(spot, jnp.array([3, 1, 2, 0])[spot]))
    return out.reshape(512, -1)


def solution(mesh):
    in_specs = (P("layer", "example", None), P("layer", "example", None), P("layer", "example"))
    out_specs = P("layer", "example")
    return jax.shard_map(shards, mesh=mesh, in_specs=in_specs, out_specs=out_specs, check_vma=False)
```

time: 351 us -> 196 us (0.56)
  waiting for transfers between devices: 299 us -> 87 us
  starting transfers between devices: 0.04 us -> 35.8 us
  other arithmetic: 2.65 us -> 20.8 us
  between operations: 13.4 us -> 3.24 us
  local copies, waits for them, and re-layouts: 0 us -> 7.32 us
  matrix products: 34.2 us -> 40.9 us
    all_gather x1 -> x0, waiting for transfers between devices: 191 us -> none  [shards(): lax.all_gather(dequant, 'example', axis=1, tiled=True)]
    reduce_scatter x1 -> x0, waiting for transfers between devices: 108 us -> none  [shards(): lax.psum_scatter(partial_value, 'layer', scatter_dimension=0, tiled=True)]
    ppermute x0 -> x27, waiting for transfers between devices: none -> 87 us  [send(): return lax.ppermute(value, BOTH, pairs)]
    ppermute x0 -> x27, starting transfers between devices: none -> 35.8 us  [send(): return lax.ppermute(value, BOTH, pairs)]
    select_n x0 -> x6, other arithmetic: none -> 7.5 us  [by_core(): return jnp.where(core == 0, zero, one)]
    dot_general x1 -> x5, matrix products: 34.2 us -> 40.9 us  [times(): lax.dot_general(jnp.concatenate(blocks, 0), train, (((1,), (1,)), ((), ()...]
    unnamed x0 -> x16, local copies, waits for them, and re-layouts: none -> 4.72 us
    concatenate x0 -> x9, other arithmetic: none -> 3.65 us  [the longest x3 2.83 us: times(): jnp.concatenate(blocks, 0)]
  transfers between devices with their start and end apart: 2 -> 27, of which waited for: 2 -> 10; matrix products, arithmetic and copies ran while one was open for 0% -> 31% of each run, Pallas kernels for 0% -> 0%
where the time goes in v1:
time: 196 us; the launch traced here: 195 us
  waiting for transfers between devices  87 us (44%)
  matrix products  40.9 us (21%)
  starting transfers between devices  35.8 us (18%)
  other arithmetic  20.8 us (11%)
  local copies, waits for them, and re-layouts  7.32 us (4%)
  between operations  3.24 us (2%)
    ppermute x27, waiting for transfers between devices, send(): return lax.ppermute(value, BOTH, pairs)  87 us
    dot_general x5, matrix products, times(): lax.dot_general(jnp.concatenate(blocks, 0), train, (((1,), (1,)), ((), ()...  40.9 us
    ppermute x27, starting transfers between devices, send(): return lax.ppermute(value, BOTH, pairs)  35.8 us
    select_n x6, other arithmetic, by_core(): return jnp.where(core == 0, zero, one)  7.5 us
    unnamed x16, local copies, waits for them, and re-layouts  4.72 us
  transfers between devices with their start and end apart: 27, of which 10 were waited for; matrix products, arithmetic and copies ran while one was open for 31% of the time, Pallas kernels for 0%

profile of v1, /device:TPU:2, one launch (start us, length us, event | category | flops | bytes accessed | tf_op | source)
XLA Modules:
  0.0 195.0 jit_solution(3854802085086549633)
XLA Ops:
  0.7 2.0 %constant_dynamic-update-slice_fusion.7 = (bf16[512,4096]{1,0:T(8,128)(2,1)}, bf16[64,4096]{1,0:T(8,128)(2,1)S(1)}) fusion(f32[64]{0:T(128)S(1)} %exponential_bitcast_fusion, bf16[1,64,4096]{2,1,0:T(8,128)(2,1)} %param.8), kind=kLoop, calls=%fused_computation.98 | loop fusion | flops 786431 | bytes 1573120
  3.2 1.7 collective-permute-start.5
  4.8 1.6 collective-permute-start.2
  10.6 5.8 %collective-permute-done = bf16[64,4096]{1,0:T(8,128)(2,1)S(1)} collective-permute-done((bf16[64,4096]{1,0:T(8,128)(2,1)S(1)}, bf16[64,4096]{1,0:T(8,128)(2,1)S(1)}, u32[]{:S(2)}, u32[]{:S(2)}) %collective-permute-start) | collective-permute-done | bytes 524320 | tf_op jit(solution)/shard_map/ppermute | solution.py:34
  16.4 4.1 %collective-permute-start.1 = (bf16[128,4096]{1,0:T(8,128)(2,1)S(1)}, bf16[128,4096]{1,0:T(8,128)(2,1)S(1)}, u32[]{:S(2)}, u32[]{:S(2)}) collective-permute-start(bf16[128,4096]{1,0:T(8,128)(2,1)S(1)} %pad_maximum_fusion.8), channel_id=1, source_target_pairs={{0,24},{1,25},{2,26},{3,27},{8,0},{9,1},{10,2},{11,3},{16,8},{17,9... | collective-permute-start | bytes 3145736 | tf_op jit(solution)/shard_map/ppermute | solution.py:34
  20.5 1.6 collective-permute-start.9
  22.1 1.7 collective-permute-start.3
  24.3 6.6 %collective-permute-done.9 = bf16[64,4096]{1,0:T(8,128)(2,1)S(1)} collective-permute-done((bf16[64,4096]{1,0:T(8,128)(2,1)S(1)}, bf16[64,4096]{1,0:T(8,128)(2,1)S(1)}, u32[]{:S(2)}, u32[]{:S(2)}) %collective-permute-start.9) | collective-permute-done | bytes 524320 | tf_op jit(solution)/shard_map/ppermute | solution.py:34
  31.1 4.8 %collective-permute-done.3 = bf16[64,4096]{1,0:T(8,128)(2,1)S(1)} collective-permute-done((bf16[64,4096]{1,0:T(8,128)(2,1)S(1)}, bf16[64,4096]{1,0:T(8,128)(2,1)S(1)}, u32[]{:S(2)}, u32[]{:S(2)}) %collective-permute-start.3) | collective-permute-done | bytes 524320 | tf_op jit(solution)/shard_map/ppermute | solution.py:34
  35.9 1.5 collective-permute-start.12
  37.5 2.9 %collective-permute-start.7 = (bf16[64,4096]{1,0:T(8,128)(2,1)S(1)}, bf16[64,4096]{1,0:T(8,128)(2,1)S(1)}, u32[]{:S(2)}, u32[]{:S(2)}) collective-permute-start(bf16[64,4096]{1,0:T(8,128)(2,1)S(1)} %collective-permute-done.3), channel_id=1, source_target_pairs={{0,3},{1,0},{2,1},{3,2},{8,11},{9,8},{10,9},{11,10},{16,19},{17,16... | collective-permute-start | bytes 1572872 | tf_op jit(solution)/shard_map/ppermute | solution.py:34
  42.6 10.1 %collective-permute-done.7 = bf16[64,4096]{1,0:T(8,128)(2,1)S(1)} collective-permute-done((bf16[64,4096]{1,0:T(8,128)(2,1)S(1)}, bf16[64,4096]{1,0:T(8,128)(2,1)S(1)}, u32[]{:S(2)}, u32[]{:S(2)}) %collective-permute-start.7) | collective-permute-done | bytes 524320 | tf_op jit(solution)/shard_map/ppermute | solution.py:34
  52.9 2.0 %collective-permute-start.4 = (bf16[128,4096]{1,0:T(8,128)(2,1)S(1)}, bf16[128,4096]{1,0:T(8,128)(2,1)S(1)}, u32[]{:S(2)}, u32[]{:S(2)}) collective-permute-start(bf16[128,4096]{1,0:T(8,128)(2,1)S(1)} %pad_maximum_fusion.8), channel_id=1, source_target_pairs={{0,8},{1,9},{2,10},{3,11},{8,16},{9,17},{10,18},{11,19},{16,24},{1... | collective-permute-start | bytes 3145736 | tf_op jit(solution)/shard_map/ppermute | solution.py:34
  58.3 2.5 %collective-permute-start.13 = (bf16[128,4096]{1,0:T(8,128)(2,1)S(1)}, bf16[128,4096]{1,0:T(8,128)(2,1)S(1)}, u32[]{:S(2)}, u32[]{:S(2)}) collective-permute-start(bf16[128,4096]{1,0:T(8,128)(2,1)S(1)} %collective-permute-done.12), channel_id=1, source_target_pairs={{0,24},{1,25},{2,26},{3,27},{8,0},{9,1},{10,2},{11,3},{16,8},{17,9... | collective-permute-start | bytes 3145736 | tf_op jit(solution)/shard_map/ppermute | solution.py:34
  60.9 6.7 %collective-permute-done.16 = bf16[128,4096]{1,0:T(8,128)(2,1)S(1)} collective-permute-done((bf16[128,4096]{1,0:T(8,128)(2,1)S(1)}, bf16[128,4096]{1,0:T(8,128)(2,1)S(1)}, u32[]{:S(2)}, u32[]{:S(2)}) %collective-permute-start.16) | collective-permute-done | bytes 1048608 | tf_op jit(solution)/shard_map/ppermute | solution.py:34
  67.7 11.1 %collective-permute-done.14 = bf16[128,4096]{1,0:T(8,128)(2,1)S(1)} collective-permute-done((bf16[128,4096]{1,0:T(8,128)(2,1)S(1)}, bf16[128,4096]{1,0:T(8,128)(2,1)S(1)}, u32[]{:S(2)}, u32[]{:S(2)}) %collective-permute-start.14) | collective-permute-done | bytes 1048608 | tf_op jit(solution)/shard_map/ppermute | solution.py:34
  78.8 2.7 %collective-permute-start.23 = (bf16[128,4096]{1,0:T(8,128)(2,1)S(1)}, bf16[128,4096]{1,0:T(8,128)(2,1)}, u32[]{:S(2)}, u32[]{:S(2)}) collective-permute-start(bf16[128,4096]{1,0:T(8,128)(2,1)S(1)} %collective-permute-done.14), channel_id=1, source_target_pairs={{0,24},{1,25},{2,26},{3,27},{8,0},{9,1},{10,2},{11,3},{16,8},{17,9... | collective-permute-start | bytes 3145736 | tf_op jit(solution)/shard_map/ppermute | solution.py:34
  83.8 6.2 %collective-permute-done.13 = bf16[128,4096]{1,0:T(8,128)(2,1)S(1)} collective-permute-done((bf16[128,4096]{1,0:T(8,128)(2,1)S(1)}, bf16[128,4096]{1,0:T(8,128)(2,1)S(1)}, u32[]{:S(2)}, u32[]{:S(2)}) %collective-permute-start.13) | collective-permute-done | bytes 1048608 | tf_op jit(solution)/shard_map/ppermute | solution.py:34
  90.4 6.5 %fusion.2 = f32[2,128,1536]{2,1,0:T(8,128)S(1)} fusion(bf16[2,128,4096]{2,1,0:T(8,128)(2,1)S(1)} %bitcast.101, bf16[1,1536,4096]{2,1,0:T(8,128)(2,1)} %param.7), kind=kOutput, calls=%fused_computation.2 | convolution fusion | flops 3221225472 | bytes 16252928 | tf_op jit(solution)/shard_map/dot_general | solution.py:60
  96.9 4.4 %collective-permute-done.23 = bf16[128,4096]{1,0:T(8,128)(2,1)} collective-permute-done((bf16[128,4096]{1,0:T(8,128)(2,1)S(1)}, bf16[128,4096]{1,0:T(8,128)(2,1)}, u32[]{:S(2)}, u32[]{:S(2)}) %collective-permute-start.23) | collective-permute-done | bytes 1048608 | tf_op jit(solution)/shard_map/ppermute | solution.py:34
  101.4 1.7 pad_maximum_fusion.3
  103.0 6.5 %fusion = f32[2,128,1536]{2,1,0:T(8,128)S(1)} fusion(bf16[2,128,4096]{2,1,0:T(8,128)(2,1)S(1)} %bitcast.102, bf16[1,1536,4096]{2,1,0:T(8,128)(2,1)} %param.7), kind=kOutput, calls=%fused_computation | convolution fusion | flops 3221225472 | bytes 16252928 | tf_op jit(solution)/shard_map/dot_general | solution.py:60
  111.2 2.7 %broadcast_select_fusion.3 = (bf16[128,4096]{1,0:T(8,128)(2,1)S(1)}, bf16[512,4096]{1,0:T(8,128)(2,1)}) fusion(bf16[128,4096]{1,0:T(8,128)(2,1)S(1)} %collective-permute-done.20, bf16[128,4096]{1,0:T(8,128)(2,1)} %collective-permute-done.8, pred[]{:T(512)S(6)} %eq.43, bf16[512,4096]{1,0:T(8,128)(2,1)} %get-tuple-element.26, ...), kind=kLoop, calls=%fused_computation.35 | loop fusion | flops 1048576 | bytes 5242881 | tf_op jit(solution)/shard_map/jit(_where)/select_n | solution.py:57
  116.8 9.3 %fusion.4 = f32[4,128,1536]{2,1,0:T(8,128)S(1)} fusion(bf16[4,128,4096]{2,1,0:T(8,128)(2,1)S(1)} %bitcast.100, bf16[1,1536,4096]{2,1,0:T(8,128)(2,1)} %param.7), kind=kOutput, calls=%fused_computation.4 | convolution fusion | flops 6442450944 | bytes 19922944 | tf_op jit(solution)/shard_map/dot_general | solution.py:60
  128.0 9.3 %fusion.6 = f32[4,128,1536]{2,1,0:T(8,128)S(1)} fusion(bf16[4,128,4096]{2,1,0:T(8,128)(2,1)S(1)} %bitcast.99, bf16[1,1536,4096]{2,1,0:T(8,128)(2,1)} %param.7), kind=kOutput, calls=%fused_computation.6 | convolution fusion | flops 6442450944 | bytes 19922944 | tf_op jit(solution)/shard_map/dot_general | solution.py:60
  137.9 1.6 copy-done.5
  139.6 9.3 %fusion.8 = f32[4,128,1536]{2,1,0:T(8,128)S(1)} fusion(bf16[4,128,4096]{2,1,0:T(8,128)(2,1)S(1)} %bitcast.103, bf16[1,1536,4096]{2,1,0:T(8,128)(2,1)} %param.7), kind=kOutput, calls=%fused_computation.8 | convolution fusion | flops 6442450944 | bytes 19922944 | tf_op jit(solution)/shard_map/dot_general | solution.py:60
  150.7 2.2 %collective-permute-start.26 = (f16[136,1536]{1,0:T(8,128)(2,1)S(1)}, f16[136,1536]{1,0:T(8,128)(2,1)S(1)}, u32[]{:S(2)}, u32[]{:S(2)}) collective-permute-start(f16[136,1536]{1,0:T(8,128)(2,1)S(1)} %pad_maximum_fusion.12), channel_id=1, source_target_pairs={{0,64},{1,65},{2,66},{3,67},{8,72},{9,73},{10,74},{11,75},{16,80},... | collective-permute-start | bytes 1253384 | tf_op jit(solution)/shard_map/ppermute | solution.py:34
  155.4 2.2 %collective-permute-start.11 = (f16[136,1536]{1,0:T(8,128)(2,1)S(1)}, f16[136,1536]{1,0:T(8,128)(2,1)S(1)}, u32[]{:S(2)}, u32[]{:S(2)}) collective-permute-start(f16[136,1536]{1,0:T(8,128)(2,1)S(1)} %pad_maximum_fusion.9), channel_id=1, source_target_pairs={{0,64},{1,65},{2,66},{3,67},{8,72},{9,73},{10,74},{11,75},{16,80},... | collective-permute-start | bytes 1253384 | tf_op jit(solution)/shard_map/ppermute | solution.py:34
  159.3 23.4 %collective-permute-done.11 = f16[136,1536]{1,0:T(8,128)(2,1)S(1)} collective-permute-done((f16[136,1536]{1,0:T(8,128)(2,1)S(1)}, f16[136,1536]{1,0:T(8,128)(2,1)S(1)}, u32[]{:S(2)}, u32[]{:S(2)}) %collective-permute-start.11) | collective-permute-done | bytes 417824 | tf_op jit(solution)/shard_map/ppermute | solution.py:34
  183.4 7.8 %collective-permute-done.18 = f16[136,1536]{1,0:T(8,128)(2,1)S(1)} collective-permute-done((f16[136,1536]{1,0:T(8,128)(2,1)S(1)}, f16[136,1536]{1,0:T(8,128)(2,1)S(1)}, u32[]{:S(2)}, u32[]{:S(2)}) %collective-permute-start.18) | collective-permute-done | bytes 417824 | tf_op jit(solution)/shard_map/ppermute | solution.py:34
  193.3 1.7 copy-done
  (104 shorter events, 27.5 us)
Async XLA Ops:
  2.7 13.7 %collective-permute-start = (bf16[64,4096]{1,0:T(8,128)(2,1)S(1)}, bf16[64,4096]{1,0:T(8,128)(2,1)S(1)}, u32[]{:S(2)}, u32[]{:S(2)}) collective-permute-start(bf16[64,4096]{1,0:T(8,128)(2,1)S(1)} %get-tuple-element.8), channel_id=1, source_target_pairs={{0,4},{1,5},{2,6},{3,7},{8,12},{9,13},{10,14},{11,15},{16,20},{17,... | collective-permute-start | bytes 1572872 | tf_op jit(solution)/shard_map/ppermute | solution.py:34
  3.2 20.6 %collective-permute-start.5 = (bf16[64,4096]{1,0:T(8,128)(2,1)S(1)}, bf16[64,4096]{1,0:T(8,128)(2,1)S(1)}, u32[]{:S(2)}, u32[]{:S(2)}) collective-permute-start(bf16[64,4096]{1,0:T(8,128)(2,1)S(1)} %get-tuple-element.8), channel_id=1, source_target_pairs={{0,1},{1,2},{2,3},{3,0},{8,9},{9,10},{10,11},{11,8},{16,17},{17,18... | collective-permute-start | bytes 1572872 | tf_op jit(solution)/shard_map/ppermute | solution.py:34
  4.8 19.5 %collective-permute-start.2 = (bf16[64,4096]{1,0:T(8,128)(2,1)S(1)}, bf16[64,4096]{1,0:T(8,128)(2,1)S(1)}, u32[]{:S(2)}, u32[]{:S(2)}) collective-permute-start(bf16[64,4096]{1,0:T(8,128)(2,1)S(1)} %get-tuple-element.8), channel_id=1, source_target_pairs={{0,3},{1,0},{2,1},{3,2},{8,11},{9,8},{10,9},{11,10},{16,19},{17,16... | collective-permute-start | bytes 1572872 | tf_op jit(solution)/shard_map/ppermute | solution.py:34
  16.4 36.5 %collective-permute-start.1 = (bf16[128,4096]{1,0:T(8,128)(2,1)S(1)}, bf16[128,4096]{1,0:T(8,128)(2,1)S(1)}, u32[]{:S(2)}, u32[]{:S(2)}) collective-permute-start(bf16[128,4096]{1,0:T(8,128)(2,1)S(1)} %pad_maximum_fusion.8), channel_id=1, source_target_pairs={{0,24},{1,25},{2,26},{3,27},{8,0},{9,1},{10,2},{11,3},{16,8},{17,9... | collective-permute-start | bytes 3145736 | tf_op jit(solution)/shard_map/ppermute | solution.py:34
  20.5 10.4 %collective-permute-start.9 = (bf16[64,4096]{1,0:T(8,128)(2,1)S(1)}, bf16[64,4096]{1,0:T(8,128)(2,1)S(1)}, u32[]{:S(2)}, u32[]{:S(2)}) collective-permute-start(bf16[64,4096]{1,0:T(8,128)(2,1)S(1)} %collective-permute-done), channel_id=1, source_target_pairs={{0,1},{1,2},{2,3},{3,0},{8,9},{9,10},{10,11},{11,8},{16,17},{17,18... | collective-permute-start | bytes 1572872 | tf_op jit(solution)/shard_map/ppermute | solution.py:34
  22.1 13.8 %collective-permute-start.3 = (bf16[64,4096]{1,0:T(8,128)(2,1)S(1)}, bf16[64,4096]{1,0:T(8,128)(2,1)S(1)}, u32[]{:S(2)}, u32[]{:S(2)}) collective-permute-start(bf16[64,4096]{1,0:T(8,128)(2,1)S(1)} %collective-permute-done), channel_id=1, source_target_pairs={{0,3},{1,0},{2,1},{3,2},{8,11},{9,8},{10,9},{11,10},{16,19},{17,16... | collective-permute-start | bytes 1572872 | tf_op jit(solution)/shard_map/ppermute | solution.py:34
  23.8 17.4 %collective-permute-start.6 = (bf16[64,4096]{1,0:T(8,128)(2,1)S(1)}, bf16[64,4096]{1,0:T(8,128)(2,1)S(1)}, u32[]{:S(2)}, u32[]{:S(2)}) collective-permute-start(bf16[64,4096]{1,0:T(8,128)(2,1)S(1)} %collective-permute-done.5), channel_id=1, source_target_pairs={{0,1},{1,2},{2,3},{3,0},{8,9},{9,10},{10,11},{11,8},{16,17},{17,18... | collective-permute-start | bytes 1572872 | tf_op jit(solution)/shard_map/ppermute | solution.py:34
  31.0 23.9 %collective-permute-start.19 = (bf16[128,4096]{1,0:T(8,128)(2,1)S(1)}, bf16[128,4096]{1,0:T(8,128)(2,1)S(1)}, u32[]{:S(2)}, u32[]{:S(2)}) collective-permute-start(bf16[128,4096]{1,0:T(8,128)(2,1)S(1)} %constant_dynamic-update-slice_fusion.4), channel_id=1, source_target_pairs={{0,8},{1,9},{2,10},{3,11},{8,16},{9,17},{10,18},{11,19},{16,24},{1... | collective-permute-start | bytes 3145736 | tf_op jit(solution)/shard_map/ppermute | solution.py:34
  35.9 20.3 %collective-permute-start.12 = (bf16[128,4096]{1,0:T(8,128)(2,1)S(1)}, bf16[128,4096]{1,0:T(8,128)(2,1)S(1)}, u32[]{:S(2)}, u32[]{:S(2)}) collective-permute-start(bf16[128,4096]{1,0:T(8,128)(2,1)S(1)} %constant_dynamic-update-slice_fusion), channel_id=1, source_target_pairs={{0,24},{1,25},{2,26},{3,27},{8,0},{9,1},{10,2},{11,3},{16,8},{17,9... | collective-permute-start | bytes 3145736 | tf_op jit(solution)/shard_map/ppermute | solution.py:34
  37.5 15.2 %collective-permute-start.7 = (bf16[64,4096]{1,0:T(8,128)(2,1)S(1)}, bf16[64,4096]{1,0:T(8,128)(2,1)S(1)}, u32[]{:S(2)}, u32[]{:S(2)}) collective-permute-start(bf16[64,4096]{1,0:T(8,128)(2,1)S(1)} %collective-permute-done.3), channel_id=1, source_target_pairs={{0,3},{1,0},{2,1},{3,2},{8,11},{9,8},{10,9},{11,10},{16,19},{17,16... | collective-permute-start | bytes 1572872 | tf_op jit(solution)/shard_map/ppermute | solution.py:34
  41.2 17.1 %collective-permute-start.15 = (bf16[128,4096]{1,0:T(8,128)(2,1)S(1)}, bf16[128,4096]{1,0:T(8,128)(2,1)S(1)}, u32[]{:S(2)}, u32[]{:S(2)}) collective-permute-start(bf16[128,4096]{1,0:T(8,128)(2,1)S(1)} %constant_dynamic-update-slice_fusion), channel_id=1, source_target_pairs={{0,8},{1,9},{2,10},{3,11},{8,16},{9,17},{10,18},{11,19},{16,24},{1... | collective-permute-start | bytes 3145736 | tf_op jit(solution)/shard_map/ppermute | solution.py:34
  52.7 14.8 %collective-permute-start.16 = (bf16[128,4096]{1,0:T(8,128)(2,1)S(1)}, bf16[128,4096]{1,0:T(8,128)(2,1)S(1)}, u32[]{:S(2)}, u32[]{:S(2)}) collective-permute-start(bf16[128,4096]{1,0:T(8,128)(2,1)S(1)} %constant_dynamic-update-slice_fusion.4), channel_id=1, source_target_pairs={{0,24},{1,25},{2,26},{3,27},{8,0},{9,1},{10,2},{11,3},{16,8},{17,9... | collective-permute-start | bytes 3145736 | tf_op jit(solution)/shard_map/ppermute | solution.py:34
  52.9 28.6 %collective-permute-start.4 = (bf16[128,4096]{1,0:T(8,128)(2,1)S(1)}, bf16[128,4096]{1,0:T(8,128)(2,1)S(1)}, u32[]{:S(2)}, u32[]{:S(2)}) collective-permute-start(bf16[128,4096]{1,0:T(8,128)(2,1)S(1)} %pad_maximum_fusion.8), channel_id=1, source_target_pairs={{0,8},{1,9},{2,10},{3,11},{8,16},{9,17},{10,18},{11,19},{16,24},{1... | collective-permute-start | bytes 3145736 | tf_op jit(solution)/shard_map/ppermute | solution.py:34
  54.9 12.8 %copy-start.1 = (bf16[128,4096]{1,0:T(8,128)(2,1)}, bf16[128,4096]{1,0:T(8,128)(2,1)S(1)}, u32[]{:S(2)}) copy-start(bf16[128,4096]{1,0:T(8,128)(2,1)S(1)} %collective-permute-done.19) | copy-start | bytes 3145732
  54.9 23.9 %collective-permute-start.14 = (bf16[128,4096]{1,0:T(8,128)(2,1)S(1)}, bf16[128,4096]{1,0:T(8,128)(2,1)S(1)}, u32[]{:S(2)}, u32[]{:S(2)}) collective-permute-start(bf16[128,4096]{1,0:T(8,128)(2,1)S(1)} %constant_dynamic-update-slice_fusion.2), channel_id=1, source_target_pairs={{0,24},{1,25},{2,26},{3,27},{8,0},{9,1},{10,2},{11,3},{16,8},{17,9... | collective-permute-start | bytes 3145736 | tf_op jit(solution)/shard_map/ppermute | solution.py:34
  56.2 11.5 %copy-start.3 = (bf16[128,4096]{1,0:T(8,128)(2,1)}, bf16[128,4096]{1,0:T(8,128)(2,1)S(1)}, u32[]{:S(2)}) copy-start(bf16[128,4096]{1,0:T(8,128)(2,1)S(1)} %collective-permute-done.12) | copy-start | bytes 3145732
  56.2 25.3 %collective-permute-start.20 = (bf16[128,4096]{1,0:T(8,128)(2,1)S(1)}, bf16[128,4096]{1,0:T(8,128)(2,1)S(1)}, u32[]{:S(2)}, u32[]{:S(2)}) collective-permute-start(bf16[128,4096]{1,0:T(8,128)(2,1)S(1)} %collective-permute-done.19), channel_id=1, source_target_pairs={{0,8},{1,9},{2,10},{3,11},{8,16},{9,17},{10,18},{11,19},{16,24},{1... | collective-permute-start | bytes 3145736 | tf_op jit(solution)/shard_map/ppermute | solution.py:34
  58.3 31.7 %collective-permute-start.13 = (bf16[128,4096]{1,0:T(8,128)(2,1)S(1)}, bf16[128,4096]{1,0:T(8,128)(2,1)S(1)}, u32[]{:S(2)}, u32[]{:S(2)}) collective-permute-start(bf16[128,4096]{1,0:T(8,128)(2,1)S(1)} %collective-permute-done.12), channel_id=1, source_target_pairs={{0,24},{1,25},{2,26},{3,27},{8,0},{9,1},{10,2},{11,3},{16,8},{17,9... | collective-permute-start | bytes 3145736 | tf_op jit(solution)/shard_map/ppermute | solution.py:34
  78.8 22.6 %collective-permute-start.23 = (bf16[128,4096]{1,0:T(8,128)(2,1)S(1)}, bf16[128,4096]{1,0:T(8,128)(2,1)}, u32[]{:S(2)}, u32[]{:S(2)}) collective-permute-start(bf16[128,4096]{1,0:T(8,128)(2,1)S(1)} %collective-permute-done.14), channel_id=1, source_target_pairs={{0,24},{1,25},{2,26},{3,27},{8,0},{9,1},{10,2},{11,3},{16,8},{17,9... | collective-permute-start | bytes 3145736 | tf_op jit(solution)/shard_map/ppermute | solution.py:34
  83.0 18.3 %collective-permute-start.24 = (bf16[128,4096]{1,0:T(8,128)(2,1)}, bf16[128,4096]{1,0:T(8,128)(2,1)}, u32[]{:S(2)}, u32[]{:S(2)}) collective-permute-start(bf16[128,4096]{1,0:T(8,128)(2,1)} %get-tuple-element.17), channel_id=1, source_target_pairs={{0,8},{1,9},{2,10},{3,11},{8,16},{9,17},{10,18},{11,19},{16,24},{1... | collective-permute-start | bytes 3145736 | tf_op jit(solution)/shard_map/ppermute | solution.py:34
  83.0 28.2 %collective-permute-start.8 = (bf16[128,4096]{1,0:T(8,128)(2,1)}, bf16[128,4096]{1,0:T(8,128)(2,1)}, u32[]{:S(2)}, u32[]{:S(2)}) collective-permute-start(bf16[128,4096]{1,0:T(8,128)(2,1)} %get-tuple-element.18), channel_id=1, source_target_pairs={{0,8},{1,9},{2,10},{3,11},{8,16},{9,17},{10,18},{11,19},{16,24},{1... | collective-permute-start | bytes 3145736 | tf_op jit(solution)/shard_map/ppermute | solution.py:34
  111.2 38.0 %collective-permute-start.25 = (f32[2,128,1536]{2,1,0:T(8,128)}, f32[2,128,1536]{2,1,0:T(8,128)}, u32[]{:S(2)}, u32[]{:S(2)}) collective-permute-start(f32[2,128,1536]{2,1,0:T(8,128)} %pad_maximum_fusion.7), channel_id=1, source_target_pairs={{0,32},{1,33},{2,34},{3,35},{8,40},{9,41},{10,42},{11,43},{16,48},... | collective-permute-start | bytes 4718600 | tf_op jit(solution)/shard_map/ppermute | solution.py:34
  113.9 1.9 copy-start.4
  127.5 25.4 %collective-permute-start.21 = (f32[2,128,1536]{2,1,0:T(8,128)}, f32[2,128,1536]{2,1,0:T(8,128)S(1)}, u32[]{:S(2)}, u32[]{:S(2)}) collective-permute-start(f32[2,128,1536]{2,1,0:T(8,128)} %pad_maximum_fusion.6), channel_id=1, source_target_pairs={{0,32},{1,33},{2,34},{3,35},{8,40},{9,41},{10,42},{11,43},{16,48},... | collective-permute-start | bytes 4718600 | tf_op jit(solution)/shard_map/ppermute | solution.py:34
  137.4 2.2 %copy-start.5 = (bf16[512,4096]{1,0:T(8,128)(2,1)S(1)}, bf16[512,4096]{1,0:T(8,128)(2,1)}, u32[]{:S(2)}) copy-start(bf16[512,4096]{1,0:T(8,128)(2,1)} %get-tuple-element.22) | copy-start | bytes 12582916
  137.6 17.2 %collective-permute-start.17 = (f32[2,128,1536]{2,1,0:T(8,128)S(1)}, f32[2,128,1536]{2,1,0:T(8,128)S(1)}, u32[]{:S(2)}, u32[]{:S(2)}) collective-permute-start(f32[2,128,1536]{2,1,0:T(8,128)S(1)} %pad_maximum_fusion.5), channel_id=1, source_target_pairs={{0,32},{1,33},{2,34},{3,35},{8,40},{9,41},{10,42},{11,43},{16,48},... | collective-permute-start | bytes 4718600 | tf_op jit(solution)/shard_map/ppermute | solution.py:34
  149.1 5.8 %collective-permute-start.10 = (f32[2,128,1536]{2,1,0:T(8,128)S(1)}, f32[2,128,1536]{2,1,0:T(8,128)S(1)}, u32[]{:S(2)}, u32[]{:S(2)}) collective-permute-start(f32[2,128,1536]{2,1,0:T(8,128)S(1)} %pad_maximum_fusion.4), channel_id=1, source_target_pairs={{0,32},{1,33},{2,34},{3,35},{8,40},{9,41},{10,42},{11,43},{16,48},... | collective-permute-start | bytes 4718600 | tf_op jit(solution)/shard_map/ppermute | solution.py:34
  150.7 41.0 %collective-permute-start.26 = (f16[136,1536]{1,0:T(8,128)(2,1)S(1)}, f16[136,1536]{1,0:T(8,128)(2,1)S(1)}, u32[]{:S(2)}, u32[]{:S(2)}) collective-permute-start(f16[136,1536]{1,0:T(8,128)(2,1)S(1)} %pad_maximum_fusion.12), channel_id=1, source_target_pairs={{0,64},{1,65},{2,66},{3,67},{8,72},{9,73},{10,74},{11,75},{16,80},... | collective-permute-start | bytes 1253384 | tf_op jit(solution)/shard_map/ppermute | solution.py:34
  153.3 38.2 %collective-permute-start.22 = (f16[136,1536]{1,0:T(8,128)(2,1)S(1)}, f16[136,1536]{1,0:T(8,128)(2,1)S(1)}, u32[]{:S(2)}, u32[]{:S(2)}) collective-permute-start(f16[136,1536]{1,0:T(8,128)(2,1)S(1)} %pad_maximum_fusion.11), channel_id=1, source_target_pairs={{0,64},{1,65},{2,66},{3,67},{8,72},{9,73},{10,74},{11,75},{16,80},... | collective-permute-start | bytes 1253384 | tf_op jit(solution)/shard_map/ppermute | solution.py:34
  155.4 27.3 %collective-permute-start.11 = (f16[136,1536]{1,0:T(8,128)(2,1)S(1)}, f16[136,1536]{1,0:T(8,128)(2,1)S(1)}, u32[]{:S(2)}, u32[]{:S(2)}) collective-permute-start(f16[136,1536]{1,0:T(8,128)(2,1)S(1)} %pad_maximum_fusion.9), channel_id=1, source_target_pairs={{0,64},{1,65},{2,66},{3,67},{8,72},{9,73},{10,74},{11,75},{16,80},... | collective-permute-start | bytes 1253384 | tf_op jit(solution)/shard_map/ppermute | solution.py:34
  157.8 33.4 %collective-permute-start.18 = (f16[136,1536]{1,0:T(8,128)(2,1)S(1)}, f16[136,1536]{1,0:T(8,128)(2,1)S(1)}, u32[]{:S(2)}, u32[]{:S(2)}) collective-permute-start(f16[136,1536]{1,0:T(8,128)(2,1)S(1)} %pad_maximum_fusion.10), channel_id=1, source_target_pairs={{0,64},{1,65},{2,66},{3,67},{8,72},{9,73},{10,74},{11,75},{16,80},... | collective-permute-start | bytes 1253384 | tf_op jit(solution)/shard_map/ppermute | solution.py:34
  193.3 1.7 copy-start
  (1 other events, 1.4 us)

commit v2 on v1

v2 whole, which is shorter than its diff:
```python
import functools

import jax
import jax.numpy as jnp
from jax import lax
from jax.experimental import pallas as pl
from jax.experimental.pallas import tpu as pltpu
from jax.sharding import PartitionSpec as P

BOTH = ("layer", "example")


def moves(step):
    pairs = []
    for x in range(4):
        for core in range(2):
            for z in range(4):
                for y in range(4):
                    tx, tc, tz, ty = step(x, core, z, y)
                    pairs.append((place(x, core, z, y), place(tx % 4, tc % 2, tz % 4, ty % 4)))
    return pairs


def place(x, core, z, y):
    return (2 * (x // 2) + core) * 32 + (2 * z + x % 2) * 4 + y


FIRST_UP = moves(lambda x, c, z, y: (x, c, z + c, y + 1 - c))
FIRST_DOWN = moves(lambda x, c, z, y: (x, c, z - c, y - 1 + c))
SECOND_UP = moves(lambda x, c, z, y: (x, c, z + 1 - c, y + c))
SECOND_DOWN = moves(lambda x, c, z, y: (x, c, z - 1 + c, y - c))
PAIR = moves(lambda x, c, z, y: (x ^ 1, c, z, y))
CORE = moves(lambda x, c, z, y: (x, c + 1, z, y))
ACROSS = moves(lambda x, c, z, y: (x + 2, c, z, y))


def send(value, pairs):
    return lax.ppermute(value, BOTH, pairs)


VMEM = 40 * 2**20
TILE = 512


def product_kernel(choices, count, core, *refs):
    blocks, train, out, rows, sems = refs[:count], *refs[count:]

    @pl.when(pl.program_id(0) == 0)
    def _():
        for slot, pair in enumerate(choices):
            for number, choice in enumerate(pair):

                @pl.when(core[0] == number)
                def _(slot=slot, choice=choice):
                    pltpu.make_async_copy(blocks[choice], rows.at[pl.ds(slot * 128, 128)], sems.at[slot]).start()

        for slot in range(len(choices)):
            pltpu.make_async_copy(blocks[0], rows.at[pl.ds(slot * 128, 128)], sems.at[slot]).wait()

    out[...] = lax.dot_general(rows[...], train[...], (((1,), (1,)), ((), ())), preferred_element_type=jnp.float32)


def products(core, pairs, train):
    depth, width = train.shape[1], train.shape[0]
    blocks, choices = [], []
    for pair in pairs:
        spots = []
        for block in pair:
            found = [n for n, known in enumerate(blocks) if known is block]
            if not found:
                blocks.append(block)
            spots.append(found[0] if found else len(blocks) - 1)
        choices.append(spots)
    rows = 128 * len(pairs)
    return pl.pallas_call(
        functools.partial(product_kernel, choices, len(blocks)),
        grid=(width // TILE,),
        in_specs=[pl.BlockSpec(memory_space=pltpu.SMEM)]
        + [pl.BlockSpec(memory_space=pl.ANY)] * len(blocks)
        + [pl.BlockSpec((TILE, depth), lambda i: (i, 0))],
        out_specs=pl.BlockSpec((rows, TILE), lambda i: (0, i)),
        out_shape=jax.ShapeDtypeStruct((rows, width), jnp.float32),
        scratch_shapes=[pltpu.VMEM((rows, depth), jnp.bfloat16), pltpu.SemaphoreType.DMA((len(pairs),))],
        compiler_params=pltpu.CompilerParams(vmem_limit_bytes=VMEM),
        cost_estimate=pl.CostEstimate(
            flops=2 * rows * depth * width, bytes_accessed=2 * depth * (width + rows) + 4 * rows * width, transcendentals=0
        ),
    )(core[None], *blocks, train)


def pick_kernel(spots, count, order, *refs):
    parts, away, keep, sems = refs[:count], *refs[count:]
    for slot in range(4):
        target = (away, keep)[slot // 2].at[pl.ds(slot % 2 * 128, 128)]
        for number, (part, block) in enumerate(spots):

            @pl.when(order[slot] == number)
            def _(slot=slot, part=part, block=block, target=target):
                pltpu.make_async_copy(parts[part].at[pl.ds(block * 128, 128)], target, sems.at[slot]).start()

    for slot in range(4):
        target = (away, keep)[slot // 2].at[pl.ds(slot % 2 * 128, 128)]
        pltpu.make_async_copy(parts[0].at[pl.ds(0, 128)], target, sems.at[slot]).wait()


def pick(order, parts, spots):
    width = parts[0].shape[1]
    half = jax.ShapeDtypeStruct((256, width), jnp.float32)
    return pl.pallas_call(
        functools.partial(pick_kernel, spots, len(parts)),
        in_specs=[pl.BlockSpec(memory_space=pltpu.SMEM)] + [pl.BlockSpec(memory_space=pl.ANY)] * len(parts),
        out_specs=[pl.BlockSpec(memory_space=pl.ANY)] * 2,
        out_shape=[half, half],
        scratch_shapes=[pltpu.SemaphoreType.DMA((4,))],
        compiler_params=pltpu.CompilerParams(vmem_limit_bytes=VMEM),
        cost_estimate=pl.CostEstimate(flops=0, bytes_accessed=8 * 512 * width, transcendentals=0),
    )(order, *parts)


def narrow_kernel(kept, got, message):
    total = kept[...] + got[...]
    peak = jnp.maximum(jnp.max(jnp.abs(total), axis=0, keepdims=True), 1e-30)
    power = 13.0 - jnp.floor(jnp.log2(peak))
    message[:128] = jnp.round(total * jnp.exp2(power)).astype(jnp.int32).astype(jnp.int16)
    message[128:] = jnp.broadcast_to(power, (16, power.shape[1])).astype(jnp.int32).astype(jnp.int16)


def narrow(kept, got):
    width = kept.shape[1]
    first = pl.BlockSpec((128, width), lambda i: (0, 0))
    return pl.pallas_call(
        narrow_kernel,
        grid=(1,),
        in_specs=[first, first],
        out_specs=pl.BlockSpec((144, width), lambda i: (0, 0)),
        out_shape=jax.ShapeDtypeStruct((144, width), jnp.int16),
        compiler_params=pltpu.CompilerParams(vmem_limit_bytes=VMEM),
        cost_estimate=pl.CostEstimate(flops=4 * 128 * width, bytes_accessed=10 * 128 * width, transcendentals=width),
    )(kept, got)


def widen(message):
    return message[:128].astype(jnp.float32) * jnp.exp2(-message[128:129].astype(jnp.float32))


def join(*values):
    return lax.optimization_barrier(values)


def shards(train_features, query_codes, query_exponents):
    layer, example = lax.axis_index("layer"), lax.axis_index("example")
    half, core = layer // 2, layer % 2
    z, low, y = example // 8, (example // 4) % 2, example % 4
    train = train_features[0]
    row_scale = jnp.exp2(-query_exponents[0].astype(jnp.float32))
    own = (query_codes[0].astype(jnp.float32) * row_scale[:, None]).astype(jnp.bfloat16)

    def by_core(zero, one):
        return jnp.where(core == 0, zero, one)

    wanted = jnp.stack([2 * (1 - half) + 1 - core, 2 * half + 1 - core, 2 * (1 - half) + core, 2 * half + core])
    steps = (wanted - z) % 4

    def order(zero, one):
        return by_core(jnp.array(zero, jnp.int32), jnp.array(one, jnp.int32))[steps]

    same = order([0, 1, 2, 3], [0, 1, 2, 3])
    crossed = order([0, 1, 2, 3], [0, 3, 2, 1])

    pair = send(own, PAIR)
    below, above = send(own, FIRST_UP), send(own, FIRST_DOWN)
    left, right = send(own, SECOND_UP), send(own, SECOND_DOWN)
    below_pair, above_pair = send(pair, FIRST_UP), send(pair, FIRST_DOWN)
    left_pair, right_pair = send(pair, SECOND_UP), send(pair, SECOND_DOWN)
    far = send(below, FIRST_UP)
    x0 = jnp.concatenate([own, pair], 0)
    x3 = jnp.concatenate([below, below_pair], 0)
    x1 = jnp.concatenate([above, above_pair], 0)
    up_1, down_1 = jnp.concatenate([left, left_pair], 0), jnp.concatenate([right, right_pair], 0)

    far_pair = send(above_pair, FIRST_DOWN)
    up_2, down_2 = send(x1, SECOND_UP), send(x1, SECOND_DOWN)
    up_3, down_3 = send(up_1, SECOND_UP), send(x3, SECOND_DOWN)
    part_a = products(core, [(x0, x0), (down_1, x1), (up_1, x3), (x1, down_1), (x3, up_1)], train)
    far_pair, up_2, down_2, up_3, down_3, part_a = join(far_pair, up_2, down_2, up_3, down_3, part_a)

    x2 = jnp.concatenate([far, far_pair], 0)
    up_4, down_5 = send(x2, SECOND_UP), send(by_core(down_3, x2), SECOND_DOWN)
    up_5, down_4 = send(x3, SECOND_UP), send(down_2, SECOND_DOWN)
    part_b = products(core, [(up_3, x2), (down_2, down_2), (up_2, down_3), (down_3, up_2), (x2, up_3)], train)
    up_4, down_5, up_5, down_4, part_b = join(up_4, down_5, up_5, down_4, part_b)

    away_0, keep_0 = pick(same, [part_a, part_b], [(0, 0), (0, 1), (1, 0), (0, 2)])
    up_6, down_6 = send(up_4, SECOND_UP), send(by_core(x2, down_3), SECOND_DOWN)
    got_0 = send(away_0, CORE)
    part_c = products(core, [(down_4, down_5), (down_5, up_4), (up_5, up_5), (up_4, down_4)], train)
    up_6, down_6, got_0, part_c = join(up_6, down_6, got_0, part_c)

    message_0 = narrow(keep_0, got_0)
    away_1, keep_1 = pick(same, [part_a, part_b, part_c], [(0, 3), (1, 1), (2, 0), (1, 2)])
    away_3, keep_3 = pick(same, [part_a, part_b, part_c], [(0, 4), (1, 3), (2, 1), (2, 2)])
    far_0, got_1, got_3 = send(message_0, ACROSS), send(away_1, CORE), send(away_3, CORE)
    part_d = products(core, [(down_6, down_6), (up_6, up_6)], train)
    got_1, got_3, part_d = join(got_1, got_3, part_d)

    message_1, message_3 = narrow(keep_1, got_1), narrow(keep_3, got_3)
    far_1, far_3 = send(message_1, ACROSS), send(message_3, ACROSS)
    away_2, keep_2 = pick(crossed, [part_b, part_c, part_d], [(0, 4), (2, 0), (2, 1), (1, 3)])
    got_2 = send(away_2, CORE)
    message_2 = narrow(keep_2, got_2)
    far_0, message_2 = join(far_0, message_2)
    far_2 = send(message_2, ACROSS)

    out = jnp.zeros((2, 4, 64, train.shape[0]), jnp.float32)
    for dy, keep, got, message in ((0, keep_0, got_0, far_0), (1, keep_1, got_1, far_1), (3, keep_3, got_3, far_3), (2, keep_2, got_2, far_2)):
        total = keep[128:] + got[128:] + widen(message)
        place_y = (y + dy) % 4
        out = lax.dynamic_update_slice(out, total[None, None, :64], (low, place_y, 0, 0))
        out = lax.dynamic_update_slice(out, total[None, None, 64:], (1 - low, place_y, 0, 0))
    return out.reshape(512, -1)


def solution(mesh):
    in_specs = (P("layer", "example", None), P("layer", "example", None), P("layer", "example"))
    out_specs = P("layer", "example")
    return jax.shard_map(shards, mesh=mesh, in_specs=in_specs, out_specs=out_specs, check_vma=False)
```

time: 196 us -> 181 us (0.923)
  Pallas kernels: 0 us -> 50.7 us
  matrix products: 40.9 us -> 0 us
  waiting for transfers between devices: 87 us -> 62.2 us
  other arithmetic: 20.8 us -> 10.4 us
  local copies, waits for them, and re-layouts: 7.32 us -> 16.2 us
  starting transfers between devices: 35.8 us -> 40.1 us
  between operations: 3.24 us -> 0.61 us
    pallas_call x0 -> x12, Pallas kernels: none -> 50.7 us  [the longest x4 44 us: products(): pl.pallas_call(functools.partial(product_kernel, choices, len(blocks)), g...]
    dot_general x5 -> x0, matrix products: 40.9 us -> none  [times(): lax.dot_general(jnp.concatenate(blocks, 0), train, (((1,), (1,)), ((), ()...]
    ppermute x27 -> x29, waiting for transfers between devices: 87 us -> 62.2 us  [send(): return lax.ppermute(value, BOTH, pairs)]
    unnamed x16 -> x64, local copies, waits for them, and re-layouts: 4.72 us -> 14.1 us
    select_n x6 -> x2, other arithmetic: 7.5 us -> 1.46 us  [by_core(): return jnp.where(core == 0, zero, one)]
    ppermute x27 -> x29, starting transfers between devices: 35.8 us -> 40.1 us  [send(): return lax.ppermute(value, BOTH, pairs)]
    another operation x4 -> x0, other arithmetic: 2.75 us -> none  [reduce(): got = send(jnp.stack([plane(1 - core), plane(3 - core)]), CORE)]
    unnamed x1 -> x0, other arithmetic: 2.04 us -> none
  transfers between devices with their start and end apart: 27 -> 29, of which waited for: 10 -> 14; matrix products, arithmetic and copies ran while one was open for 31% -> 6% of each run, Pallas kernels for 0% -> 26%
where the time goes in v2:
time: 181 us; the launch traced here: 180 us
  waiting for transfers between devices  62.2 us (34%)
  Pallas kernels  50.7 us (28%)
  starting transfers between devices  40.1 us (22%)
  local copies, waits for them, and re-layouts  16.2 us (9%)
  other arithmetic  10.4 us (6%)
    ppermute x29, waiting for transfers between devices, send(): return lax.ppermute(value, BOTH, pairs)  62.2 us
    pallas_call x4, Pallas kernels, products(): pl.pallas_call(functools.partial(product_kernel, choices, len(blocks)), g...  44 us
    ppermute x29, starting transfers between devices, send(): return lax.ppermute(value, BOTH, pairs)  40.1 us
    unnamed x64, local copies, waits for them, and re-layouts  14.1 us
    pallas_call x4, Pallas kernels, pick(): pl.pallas_call(functools.partial(pick_kernel, spots, len(parts)), in_spec...  4.48 us
  transfers between devices with their start and end apart: 29, of which 14 were waited for; matrix products, arithmetic and copies ran while one was open for 6% of the time, Pallas kernels for 26%

profile of v2, /device:TPU:2, one launch (start us, length us, event | category | flops | bytes accessed | tf_op | source)
XLA Modules:
  0.0 180.3 jit_solution(17688877690265137197)
XLA Ops:
  2.4 3.1 %collective-permute-start.3 = (bf16[64,4096]{1,0:T(8,128)(2,1)S(1)}, bf16[64,4096]{1,0:T(8,128)(2,1)S(1)}, u32[]{:S(2)}, u32[]{:S(2)}) collective-permute-start(bf16[64,4096]{1,0:T(8,128)(2,1)S(1)} %fusion), channel_id=1, source_target_pairs={{0,3},{1,0},{2,1},{3,2},{8,11},{9,8},{10,9},{11,10},{16,19},{17,16... | collective-permute-start | bytes 1572872 | tf_op jit(solution)/shard_map/ppermute | solution.py:38
  5.5 1.9 %collective-permute-start.6 = (bf16[64,4096]{1,0:T(8,128)(2,1)S(1)}, bf16[64,4096]{1,0:T(8,128)(2,1)S(1)}, u32[]{:S(2)}, u32[]{:S(2)}) collective-permute-start(bf16[64,4096]{1,0:T(8,128)(2,1)S(1)} %fusion), channel_id=1, source_target_pairs={{0,8},{1,9},{2,10},{3,11},{8,16},{9,17},{10,18},{11,19},{16,24},{1... | collective-permute-start | bytes 1572872 | tf_op jit(solution)/shard_map/ppermute | solution.py:38
  7.4 2.1 %collective-permute-start.12 = (bf16[64,4096]{1,0:T(8,128)(2,1)S(1)}, bf16[64,4096]{1,0:T(8,128)(2,1)}, u32[]{:S(2)}, u32[]{:S(2)}) collective-permute-start(bf16[64,4096]{1,0:T(8,128)(2,1)S(1)} %fusion), channel_id=1, source_target_pairs={{0,24},{1,25},{2,26},{3,27},{8,0},{9,1},{10,2},{11,3},{16,8},{17,9... | collective-permute-start | bytes 1572872 | tf_op jit(solution)/shard_map/ppermute | solution.py:38
  9.5 6.2 %collective-permute-done = bf16[64,4096]{1,0:T(8,128)(2,1)} collective-permute-done((bf16[64,4096]{1,0:T(8,128)(2,1)S(1)}, bf16[64,4096]{1,0:T(8,128)(2,1)}, u32[]{:S(2)}, u32[]{:S(2)}) %collective-permute-start) | collective-permute-done | bytes 524320 | tf_op jit(solution)/shard_map/ppermute | solution.py:38
  15.7 3.0 %collective-permute-start.1 = (bf16[64,4096]{1,0:T(8,128)(2,1)}, bf16[64,4096]{1,0:T(8,128)(2,1)S(1)}, u32[]{:S(2)}, u32[]{:S(2)}) collective-permute-start(bf16[64,4096]{1,0:T(8,128)(2,1)} %collective-permute-done), channel_id=1, source_target_pairs={{0,3},{1,0},{2,1},{3,2},{8,11},{9,8},{10,9},{11,10},{16,19},{17,16... | collective-permute-start | bytes 1572872 | tf_op jit(solution)/shard_map/ppermute | solution.py:38
  22.1 2.2 %collective-permute-start.13 = (bf16[64,4096]{1,0:T(8,128)(2,1)}, bf16[64,4096]{1,0:T(8,128)(2,1)S(1)}, u32[]{:S(2)}, u32[]{:S(2)}) collective-permute-start(bf16[64,4096]{1,0:T(8,128)(2,1)} %collective-permute-done), channel_id=1, source_target_pairs={{0,24},{1,25},{2,26},{3,27},{8,0},{9,1},{10,2},{11,3},{16,8},{17,9... | collective-permute-start | bytes 1572872 | tf_op jit(solution)/shard_map/ppermute | solution.py:38
  24.3 3.7 %collective-permute-done.1 = bf16[64,4096]{1,0:T(8,128)(2,1)S(1)} collective-permute-done((bf16[64,4096]{1,0:T(8,128)(2,1)}, bf16[64,4096]{1,0:T(8,128)(2,1)S(1)}, u32[]{:S(2)}, u32[]{:S(2)}) %collective-permute-start.1) | collective-permute-done | bytes 524320 | tf_op jit(solution)/shard_map/ppermute | solution.py:38
  28.1 7.1 %collective-permute-done.10 = bf16[64,4096]{1,0:T(8,128)(2,1)S(1)} collective-permute-done((bf16[64,4096]{1,0:T(8,128)(2,1)}, bf16[64,4096]{1,0:T(8,128)(2,1)S(1)}, u32[]{:S(2)}, u32[]{:S(2)}) %collective-permute-start.10) | collective-permute-done | bytes 524320 | tf_op jit(solution)/shard_map/ppermute | solution.py:38
  35.2 2.0 %collective-permute-done.7 = bf16[64,4096]{1,0:T(8,128)(2,1)S(1)} collective-permute-done((bf16[64,4096]{1,0:T(8,128)(2,1)}, bf16[64,4096]{1,0:T(8,128)(2,1)S(1)}, u32[]{:S(2)}, u32[]{:S(2)}) %collective-permute-start.7) | collective-permute-done | bytes 524320 | tf_op jit(solution)/shard_map/ppermute | solution.py:38
  37.2 2.8 %collective-permute-start.5 = (bf16[128,4096]{1,0:T(8,128)(2,1)S(1)}, bf16[128,4096]{1,0:T(8,128)(2,1)}, u32[]{:S(2)}, u32[]{:S(2)}) collective-permute-start(bf16[128,4096]{1,0:T(8,128)(2,1)S(1)} %constant_dynamic-update-slice_fusion.refs_2_), channel_id=1, source_target_pairs={{0,24},{1,25},{2,26},{3,27},{8,0},{9,1},{10,2},{11,3},{16,8},{17,9... | collective-permute-start | bytes 3145736 | tf_op jit(solution)/shard_map/ppermute | solution.py:38
  40.0 2.1 %collective-permute-start.11 = (bf16[128,4096]{1,0:T(8,128)(2,1)S(1)}, bf16[128,4096]{1,0:T(8,128)(2,1)S(1)}, u32[]{:S(2)}, u32[]{:S(2)}) collective-permute-start(bf16[128,4096]{1,0:T(8,128)(2,1)S(1)} %constant_dynamic-update-slice_fusion.4.refs_4_), channel_id=1, source_target_pairs={{0,24},{1,25},{2,26},{3,27},{8,0},{9,1},{10,2},{11,3},{16,8},{17,9... | collective-permute-start | bytes 3145736 | tf_op jit(solution)/shard_map/ppermute | solution.py:38
  44.9 11.6 %shard_map.73.refs_0_ = f32[640,1536]{1,0:T(8,128)S(1)} custom-call(s32[1]{0:T(128)} %bitcast.7.core, bf16[128,4096]{1,0:T(8,128)(2,1)S(1)} %pad_maximum_fusion.refs_0_, bf16[128,4096]{1,0:T(8,128)(2,1)S(1)} %pad_maximum_fusion.1.refs_1_, bf16[128,4096]{1,0:T(8,128)(2,1)S(1)} %constant_dynamic-update-slice_fusion.refs_2_, ...), custom_call_target="tpu_custom_call" | custom-call | flops 8053063680 | bytes 21757952 | tf_op jit(solution)/shard_map/pallas_call | solution.py:75
  56.5 3.2 %collective-permute-done.2 = bf16[64,4096]{1,0:T(8,128)(2,1)S(1)} collective-permute-done((bf16[64,4096]{1,0:T(8,128)(2,1)S(1)}, bf16[64,4096]{1,0:T(8,128)(2,1)S(1)}, u32[]{:S(2)}, u32[]{:S(2)}) %collective-permute-start.2) | collective-permute-done | bytes 524320 | tf_op jit(solution)/shard_map/ppermute | solution.py:38
  59.7 3.7 %collective-permute-start.17 = (bf16[128,4096]{1,0:T(8,128)(2,1)S(1)}, bf16[128,4096]{1,0:T(8,128)(2,1)}, u32[]{:S(2)}, u32[]{:S(2)}) collective-permute-start(bf16[128,4096]{1,0:T(8,128)(2,1)S(1)} %constant_dynamic-update-slice_fusion.4.refs_4_), channel_id=1, source_target_pairs={{0,8},{1,9},{2,10},{3,11},{8,16},{9,17},{10,18},{11,19},{16,24},{1... | collective-permute-start | bytes 3145736 | tf_op jit(solution)/shard_map/ppermute | solution.py:38
  63.4 6.0 %collective-permute-done.11.refs_4_ = bf16[128,4096]{1,0:T(8,128)(2,1)S(1)} collective-permute-done((bf16[128,4096]{1,0:T(8,128)(2,1)S(1)}, bf16[128,4096]{1,0:T(8,128)(2,1)S(1)}, u32[]{:S(2)}, u32[]{:S(2)}) %collective-permute-start.11) | collective-permute-done | bytes 1048608 | tf_op jit(solution)/shard_map/ppermute | solution.py:38
  69.5 1.9 %collective-permute-start.15 = (bf16[128,4096]{1,0:T(8,128)(2,1)S(1)}, bf16[128,4096]{1,0:T(8,128)(2,1)}, u32[]{:S(2)}, u32[]{:S(2)}) collective-permute-start(bf16[128,4096]{1,0:T(8,128)(2,1)S(1)} %constant_dynamic-update-slice_fusion.6.refs_1_), channel_id=1, source_target_pairs={{0,8},{1,9},{2,10},{3,11},{8,16},{9,17},{10,18},{11,19},{16,24},{1... | collective-permute-start | bytes 3145736 | tf_op jit(solution)/shard_map/ppermute | solution.py:38
  72.9 1.8 %collective-permute-start.16 = (bf16[128,4096]{1,0:T(8,128)(2,1)}, bf16[128,4096]{1,0:T(8,128)(2,1)}, u32[]{:S(2)}, u32[]{:S(2)}) collective-permute-start(bf16[128,4096]{1,0:T(8,128)(2,1)} %get-tuple-element.62), channel_id=1, source_target_pairs={{0,24},{1,25},{2,26},{3,27},{8,0},{9,1},{10,2},{11,3},{16,8},{17,9... | collective-permute-start | bytes 3145736 | tf_op jit(solution)/shard_map/ppermute | solution.py:38
  74.7 1.7 collective-permute-start.18
  79.7 13.1 %shard_map.74.refs_1_.refs_0_ = f32[640,1536]{1,0:T(8,128)S(1)} custom-call(s32[1]{0:T(128)} %bitcast.7.core, bf16[128,4096]{1,0:T(8,128)(2,1)S(1)} %copy-done.26, bf16[128,4096]{1,0:T(8,128)(2,1)S(1)} %constant_dynamic-update-slice_fusion.6.refs_1_, bf16[128,4096]{1,0:T(8,128)(2,1)} %collective-permute-done.5.refs_2_, bf16[128,4096]{1,0:T(8,128)(2,1)S(1)} %copy-done.24, ...), custom_call_target="tpu_custom_call" | custom-call | flops 8053063680 | bytes 21757952 | tf_op jit(solution)/shard_map/pallas_call | solution.py:75
  92.8 6.5 %collective-permute-done.18.refs_0_ = bf16[128,4096]{1,0:T(8,128)(2,1)} collective-permute-done((bf16[128,4096]{1,0:T(8,128)(2,1)}, bf16[128,4096]{1,0:T(8,128)(2,1)}, u32[]{:S(2)}, u32[]{:S(2)}) %collective-permute-start.18) | collective-permute-done | bytes 1048608 | tf_op jit(solution)/shard_map/ppermute | solution.py:38
  100.3 3.1 %collective-permute-start.20 = (bf16[128,4096]{1,0:T(8,128)(2,1)S(1)}, bf16[128,4096]{1,0:T(8,128)(2,1)S(1)}, u32[]{:S(2)}, u32[]{:S(2)}) collective-permute-start(bf16[128,4096]{1,0:T(8,128)(2,1)S(1)} %copy-done.28), channel_id=1, source_target_pairs={{0,24},{1,25},{2,26},{3,27},{8,0},{9,1},{10,2},{11,3},{16,8},{17,9... | collective-permute-start | bytes 3145736 | tf_op jit(solution)/shard_map/ppermute | solution.py:38
  103.4 12.1 %shard_map.76.refs_2_.refs_1_ = f32[512,1536]{1,0:T(8,128)S(1)} custom-call(s32[1]{0:T(128)} %bitcast.7.core, bf16[128,4096]{1,0:T(8,128)(2,1)} %collective-permute-done.18.refs_0_, bf16[128,4096]{1,0:T(8,128)(2,1)} %collective-permute-done.16.refs_1_, bf16[128,4096]{1,0:T(8,128)(2,1)} %collective-permute-done.15.refs_2_, ...), custom_call_target="tpu_custom_call" | custom-call | flops 6442450944 | bytes 19922944 | tf_op jit(solution)/shard_map/pallas_call | solution.py:75
  115.7 3.9 %collective-permute-done.19.refs_1_ = bf16[128,4096]{1,0:T(8,128)(2,1)S(1)} collective-permute-done((bf16[128,4096]{1,0:T(8,128)(2,1)}, bf16[128,4096]{1,0:T(8,128)(2,1)S(1)}, u32[]{:S(2)}, u32[]{:S(2)}) %collective-permute-start.19) | collective-permute-done | bytes 1048608 | tf_op jit(solution)/shard_map/ppermute | solution.py:38
  123.2 7.2 %shard_map.80.refs_2_ = f32[256,1536]{1,0:T(8,128)S(1)} custom-call(s32[1]{0:T(128)} %bitcast.7.core, bf16[128,4096]{1,0:T(8,128)(2,1)S(1)} %collective-permute-done.20.refs_0_, bf16[128,4096]{1,0:T(8,128)(2,1)S(1)} %collective-permute-done.19.refs_1_, bf16[1536,4096]{1,0:T(8,128)(2,1)} %bitcast.49), custom_call_target="tpu_custom_call" | custom-call | flops 3221225472 | bytes 16252928 | tf_op jit(solution)/shard_map/pallas_call | solution.py:75
  132.6 2.3 %collective-permute-start.27 = (s16[144,1536]{1,0:T(8,128)(2,1)}, s16[144,1536]{1,0:T(8,128)(2,1)}, u32[]{:S(2)}, u32[]{:S(2)}) collective-permute-start(s16[144,1536]{1,0:T(8,128)(2,1)} %shard_map.84), channel_id=1, source_target_pairs={{0,64},{1,65},{2,66},{3,67},{8,72},{9,73},{10,74},{11,75},{16,80},... | collective-permute-start | bytes 1327112 | tf_op jit(solution)/shard_map/ppermute | solution.py:38
  137.7 2.1 %copy-done.1 = f32[640,1536]{1,0:T(8,128)S(1)} copy-done((f32[640,1536]{1,0:T(8,128)S(1)}, f32[640,1536]{1,0:T(8,128)}, u32[]{:S(2)}) %copy-start.1) | copy-done | bytes 3932184
  141.3 1.7 shard_map.81
  147.2 2.3 %collective-permute-start.22 = (s16[144,1536]{1,0:T(8,128)(2,1)S(1)}, s16[144,1536]{1,0:T(8,128)(2,1)S(1)}, u32[]{:S(2)}, u32[]{:S(2)}) collective-permute-start(s16[144,1536]{1,0:T(8,128)(2,1)S(1)} %shard_map.77), channel_id=1, source_target_pairs={{0,64},{1,65},{2,66},{3,67},{8,72},{9,73},{10,74},{11,75},{16,80},... | collective-permute-start | bytes 1327112 | tf_op jit(solution)/shard_map/ppermute | solution.py:38
  150.3 6.6 %collective-permute-done.26 = s16[144,1536]{1,0:T(8,128)(2,1)} collective-permute-done((s16[144,1536]{1,0:T(8,128)(2,1)}, s16[144,1536]{1,0:T(8,128)(2,1)}, u32[]{:S(2)}, u32[]{:S(2)}) %collective-permute-start.26) | collective-permute-done | bytes 442400 | tf_op jit(solution)/shard_map/ppermute | solution.py:38
  160.7 4.7 %collective-permute-done.22 = s16[144,1536]{1,0:T(8,128)(2,1)S(1)} collective-permute-done((s16[144,1536]{1,0:T(8,128)(2,1)S(1)}, s16[144,1536]{1,0:T(8,128)(2,1)S(1)}, u32[]{:S(2)}, u32[]{:S(2)}) %collective-permute-start.22) | collective-permute-done | bytes 442400 | tf_op jit(solution)/shard_map/ppermute | solution.py:38
  165.4 2.3 %collective-permute-start.28 = (s16[144,1536]{1,0:T(8,128)(2,1)S(1)}, s16[144,1536]{1,0:T(8,128)(2,1)S(1)}, u32[]{:S(2)}, u32[]{:S(2)}) collective-permute-start(s16[144,1536]{1,0:T(8,128)(2,1)S(1)} %shard_map.82), channel_id=1, source_target_pairs={{0,64},{1,65},{2,66},{3,67},{8,72},{9,73},{10,74},{11,75},{16,80},... | collective-permute-start | bytes 1327112 | tf_op jit(solution)/shard_map/ppermute | solution.py:38
  168.6 9.7 %collective-permute-done.28 = s16[144,1536]{1,0:T(8,128)(2,1)S(1)} collective-permute-done((s16[144,1536]{1,0:T(8,128)(2,1)S(1)}, s16[144,1536]{1,0:T(8,128)(2,1)S(1)}, u32[]{:S(2)}, u32[]{:S(2)}) %collective-permute-start.28) | collective-permute-done | bytes 442400 | tf_op jit(solution)/shard_map/ppermute | solution.py:38
  (134 shorter events, 35.8 us)
Async XLA Ops:
  1.9 13.8 %collective-permute-start = (bf16[64,4096]{1,0:T(8,128)(2,1)S(1)}, bf16[64,4096]{1,0:T(8,128)(2,1)}, u32[]{:S(2)}, u32[]{:S(2)}) collective-permute-start(bf16[64,4096]{1,0:T(8,128)(2,1)S(1)} %fusion), channel_id=1, source_target_pairs={{0,4},{1,5},{2,6},{3,7},{8,12},{9,13},{10,14},{11,15},{16,20},{17,... | collective-permute-start | bytes 1572872 | tf_op jit(solution)/shard_map/ppermute | solution.py:38
  2.4 17.5 %collective-permute-start.3 = (bf16[64,4096]{1,0:T(8,128)(2,1)S(1)}, bf16[64,4096]{1,0:T(8,128)(2,1)S(1)}, u32[]{:S(2)}, u32[]{:S(2)}) collective-permute-start(bf16[64,4096]{1,0:T(8,128)(2,1)S(1)} %fusion), channel_id=1, source_target_pairs={{0,3},{1,0},{2,1},{3,2},{8,11},{9,8},{10,9},{11,10},{16,19},{17,16... | collective-permute-start | bytes 1572872 | tf_op jit(solution)/shard_map/ppermute | solution.py:38
  5.5 15.4 %collective-permute-start.9 = (bf16[64,4096]{1,0:T(8,128)(2,1)S(1)}, bf16[64,4096]{1,0:T(8,128)(2,1)S(1)}, u32[]{:S(2)}, u32[]{:S(2)}) collective-permute-start(bf16[64,4096]{1,0:T(8,128)(2,1)S(1)} %fusion), channel_id=1, source_target_pairs={{0,1},{1,2},{2,3},{3,0},{8,9},{9,10},{10,11},{11,8},{16,17},{17,18... | collective-permute-start | bytes 1572872 | tf_op jit(solution)/shard_map/ppermute | solution.py:38
  5.5 16.6 %collective-permute-start.6 = (bf16[64,4096]{1,0:T(8,128)(2,1)S(1)}, bf16[64,4096]{1,0:T(8,128)(2,1)S(1)}, u32[]{:S(2)}, u32[]{:S(2)}) collective-permute-start(bf16[64,4096]{1,0:T(8,128)(2,1)S(1)} %fusion), channel_id=1, source_target_pairs={{0,8},{1,9},{2,10},{3,11},{8,16},{9,17},{10,18},{11,19},{16,24},{1... | collective-permute-start | bytes 1572872 | tf_op jit(solution)/shard_map/ppermute | solution.py:38
  7.4 32.6 %collective-permute-start.12 = (bf16[64,4096]{1,0:T(8,128)(2,1)S(1)}, bf16[64,4096]{1,0:T(8,128)(2,1)}, u32[]{:S(2)}, u32[]{:S(2)}) collective-permute-start(bf16[64,4096]{1,0:T(8,128)(2,1)S(1)} %fusion), channel_id=1, source_target_pairs={{0,24},{1,25},{2,26},{3,27},{8,0},{9,1},{10,2},{11,3},{16,8},{17,9... | collective-permute-start | bytes 1572872 | tf_op jit(solution)/shard_map/ppermute | solution.py:38
  15.7 12.3 %collective-permute-start.1 = (bf16[64,4096]{1,0:T(8,128)(2,1)}, bf16[64,4096]{1,0:T(8,128)(2,1)S(1)}, u32[]{:S(2)}, u32[]{:S(2)}) collective-permute-start(bf16[64,4096]{1,0:T(8,128)(2,1)} %collective-permute-done), channel_id=1, source_target_pairs={{0,3},{1,0},{2,1},{3,2},{8,11},{9,8},{10,9},{11,10},{16,19},{17,16... | collective-permute-start | bytes 1572872 | tf_op jit(solution)/shard_map/ppermute | solution.py:38
  19.9 15.2 %collective-permute-start.10 = (bf16[64,4096]{1,0:T(8,128)(2,1)}, bf16[64,4096]{1,0:T(8,128)(2,1)S(1)}, u32[]{:S(2)}, u32[]{:S(2)}) collective-permute-start(bf16[64,4096]{1,0:T(8,128)(2,1)} %collective-permute-done), channel_id=1, source_target_pairs={{0,1},{1,2},{2,3},{3,0},{8,9},{9,10},{10,11},{11,8},{16,17},{17,18... | collective-permute-start | bytes 1572872 | tf_op jit(solution)/shard_map/ppermute | solution.py:38
  20.9 16.3 %collective-permute-start.7 = (bf16[64,4096]{1,0:T(8,128)(2,1)}, bf16[64,4096]{1,0:T(8,128)(2,1)S(1)}, u32[]{:S(2)}, u32[]{:S(2)}) collective-permute-start(bf16[64,4096]{1,0:T(8,128)(2,1)} %collective-permute-done), channel_id=1, source_target_pairs={{0,8},{1,9},{2,10},{3,11},{8,16},{9,17},{10,18},{11,19},{16,24},{1... | collective-permute-start | bytes 1572872 | tf_op jit(solution)/shard_map/ppermute | solution.py:38
  22.1 20.0 %collective-permute-start.13 = (bf16[64,4096]{1,0:T(8,128)(2,1)}, bf16[64,4096]{1,0:T(8,128)(2,1)S(1)}, u32[]{:S(2)}, u32[]{:S(2)}) collective-permute-start(bf16[64,4096]{1,0:T(8,128)(2,1)} %collective-permute-done), channel_id=1, source_target_pairs={{0,24},{1,25},{2,26},{3,27},{8,0},{9,1},{10,2},{11,3},{16,8},{17,9... | collective-permute-start | bytes 1572872 | tf_op jit(solution)/shard_map/ppermute | solution.py:38
  28.0 16.8 %collective-permute-start.14 = (bf16[64,4096]{1,0:T(8,128)(2,1)S(1)}, bf16[64,4096]{1,0:T(8,128)(2,1)S(1)}, u32[]{:S(2)}, u32[]{:S(2)}) collective-permute-start(bf16[64,4096]{1,0:T(8,128)(2,1)S(1)} %collective-permute-done.9), channel_id=1, source_target_pairs={{0,1},{1,2},{2,3},{3,0},{8,9},{9,10},{10,11},{11,8},{16,17},{17,18... | collective-permute-start | bytes 1572872 | tf_op jit(solution)/shard_map/ppermute | solution.py:38
  35.1 34.3 %collective-permute-start.4 = (bf16[128,4096]{1,0:T(8,128)(2,1)S(1)}, bf16[128,4096]{1,0:T(8,128)(2,1)S(1)}, u32[]{:S(2)}, u32[]{:S(2)}) collective-permute-start(bf16[128,4096]{1,0:T(8,128)(2,1)S(1)} %constant_dynamic-update-slice_fusion.refs_2_), channel_id=1, source_target_pairs={{0,8},{1,9},{2,10},{3,11},{8,16},{9,17},{10,18},{11,19},{16,24},{1... | collective-permute-start | bytes 3145736 | tf_op jit(solution)/shard_map/ppermute | solution.py:38
  37.2 32.2 %collective-permute-start.5 = (bf16[128,4096]{1,0:T(8,128)(2,1)S(1)}, bf16[128,4096]{1,0:T(8,128)(2,1)}, u32[]{:S(2)}, u32[]{:S(2)}) collective-permute-start(bf16[128,4096]{1,0:T(8,128)(2,1)S(1)} %constant_dynamic-update-slice_fusion.refs_2_), channel_id=1, source_target_pairs={{0,24},{1,25},{2,26},{3,27},{8,0},{9,1},{10,2},{11,3},{16,8},{17,9... | collective-permute-start | bytes 3145736 | tf_op jit(solution)/shard_map/ppermute | solution.py:38
  40.0 29.4 %collective-permute-start.11 = (bf16[128,4096]{1,0:T(8,128)(2,1)S(1)}, bf16[128,4096]{1,0:T(8,128)(2,1)S(1)}, u32[]{:S(2)}, u32[]{:S(2)}) collective-permute-start(bf16[128,4096]{1,0:T(8,128)(2,1)S(1)} %constant_dynamic-update-slice_fusion.4.refs_4_), channel_id=1, source_target_pairs={{0,24},{1,25},{2,26},{3,27},{8,0},{9,1},{10,2},{11,3},{16,8},{17,9... | collective-permute-start | bytes 3145736 | tf_op jit(solution)/shard_map/ppermute | solution.py:38
  42.1 27.3 %collective-permute-start.8 = (bf16[128,4096]{1,0:T(8,128)(2,1)S(1)}, bf16[128,4096]{1,0:T(8,128)(2,1)S(1)}, u32[]{:S(2)}, u32[]{:S(2)}) collective-permute-start(bf16[128,4096]{1,0:T(8,128)(2,1)S(1)} %constant_dynamic-update-slice_fusion.2.refs_3_), channel_id=1, source_target_pairs={{0,8},{1,9},{2,10},{3,11},{8,16},{9,17},{10,18},{11,19},{16,24},{1... | collective-permute-start | bytes 3145736 | tf_op jit(solution)/shard_map/ppermute | solution.py:38
  44.9 14.9 %collective-permute-start.2 = (bf16[64,4096]{1,0:T(8,128)(2,1)S(1)}, bf16[64,4096]{1,0:T(8,128)(2,1)S(1)}, u32[]{:S(2)}, u32[]{:S(2)}) collective-permute-start(bf16[64,4096]{1,0:T(8,128)(2,1)S(1)} %collective-permute-done.1), channel_id=1, source_target_pairs={{0,3},{1,0},{2,1},{3,2},{8,11},{9,8},{10,9},{11,10},{16,19},{17,16... | collective-permute-start | bytes 1572872 | tf_op jit(solution)/shard_map/ppermute | solution.py:38
  56.5 16.4 %copy-start.2 = (f32[640,1536]{1,0:T(8,128)}, f32[640,1536]{1,0:T(8,128)S(1)}, u32[]{:S(2)}) copy-start(f32[640,1536]{1,0:T(8,128)S(1)} %shard_map.73.refs_0_) | copy-start | bytes 11796484
  59.7 33.0 %collective-permute-start.17 = (bf16[128,4096]{1,0:T(8,128)(2,1)S(1)}, bf16[128,4096]{1,0:T(8,128)(2,1)}, u32[]{:S(2)}, u32[]{:S(2)}) collective-permute-start(bf16[128,4096]{1,0:T(8,128)(2,1)S(1)} %constant_dynamic-update-slice_fusion.4.refs_4_), channel_id=1, source_target_pairs={{0,8},{1,9},{2,10},{3,11},{8,16},{9,17},{10,18},{11,19},{16,24},{1... | collective-permute-start | bytes 3145736 | tf_op jit(solution)/shard_map/ppermute | solution.py:38
  69.5 23.3 %collective-permute-start.15 = (bf16[128,4096]{1,0:T(8,128)(2,1)S(1)}, bf16[128,4096]{1,0:T(8,128)(2,1)}, u32[]{:S(2)}, u32[]{:S(2)}) collective-permute-start(bf16[128,4096]{1,0:T(8,128)(2,1)S(1)} %constant_dynamic-update-slice_fusion.6.refs_1_), channel_id=1, source_target_pairs={{0,8},{1,9},{2,10},{3,11},{8,16},{9,17},{10,18},{11,19},{16,24},{1... | collective-permute-start | bytes 3145736 | tf_op jit(solution)/shard_map/ppermute | solution.py:38
  72.9 19.9 %collective-permute-start.16 = (bf16[128,4096]{1,0:T(8,128)(2,1)}, bf16[128,4096]{1,0:T(8,128)(2,1)}, u32[]{:S(2)}, u32[]{:S(2)}) collective-permute-start(bf16[128,4096]{1,0:T(8,128)(2,1)} %get-tuple-element.62), channel_id=1, source_target_pairs={{0,24},{1,25},{2,26},{3,27},{8,0},{9,1},{10,2},{11,3},{16,8},{17,9... | collective-permute-start | bytes 3145736 | tf_op jit(solution)/shard_map/ppermute | solution.py:38
  74.7 24.5 %collective-permute-start.18 = (bf16[128,4096]{1,0:T(8,128)(2,1)}, bf16[128,4096]{1,0:T(8,128)(2,1)}, u32[]{:S(2)}, u32[]{:S(2)}) collective-permute-start(bf16[128,4096]{1,0:T(8,128)(2,1)} %collective-permute-done.5.refs_2_), channel_id=1, source_target_pairs={{0,24},{1,25},{2,26},{3,27},{8,0},{9,1},{10,2},{11,3},{16,8},{17,9... | collective-permute-start | bytes 3145736 | tf_op jit(solution)/shard_map/ppermute | solution.py:38
  79.7 19.6 %copy-start.3 = (f32[640,1536]{1,0:T(8,128)S(1)}, f32[640,1536]{1,0:T(8,128)}, u32[]{:S(2)}) copy-start(f32[640,1536]{1,0:T(8,128)} %copy-done.2) | copy-start | bytes 11796484
  92.7 29.0 %copy-start = (f32[640,1536]{1,0:T(8,128)}, f32[640,1536]{1,0:T(8,128)S(1)}, u32[]{:S(2)}) copy-start(f32[640,1536]{1,0:T(8,128)S(1)} %shard_map.74.refs_1_.refs_0_) | copy-start | bytes 11796484
  100.2 19.4 %collective-permute-start.21 = (f32[256,1536]{1,0:T(8,128)S(1)}, f32[256,1536]{1,0:T(8,128)S(1)}, u32[]{:S(2)}, u32[]{:S(2)}) collective-permute-start(f32[256,1536]{1,0:T(8,128)S(1)} %get-tuple-element.42), channel_id=1, source_target_pairs={{0,32},{1,33},{2,34},{3,35},{8,40},{9,41},{10,42},{11,43},{16,48},... | collective-permute-start | bytes 4718600 | tf_op jit(solution)/shard_map/ppermute | solution.py:38
  100.3 15.4 %collective-permute-start.20 = (bf16[128,4096]{1,0:T(8,128)(2,1)S(1)}, bf16[128,4096]{1,0:T(8,128)(2,1)S(1)}, u32[]{:S(2)}, u32[]{:S(2)}) collective-permute-start(bf16[128,4096]{1,0:T(8,128)(2,1)S(1)} %copy-done.28), channel_id=1, source_target_pairs={{0,24},{1,25},{2,26},{3,27},{8,0},{9,1},{10,2},{11,3},{16,8},{17,9... | collective-permute-start | bytes 3145736 | tf_op jit(solution)/shard_map/ppermute | solution.py:38
  103.4 16.2 %collective-permute-start.19 = (bf16[128,4096]{1,0:T(8,128)(2,1)}, bf16[128,4096]{1,0:T(8,128)(2,1)S(1)}, u32[]{:S(2)}, u32[]{:S(2)}) collective-permute-start(bf16[128,4096]{1,0:T(8,128)(2,1)} %collective-permute-done.15.refs_2_), channel_id=1, source_target_pairs={{0,8},{1,9},{2,10},{3,11},{8,16},{9,17},{10,18},{11,19},{16,24},{1... | collective-permute-start | bytes 3145736 | tf_op jit(solution)/shard_map/ppermute | solution.py:38
  122.6 8.9 %collective-permute-start.24 = (f32[256,1536]{1,0:T(8,128)S(1)}, f32[256,1536]{1,0:T(8,128)S(1)}, u32[]{:S(2)}, u32[]{:S(2)}) collective-permute-start(f32[256,1536]{1,0:T(8,128)S(1)} %get-tuple-element.49), channel_id=1, source_target_pairs={{0,32},{1,33},{2,34},{3,35},{8,40},{9,41},{10,42},{11,43},{16,48},... | collective-permute-start | bytes 4718600 | tf_op jit(solution)/shard_map/ppermute | solution.py:38
  122.7 8.9 %collective-permute-start.23 = (f32[256,1536]{1,0:T(8,128)S(1)}, f32[256,1536]{1,0:T(8,128)S(1)}, u32[]{:S(2)}, u32[]{:S(2)}) collective-permute-start(f32[256,1536]{1,0:T(8,128)S(1)} %get-tuple-element.48), channel_id=1, source_target_pairs={{0,32},{1,33},{2,34},{3,35},{8,40},{9,41},{10,42},{11,43},{16,48},... | collective-permute-start | bytes 4718600 | tf_op jit(solution)/shard_map/ppermute | solution.py:38
  132.6 16.9 %collective-permute-start.27 = (s16[144,1536]{1,0:T(8,128)(2,1)}, s16[144,1536]{1,0:T(8,128)(2,1)}, u32[]{:S(2)}, u32[]{:S(2)}) collective-permute-start(s16[144,1536]{1,0:T(8,128)(2,1)} %shard_map.84), channel_id=1, source_target_pairs={{0,64},{1,65},{2,66},{3,67},{8,72},{9,73},{10,74},{11,75},{16,80},... | collective-permute-start | bytes 1327112 | tf_op jit(solution)/shard_map/ppermute | solution.py:38
  135.8 21.1 %collective-permute-start.26 = (s16[144,1536]{1,0:T(8,128)(2,1)}, s16[144,1536]{1,0:T(8,128)(2,1)}, u32[]{:S(2)}, u32[]{:S(2)}) collective-permute-start(s16[144,1536]{1,0:T(8,128)(2,1)} %shard_map.83), channel_id=1, source_target_pairs={{0,64},{1,65},{2,66},{3,67},{8,72},{9,73},{10,74},{11,75},{16,80},... | collective-permute-start | bytes 1327112 | tf_op jit(solution)/shard_map/ppermute | solution.py:38
  144.2 16.3 %collective-permute-start.25 = (f32[256,1536]{1,0:T(8,128)}, f32[256,1536]{1,0:T(8,128)S(1)}, u32[]{:S(2)}, u32[]{:S(2)}) collective-permute-start(f32[256,1536]{1,0:T(8,128)} %get-tuple-element.54), channel_id=1, source_target_pairs={{0,32},{1,33},{2,34},{3,35},{8,40},{9,41},{10,42},{11,43},{16,48},... | collective-permute-start | bytes 4718600 | tf_op jit(solution)/shard_map/ppermute | solution.py:38
  147.2 18.3 %collective-permute-start.22 = (s16[144,1536]{1,0:T(8,128)(2,1)S(1)}, s16[144,1536]{1,0:T(8,128)(2,1)S(1)}, u32[]{:S(2)}, u32[]{:S(2)}) collective-permute-start(s16[144,1536]{1,0:T(8,128)(2,1)S(1)} %shard_map.77), channel_id=1, source_target_pairs={{0,64},{1,65},{2,66},{3,67},{8,72},{9,73},{10,74},{11,75},{16,80},... | collective-permute-start | bytes 1327112 | tf_op jit(solution)/shard_map/ppermute | solution.py:38
  165.4 12.8 %collective-permute-start.28 = (s16[144,1536]{1,0:T(8,128)(2,1)S(1)}, s16[144,1536]{1,0:T(8,128)(2,1)S(1)}, u32[]{:S(2)}, u32[]{:S(2)}) collective-permute-start(s16[144,1536]{1,0:T(8,128)(2,1)S(1)} %shard_map.82), channel_id=1, source_target_pairs={{0,64},{1,65},{2,66},{3,67},{8,72},{9,73},{10,74},{11,75},{16,80},... | collective-permute-start | bytes 1327112 | tf_op jit(solution)/shard_map/ppermute | solution.py:38
  (27 other events, 159.5 us)

commit v3 on v2

--- a/solution.py
+++ b/solution.py
@@ -38,7 +38,6 @@
     return lax.ppermute(value, BOTH, pairs)
 
 
-VMEM = 40 * 2**20
 TILE = 512
 
 
@@ -81,7 +80,7 @@
         out_specs=pl.BlockSpec((rows, TILE), lambda i: (0, i)),
         out_shape=jax.ShapeDtypeStruct((rows, width), jnp.float32),
         scratch_shapes=[pltpu.VMEM((rows, depth), jnp.bfloat16), pltpu.SemaphoreType.DMA((len(pairs),))],
-        compiler_params=pltpu.CompilerParams(vmem_limit_bytes=VMEM),
+        compiler_params=pltpu.CompilerParams(vmem_limit_bytes=40 * 2**20),
         cost_estimate=pl.CostEstimate(
             flops=2 * rows * depth * width, bytes_accessed=2 * depth * (width + rows) + 4 * rows * width, transcendentals=0
         ),
@@ -112,7 +111,7 @@
         out_specs=[pl.BlockSpec(memory_space=pl.ANY)] * 2,
         out_shape=[half, half],
         scratch_shapes=[pltpu.SemaphoreType.DMA((4,))],
-        compiler_params=pltpu.CompilerParams(vmem_limit_bytes=VMEM),
+        compiler_params=pltpu.CompilerParams(vmem_limit_bytes=2 * 2**20),
         cost_estimate=pl.CostEstimate(flops=0, bytes_accessed=8 * 512 * width, transcendentals=0),
     )(order, *parts)
 
@@ -134,7 +133,7 @@
         in_specs=[first, first],
         out_specs=pl.BlockSpec((144, width), lambda i: (0, 0)),
         out_shape=jax.ShapeDtypeStruct((144, width), jnp.int16),
-        compiler_params=pltpu.CompilerParams(vmem_limit_bytes=VMEM),
+        compiler_params=pltpu.CompilerParams(vmem_limit_bytes=8 * 2**20),
         cost_estimate=pl.CostEstimate(flops=4 * 128 * width, bytes_accessed=10 * 128 * width, transcendentals=width),
     )(kept, got)
 
@@ -159,13 +158,7 @@
         return jnp.where(core == 0, zero, one)
 
     wanted = jnp.stack([2 * (1 - half) + 1 - core, 2 * half + 1 - core, 2 * (1 - half) + core, 2 * half + core])
-    steps = (wanted - z) % 4
-
-    def order(zero, one):
-        return by_core(jnp.array(zero, jnp.int32), jnp.array(one, jnp.int32))[steps]
-
-    same = order([0, 1, 2, 3], [0, 1, 2, 3])
-    crossed = order([0, 1, 2, 3], [0, 3, 2, 1])
+    order = (wanted - z) % 4
 
     pair = send(own, PAIR)
     below, above = send(own, FIRST_UP), send(own, FIRST_DOWN)
@@ -185,30 +178,38 @@
     far_pair, up_2, down_2, up_3, down_3, part_a = join(far_pair, up_2, down_2, up_3, down_3, part_a)
 
     x2 = jnp.concatenate([far, far_pair], 0)
-    up_4, down_5 = send(x2, SECOND_UP), send(by_core(down_3, x2), SECOND_DOWN)
-    up_5, down_4 = send(x3, SECOND_UP), send(down_2, SECOND_DOWN)
-    part_b = products(core, [(up_3, x2), (down_2, down_2), (up_2, down_3), (down_3, up_2), (x2, up_3)], train)
-    up_4, down_5, up_5, down_4, part_b = join(up_4, down_5, up_5, down_4, part_b)
-
-    away_0, keep_0 = pick(same, [part_a, part_b], [(0, 0), (0, 1), (1, 0), (0, 2)])
-    up_6, down_6 = send(up_4, SECOND_UP), send(by_core(x2, down_3), SECOND_DOWN)
+    up_5, down_4 = send(x3, SECOND_UP), send(by_core(down_2, x2), SECOND_DOWN)
+    part_b = products(core, [(up_3, x2), (down_2, down_2), (up_2, down_3), (down_3, up_2)], train)
+    up_5, down_4, part_b = join(up_5, down_4, part_b)
+
+    away_0, keep_0 = pick(order, [part_a, part_b], [(0, 0), (0, 1), (1, 0), (0, 2)])
+    up_4, down_5 = send(x2, SECOND_UP), send(down_3, SECOND_DOWN)
     got_0 = send(away_0, CORE)
-    part_c = products(core, [(down_4, down_5), (down_5, up_4), (up_5, up_5), (up_4, down_4)], train)
-    up_6, down_6, got_0, part_c = join(up_6, down_6, got_0, part_c)
+    part_c = products(core, [(down_4, down_4), (up_5, up_5), (x2, up_3)], train)
+    up_4, down_5, got_0, part_c = join(up_4, down_5, got_0, part_c)
 
     message_0 = narrow(keep_0, got_0)
-    away_1, keep_1 = pick(same, [part_a, part_b, part_c], [(0, 3), (1, 1), (2, 0), (1, 2)])
-    away_3, keep_3 = pick(same, [part_a, part_b, part_c], [(0, 4), (1, 3), (2, 1), (2, 2)])
-    far_0, got_1, got_3 = send(message_0, ACROSS), send(away_1, CORE), send(away_3, CORE)
-    part_d = products(core, [(down_6, down_6), (up_6, up_6)], train)
-    got_1, got_3, part_d = join(got_1, got_3, part_d)
-
-    message_1, message_3 = narrow(keep_1, got_1), narrow(keep_3, got_3)
-    far_1, far_3 = send(message_1, ACROSS), send(message_3, ACROSS)
-    away_2, keep_2 = pick(crossed, [part_b, part_c, part_d], [(0, 4), (2, 0), (2, 1), (1, 3)])
+    message_0, order = join(message_0, order)
+    away_1, keep_1 = pick(order, [part_a, part_b, part_c], [(0, 3), (1, 1), (2, 0), (1, 2)])
+    up_6, down_6 = send(up_4, SECOND_UP), send(by_core(x2, down_2), SECOND_DOWN)
+    got_1, far_0 = send(away_1, CORE), send(message_0, ACROSS)
+    part_d = products(core, [(down_5, up_4), (up_4, down_5)], train)
+    up_6, down_6, got_1, far_0, part_d = join(up_6, down_6, got_1, far_0, part_d)
+
+    message_1, order = join(narrow(keep_1, got_1), order)
+    away_3, keep_3 = pick(order, [part_a, part_b, part_c, part_d], [(0, 4), (1, 3), (3, 0), (2, 1)])
+    got_3 = send(away_3, CORE)
+    message_1, got_3 = join(message_1, got_3)
+    far_1 = send(message_1, ACROSS)
+    message_3 = narrow(keep_3, got_3)
+    down_6, up_6, message_3 = join(down_6, up_6, message_3)
+    far_3 = send(message_3, ACROSS)
+    part_e = products(core, [(down_6, down_6), (up_6, up_6)], train)
+    far_1, part_e = join(far_1, part_e)
+    away_2, keep_2 = pick(order, [part_c, part_d, part_e], [(0, 2), (2, 0), (2, 1), (1, 1)])
     got_2 = send(away_2, CORE)
     message_2 = narrow(keep_2, got_2)
-    far_0, message_2 = join(far_0, message_2)
+    keep_3, message_2 = join(keep_3, message_2)
     far_2 = send(message_2, ACROSS)
 
     out = jnp.zeros((2, 4, 64, train.shape[0]), jnp.float32)

time: 181 us -> 175 us (0.967)
  local copies, waits for them, and re-layouts: 16.2 us -> 8.28 us
  Pallas kernels: 50.7 us -> 55.5 us
  waiting for transfers between devices: 62.2 us -> 59.9 us
    unnamed x64 -> x50, local copies, waits for them, and re-layouts: 14.1 us -> 6.71 us
    pallas_call x4 -> x5, Pallas kernels: 44 us -> 49 us  [products(): pl.pallas_call(functools.partial(product_kernel, choices, len(blocks)), g...]
    ppermute x29, waiting for transfers between devices: 62.2 us -> 59.9 us  [send(): return lax.ppermute(value, BOTH, pairs)]
  transfers between devices with their start and end apart: 29 -> 29, of which waited for: 14 -> 15; matrix products, arithmetic and copies ran while one was open for 6% -> 5% of each run, Pallas kernels for 26% -> 29%
where the time goes in v3:
time: 175 us
  waiting for transfers between devices  59.9 us (34%)
  Pallas kernels  55.5 us (32%)
  starting transfers between devices  41.5 us (24%)
  other arithmetic  8.97 us (5%)
  local copies, waits for them, and re-layouts  8.28 us (5%)
    ppermute x29, waiting for transfers between devices, send(): return lax.ppermute(value, BOTH, pairs)  59.9 us
    pallas_call x5, Pallas kernels, products(): pl.pallas_call(functools.partial(product_kernel, choices, len(blocks)), g...  49 us
    ppermute x29, starting transfers between devices, send(): return lax.ppermute(value, BOTH, pairs)  41.5 us
    unnamed x50, local copies, waits for them, and re-layouts  6.71 us
    pallas_call x4, Pallas kernels, pick(): pl.pallas_call(functools.partial(pick_kernel, spots, len(parts)), in_spec...  4.72 us
  transfers between devices with their start and end apart: 29, of which 15 were waited for; matrix products, arithmetic and copies ran while one was open for 5% of the time, Pallas kernels for 29%

profile of v3, /device:TPU:2, one launch (start us, length us, event | category | flops | bytes accessed | tf_op | source)
XLA Modules:
  0.0 174.8 jit_solution(11083080489878346851)
XLA Ops:
  2.4 3.1 %collective-permute-start.3 = (bf16[64,4096]{1,0:T(8,128)(2,1)S(1)}, bf16[64,4096]{1,0:T(8,128)(2,1)S(1)}, u32[]{:S(2)}, u32[]{:S(2)}) collective-permute-start(bf16[64,4096]{1,0:T(8,128)(2,1)S(1)} %fusion), channel_id=1, source_target_pairs={{0,3},{1,0},{2,1},{3,2},{8,11},{9,8},{10,9},{11,10},{16,19},{17,16... | collective-permute-start | bytes 1572872 | tf_op jit(solution)/shard_map/ppermute | solution.py:38
  5.5 1.9 %collective-permute-start.6 = (bf16[64,4096]{1,0:T(8,128)(2,1)S(1)}, bf16[64,4096]{1,0:T(8,128)(2,1)S(1)}, u32[]{:S(2)}, u32[]{:S(2)}) collective-permute-start(bf16[64,4096]{1,0:T(8,128)(2,1)S(1)} %fusion), channel_id=1, source_target_pairs={{0,8},{1,9},{2,10},{3,11},{8,16},{9,17},{10,18},{11,19},{16,24},{1... | collective-permute-start | bytes 1572872 | tf_op jit(solution)/shard_map/ppermute | solution.py:38
  7.4 2.1 %collective-permute-start.12 = (bf16[64,4096]{1,0:T(8,128)(2,1)S(1)}, bf16[64,4096]{1,0:T(8,128)(2,1)}, u32[]{:S(2)}, u32[]{:S(2)}) collective-permute-start(bf16[64,4096]{1,0:T(8,128)(2,1)S(1)} %fusion), channel_id=1, source_target_pairs={{0,24},{1,25},{2,26},{3,27},{8,0},{9,1},{10,2},{11,3},{16,8},{17,9... | collective-permute-start | bytes 1572872 | tf_op jit(solution)/shard_map/ppermute | solution.py:38
  9.5 6.1 %collective-permute-done = bf16[64,4096]{1,0:T(8,128)(2,1)S(1)} collective-permute-done((bf16[64,4096]{1,0:T(8,128)(2,1)S(1)}, bf16[64,4096]{1,0:T(8,128)(2,1)S(1)}, u32[]{:S(2)}, u32[]{:S(2)}) %collective-permute-start) | collective-permute-done | bytes 524320 | tf_op jit(solution)/shard_map/ppermute | solution.py:38
  15.6 3.0 %collective-permute-start.1 = (bf16[64,4096]{1,0:T(8,128)(2,1)S(1)}, bf16[64,4096]{1,0:T(8,128)(2,1)S(1)}, u32[]{:S(2)}, u32[]{:S(2)}) collective-permute-start(bf16[64,4096]{1,0:T(8,128)(2,1)S(1)} %collective-permute-done), channel_id=1, source_target_pairs={{0,3},{1,0},{2,1},{3,2},{8,11},{9,8},{10,9},{11,10},{16,19},{17,16... | collective-permute-start | bytes 1572872 | tf_op jit(solution)/shard_map/ppermute | solution.py:38
  18.8 2.1 %collective-permute-done.9 = bf16[64,4096]{1,0:T(8,128)(2,1)S(1)} collective-permute-done((bf16[64,4096]{1,0:T(8,128)(2,1)S(1)}, bf16[64,4096]{1,0:T(8,128)(2,1)S(1)}, u32[]{:S(2)}, u32[]{:S(2)}) %collective-permute-start.9) | collective-permute-done | bytes 524320 | tf_op jit(solution)/shard_map/ppermute | solution.py:38
  21.7 3.2 %collective-permute-start.13 = (bf16[64,4096]{1,0:T(8,128)(2,1)S(1)}, bf16[64,4096]{1,0:T(8,128)(2,1)S(1)}, u32[]{:S(2)}, u32[]{:S(2)}) collective-permute-start(bf16[64,4096]{1,0:T(8,128)(2,1)S(1)} %collective-permute-done), channel_id=1, source_target_pairs={{0,24},{1,25},{2,26},{3,27},{8,0},{9,1},{10,2},{11,3},{16,8},{17,9... | collective-permute-start | bytes 1572872 | tf_op jit(solution)/shard_map/ppermute | solution.py:38
  25.0 2.3 %collective-permute-done.1 = bf16[64,4096]{1,0:T(8,128)(2,1)S(1)} collective-permute-done((bf16[64,4096]{1,0:T(8,128)(2,1)S(1)}, bf16[64,4096]{1,0:T(8,128)(2,1)S(1)}, u32[]{:S(2)}, u32[]{:S(2)}) %collective-permute-start.1) | collective-permute-done | bytes 524320 | tf_op jit(solution)/shard_map/ppermute | solution.py:38
  27.3 7.1 %collective-permute-done.10 = bf16[64,4096]{1,0:T(8,128)(2,1)S(1)} collective-permute-done((bf16[64,4096]{1,0:T(8,128)(2,1)S(1)}, bf16[64,4096]{1,0:T(8,128)(2,1)S(1)}, u32[]{:S(2)}, u32[]{:S(2)}) %collective-permute-start.10) | collective-permute-done | bytes 524320 | tf_op jit(solution)/shard_map/ppermute | solution.py:38
  37.0 2.6 %collective-permute-start.5 = (bf16[128,4096]{1,0:T(8,128)(2,1)S(1)}, bf16[128,4096]{1,0:T(8,128)(2,1)S(1)}, u32[]{:S(2)}, u32[]{:S(2)}) collective-permute-start(bf16[128,4096]{1,0:T(8,128)(2,1)S(1)} %constant_dynamic-update-slice_fusion.refs_2_), channel_id=1, source_target_pairs={{0,24},{1,25},{2,26},{3,27},{8,0},{9,1},{10,2},{11,3},{16,8},{17,9... | collective-permute-start | bytes 3145736 | tf_op jit(solution)/shard_map/ppermute | solution.py:38
  39.6 2.1 %collective-permute-start.11 = (bf16[128,4096]{1,0:T(8,128)(2,1)}, bf16[128,4096]{1,0:T(8,128)(2,1)}, u32[]{:S(2)}, u32[]{:S(2)}) collective-permute-start(bf16[128,4096]{1,0:T(8,128)(2,1)} %constant_dynamic-update-slice_fusion.4.refs_4_), channel_id=1, source_target_pairs={{0,24},{1,25},{2,26},{3,27},{8,0},{9,1},{10,2},{11,3},{16,8},{17,9... | collective-permute-start | bytes 3145736 | tf_op jit(solution)/shard_map/ppermute | solution.py:38
  42.8 2.0 %collective-permute-done.15 = bf16[64,4096]{1,0:T(8,128)(2,1)S(1)} collective-permute-done((bf16[64,4096]{1,0:T(8,128)(2,1)S(1)}, bf16[64,4096]{1,0:T(8,128)(2,1)S(1)}, u32[]{:S(2)}, u32[]{:S(2)}) %collective-permute-start.15) | collective-permute-done | bytes 524320 | tf_op jit(solution)/shard_map/ppermute | solution.py:38
  44.8 13.0 %shard_map.37.refs_0_ = f32[640,1536]{1,0:T(8,128)S(1)} custom-call(s32[1]{0:T(128)} %bitcast.6.core, bf16[128,4096]{1,0:T(8,128)(2,1)S(1)} %pad_maximum_fusion.refs_0_, bf16[128,4096]{1,0:T(8,128)(2,1)S(1)} %pad_maximum_fusion.1.refs_1_, bf16[128,4096]{1,0:T(8,128)(2,1)S(1)} %constant_dynamic-update-slice_fusion.refs_2_, ...), custom_call_target="tpu_custom_call" | custom-call | flops 8053063680 | bytes 21757952 | tf_op jit(solution)/shard_map/pallas_call | solution.py:74
  57.8 1.8 %collective-permute-done.2 = bf16[64,4096]{1,0:T(8,128)(2,1)S(1)} collective-permute-done((bf16[64,4096]{1,0:T(8,128)(2,1)S(1)}, bf16[64,4096]{1,0:T(8,128)(2,1)S(1)}, u32[]{:S(2)}, u32[]{:S(2)}) %collective-permute-start.2) | collective-permute-done | bytes 524320 | tf_op jit(solution)/shard_map/ppermute | solution.py:38
  59.7 4.0 %collective-permute-start.14 = (bf16[128,4096]{1,0:T(8,128)(2,1)}, bf16[128,4096]{1,0:T(8,128)(2,1)}, u32[]{:S(2)}, u32[]{:S(2)}) collective-permute-start(bf16[128,4096]{1,0:T(8,128)(2,1)} %constant_dynamic-update-slice_fusion.4.refs_4_), channel_id=1, source_target_pairs={{0,8},{1,9},{2,10},{3,11},{8,16},{9,17},{10,18},{11,19},{16,24},{1... | collective-permute-start | bytes 3145736 | tf_op jit(solution)/shard_map/ppermute | solution.py:38
  63.7 5.1 %collective-permute-done.11.refs_4_ = bf16[128,4096]{1,0:T(8,128)(2,1)} collective-permute-done((bf16[128,4096]{1,0:T(8,128)(2,1)}, bf16[128,4096]{1,0:T(8,128)(2,1)}, u32[]{:S(2)}, u32[]{:S(2)}) %collective-permute-start.11) | collective-permute-done | bytes 1048608 | tf_op jit(solution)/shard_map/ppermute | solution.py:38
  70.5 3.7 %collective-permute-start.16 = (bf16[128,4096]{1,0:T(8,128)(2,1)}, bf16[128,4096]{1,0:T(8,128)(2,1)}, u32[]{:S(2)}, u32[]{:S(2)}) collective-permute-start(bf16[128,4096]{1,0:T(8,128)(2,1)} %get-tuple-element.84), channel_id=1, source_target_pairs={{0,24},{1,25},{2,26},{3,27},{8,0},{9,1},{10,2},{11,3},{16,8},{17,9... | collective-permute-start | bytes 3145736 | tf_op jit(solution)/shard_map/ppermute | solution.py:38
  75.5 11.4 %shard_map.38.refs_1_ = f32[512,1536]{1,0:T(8,128)S(1)} custom-call(s32[1]{0:T(128)} %bitcast.6.core, bf16[128,4096]{1,0:T(8,128)(2,1)S(1)} %collective-permute-done.8.refs_0_.refs_3_, bf16[128,4096]{1,0:T(8,128)(2,1)S(1)} %constant_dynamic-update-slice_fusion.6.refs_1_.refs_2_, bf16[128,4096]{1,0:T(8,128)(2,1)S(1)} %collective-permute-done.5.refs_2_, ...), custom_call_target="tpu_custom_call" | custom-call | flops 6442450944 | bytes 19922944 | tf_op jit(solution)/shard_map/pallas_call | solution.py:74
  88.2 3.6 %collective-permute-start.18 = (bf16[128,4096]{1,0:T(8,128)(2,1)}, bf16[128,4096]{1,0:T(8,128)(2,1)S(1)}, u32[]{:S(2)}, u32[]{:S(2)}) collective-permute-start(bf16[128,4096]{1,0:T(8,128)(2,1)} %collective-permute-done.11.refs_4_), channel_id=1, source_target_pairs={{0,24},{1,25},{2,26},{3,27},{8,0},{9,1},{10,2},{11,3},{16,8},{17,9... | collective-permute-start | bytes 3145736 | tf_op jit(solution)/shard_map/ppermute | solution.py:38
  91.9 10.1 %shard_map.40.refs_2_.refs_0_ = f32[384,1536]{1,0:T(8,128)S(1)} custom-call(s32[1]{0:T(128)} %bitcast.6.core, bf16[128,4096]{1,0:T(8,128)(2,1)} %collective-permute-done.16.refs_0_, bf16[128,4096]{1,0:T(8,128)(2,1)} %collective-permute-done.14.refs_1_, bf16[128,4096]{1,0:T(8,128)(2,1)S(1)} %constant_dynamic-update-slice_fusion.6.refs_1_.refs_2_, ...), custom_call_target="tpu_custom_call" | custom-call | flops 4831838208 | bytes 18087936 | tf_op jit(solution)/shard_map/pallas_call | solution.py:74
  102.0 2.5 %collective-permute-done.17.refs_1_ = bf16[128,4096]{1,0:T(8,128)(2,1)S(1)} collective-permute-done((bf16[128,4096]{1,0:T(8,128)(2,1)S(1)}, bf16[128,4096]{1,0:T(8,128)(2,1)S(1)}, u32[]{:S(2)}, u32[]{:S(2)}) %collective-permute-start.17) | collective-permute-done | bytes 1048608 | tf_op jit(solution)/shard_map/ppermute | solution.py:38
  106.4 3.5 %collective-permute-start.21 = (bf16[128,4096]{1,0:T(8,128)(2,1)S(1)}, bf16[128,4096]{1,0:T(8,128)(2,1)S(1)}, u32[]{:S(2)}, u32[]{:S(2)}) collective-permute-start(bf16[128,4096]{1,0:T(8,128)(2,1)S(1)} %copy-done.21), channel_id=1, source_target_pairs={{0,24},{1,25},{2,26},{3,27},{8,0},{9,1},{10,2},{11,3},{16,8},{17,9... | collective-permute-start | bytes 3145736 | tf_op jit(solution)/shard_map/ppermute | solution.py:38
  109.9 2.0 %collective-permute-start.23 = (s16[144,1536]{1,0:T(8,128)(2,1)S(1)}, s16[144,1536]{1,0:T(8,128)(2,1)S(1)}, u32[]{:S(2)}, u32[]{:S(2)}) collective-permute-start(s16[144,1536]{1,0:T(8,128)(2,1)S(1)} %shard_map.41), channel_id=1, source_target_pairs={{0,64},{1,65},{2,66},{3,67},{8,72},{9,73},{10,74},{11,75},{16,80},... | collective-permute-start | bytes 1327112 | tf_op jit(solution)/shard_map/ppermute | solution.py:38
  111.9 7.2 %shard_map.43.refs_3_.refs_1_ = f32[256,1536]{1,0:T(8,128)S(1)} custom-call(s32[1]{0:T(128)} %bitcast.6.core, bf16[128,4096]{1,0:T(8,128)(2,1)S(1)} %collective-permute-done.18.refs_0_, bf16[128,4096]{1,0:T(8,128)(2,1)S(1)} %collective-permute-done.17.refs_1_, bf16[1536,4096]{1,0:T(8,128)(2,1)} %bitcast.47), custom_call_target="tpu_custom_call" | custom-call | flops 3221225472 | bytes 16252928 | tf_op jit(solution)/shard_map/pallas_call | solution.py:74
  119.1 3.1 %collective-permute-done.21.refs_0_ = bf16[128,4096]{1,0:T(8,128)(2,1)S(1)} collective-permute-done((bf16[128,4096]{1,0:T(8,128)(2,1)S(1)}, bf16[128,4096]{1,0:T(8,128)(2,1)S(1)}, u32[]{:S(2)}, u32[]{:S(2)}) %collective-permute-start.21) | collective-permute-done | bytes 1048608 | tf_op jit(solution)/shard_map/ppermute | solution.py:38
  122.2 3.7 %collective-permute-done.20.refs_1_ = bf16[128,4096]{1,0:T(8,128)(2,1)S(1)} collective-permute-done((bf16[128,4096]{1,0:T(8,128)(2,1)S(1)}, bf16[128,4096]{1,0:T(8,128)(2,1)S(1)}, u32[]{:S(2)}, u32[]{:S(2)}) %collective-permute-start.20) | collective-permute-done | bytes 1048608 | tf_op jit(solution)/shard_map/ppermute | solution.py:38
  135.2 2.1 %collective-permute-start.25 = (s16[144,1536]{1,0:T(8,128)(2,1)S(1)}, s16[144,1536]{1,0:T(8,128)(2,1)S(1)}, u32[]{:S(2)}, u32[]{:S(2)}) collective-permute-start(s16[144,1536]{1,0:T(8,128)(2,1)S(1)} %copy-done.17), channel_id=1, source_target_pairs={{0,64},{1,65},{2,66},{3,67},{8,72},{9,73},{10,74},{11,75},{16,80},... | collective-permute-start | bytes 1327112 | tf_op jit(solution)/shard_map/ppermute | solution.py:38
  138.9 7.3 %shard_map.47.refs_2_ = f32[256,1536]{1,0:T(8,128)S(1)} custom-call(s32[1]{0:T(128)} %bitcast.6.core, bf16[128,4096]{1,0:T(8,128)(2,1)S(1)} %collective-permute-done.21.refs_0_, bf16[128,4096]{1,0:T(8,128)(2,1)S(1)} %copy-done.13, bf16[1536,4096]{1,0:T(8,128)(2,1)} %bitcast.48), custom_call_target="tpu_custom_call" | custom-call | flops 3221225472 | bytes 16252928 | tf_op jit(solution)/shard_map/pallas_call | solution.py:74
  146.3 3.5 %collective-permute-done.25 = s16[144,1536]{1,0:T(8,128)(2,1)S(1)} collective-permute-done((s16[144,1536]{1,0:T(8,128)(2,1)S(1)}, s16[144,1536]{1,0:T(8,128)(2,1)S(1)}, u32[]{:S(2)}, u32[]{:S(2)}) %collective-permute-start.25) | collective-permute-done | bytes 442400 | tf_op jit(solution)/shard_map/ppermute | solution.py:38
  150.9 8.0 %collective-permute-done.27 = s16[144,1536]{1,0:T(8,128)(2,1)S(1)} collective-permute-done((s16[144,1536]{1,0:T(8,128)(2,1)S(1)}, s16[144,1536]{1,0:T(8,128)(2,1)S(1)}, u32[]{:S(2)}, u32[]{:S(2)}) %collective-permute-start.27) | collective-permute-done | bytes 442400 | tf_op jit(solution)/shard_map/ppermute | solution.py:38
  159.4 2.1 %collective-permute-start.28 = (s16[144,1536]{1,0:T(8,128)(2,1)S(1)}, s16[144,1536]{1,0:T(8,128)(2,1)S(1)}, u32[]{:S(2)}, u32[]{:S(2)}) collective-permute-start(s16[144,1536]{1,0:T(8,128)(2,1)S(1)} %shard_map.49), channel_id=1, source_target_pairs={{0,64},{1,65},{2,66},{3,67},{8,72},{9,73},{10,74},{11,75},{16,80},... | collective-permute-start | bytes 1327112 | tf_op jit(solution)/shard_map/ppermute | solution.py:38
  162.9 9.9 %collective-permute-done.28 = s16[144,1536]{1,0:T(8,128)(2,1)S(1)} collective-permute-done((s16[144,1536]{1,0:T(8,128)(2,1)S(1)}, s16[144,1536]{1,0:T(8,128)(2,1)S(1)}, u32[]{:S(2)}, u32[]{:S(2)}) %collective-permute-start.28) | collective-permute-done | bytes 442400 | tf_op jit(solution)/shard_map/ppermute | solution.py:38
  (116 shorter events, 28.9 us)
Async XLA Ops:
  1.9 13.7 %collective-permute-start = (bf16[64,4096]{1,0:T(8,128)(2,1)S(1)}, bf16[64,4096]{1,0:T(8,128)(2,1)S(1)}, u32[]{:S(2)}, u32[]{:S(2)}) collective-permute-start(bf16[64,4096]{1,0:T(8,128)(2,1)S(1)} %fusion), channel_id=1, source_target_pairs={{0,4},{1,5},{2,6},{3,7},{8,12},{9,13},{10,14},{11,15},{16,20},{17,... | collective-permute-start | bytes 1572872 | tf_op jit(solution)/shard_map/ppermute | solution.py:38
  2.4 16.3 %collective-permute-start.3 = (bf16[64,4096]{1,0:T(8,128)(2,1)S(1)}, bf16[64,4096]{1,0:T(8,128)(2,1)S(1)}, u32[]{:S(2)}, u32[]{:S(2)}) collective-permute-start(bf16[64,4096]{1,0:T(8,128)(2,1)S(1)} %fusion), channel_id=1, source_target_pairs={{0,3},{1,0},{2,1},{3,2},{8,11},{9,8},{10,9},{11,10},{16,19},{17,16... | collective-permute-start | bytes 1572872 | tf_op jit(solution)/shard_map/ppermute | solution.py:38
  5.5 15.4 %collective-permute-start.9 = (bf16[64,4096]{1,0:T(8,128)(2,1)S(1)}, bf16[64,4096]{1,0:T(8,128)(2,1)S(1)}, u32[]{:S(2)}, u32[]{:S(2)}) collective-permute-start(bf16[64,4096]{1,0:T(8,128)(2,1)S(1)} %fusion), channel_id=1, source_target_pairs={{0,1},{1,2},{2,3},{3,0},{8,9},{9,10},{10,11},{11,8},{16,17},{17,18... | collective-permute-start | bytes 1572872 | tf_op jit(solution)/shard_map/ppermute | solution.py:38
  5.5 16.2 %collective-permute-start.6 = (bf16[64,4096]{1,0:T(8,128)(2,1)S(1)}, bf16[64,4096]{1,0:T(8,128)(2,1)S(1)}, u32[]{:S(2)}, u32[]{:S(2)}) collective-permute-start(bf16[64,4096]{1,0:T(8,128)(2,1)S(1)} %fusion), channel_id=1, source_target_pairs={{0,8},{1,9},{2,10},{3,11},{8,16},{9,17},{10,18},{11,19},{16,24},{1... | collective-permute-start | bytes 1572872 | tf_op jit(solution)/shard_map/ppermute | solution.py:38
  7.4 32.1 %collective-permute-start.12 = (bf16[64,4096]{1,0:T(8,128)(2,1)S(1)}, bf16[64,4096]{1,0:T(8,128)(2,1)}, u32[]{:S(2)}, u32[]{:S(2)}) collective-permute-start(bf16[64,4096]{1,0:T(8,128)(2,1)S(1)} %fusion), channel_id=1, source_target_pairs={{0,24},{1,25},{2,26},{3,27},{8,0},{9,1},{10,2},{11,3},{16,8},{17,9... | collective-permute-start | bytes 1572872 | tf_op jit(solution)/shard_map/ppermute | solution.py:38
  15.6 11.7 %collective-permute-start.1 = (bf16[64,4096]{1,0:T(8,128)(2,1)S(1)}, bf16[64,4096]{1,0:T(8,128)(2,1)S(1)}, u32[]{:S(2)}, u32[]{:S(2)}) collective-permute-start(bf16[64,4096]{1,0:T(8,128)(2,1)S(1)} %collective-permute-done), channel_id=1, source_target_pairs={{0,3},{1,0},{2,1},{3,2},{8,11},{9,8},{10,9},{11,10},{16,19},{17,16... | collective-permute-start | bytes 1572872 | tf_op jit(solution)/shard_map/ppermute | solution.py:38
  18.7 15.7 %collective-permute-start.10 = (bf16[64,4096]{1,0:T(8,128)(2,1)S(1)}, bf16[64,4096]{1,0:T(8,128)(2,1)S(1)}, u32[]{:S(2)}, u32[]{:S(2)}) collective-permute-start(bf16[64,4096]{1,0:T(8,128)(2,1)S(1)} %collective-permute-done), channel_id=1, source_target_pairs={{0,1},{1,2},{2,3},{3,0},{8,9},{9,10},{10,11},{11,8},{16,17},{17,18... | collective-permute-start | bytes 1572872 | tf_op jit(solution)/shard_map/ppermute | solution.py:38
  20.9 16.1 %collective-permute-start.7 = (bf16[64,4096]{1,0:T(8,128)(2,1)S(1)}, bf16[64,4096]{1,0:T(8,128)(2,1)S(1)}, u32[]{:S(2)}, u32[]{:S(2)}) collective-permute-start(bf16[64,4096]{1,0:T(8,128)(2,1)S(1)} %collective-permute-done), channel_id=1, source_target_pairs={{0,8},{1,9},{2,10},{3,11},{8,16},{9,17},{10,18},{11,19},{16,24},{1... | collective-permute-start | bytes 1572872 | tf_op jit(solution)/shard_map/ppermute | solution.py:38
  21.7 19.9 %collective-permute-start.13 = (bf16[64,4096]{1,0:T(8,128)(2,1)S(1)}, bf16[64,4096]{1,0:T(8,128)(2,1)S(1)}, u32[]{:S(2)}, u32[]{:S(2)}) collective-permute-start(bf16[64,4096]{1,0:T(8,128)(2,1)S(1)} %collective-permute-done), channel_id=1, source_target_pairs={{0,24},{1,25},{2,26},{3,27},{8,0},{9,1},{10,2},{11,3},{16,8},{17,9... | collective-permute-start | bytes 1572872 | tf_op jit(solution)/shard_map/ppermute | solution.py:38
  27.3 17.5 %collective-permute-start.15 = (bf16[64,4096]{1,0:T(8,128)(2,1)S(1)}, bf16[64,4096]{1,0:T(8,128)(2,1)S(1)}, u32[]{:S(2)}, u32[]{:S(2)}) collective-permute-start(bf16[64,4096]{1,0:T(8,128)(2,1)S(1)} %collective-permute-done.9), channel_id=1, source_target_pairs={{0,1},{1,2},{2,3},{3,0},{8,9},{9,10},{10,11},{11,8},{16,17},{17,18... | collective-permute-start | bytes 1572872 | tf_op jit(solution)/shard_map/ppermute | solution.py:38
  34.4 34.4 %collective-permute-start.4 = (bf16[128,4096]{1,0:T(8,128)(2,1)S(1)}, bf16[128,4096]{1,0:T(8,128)(2,1)S(1)}, u32[]{:S(2)}, u32[]{:S(2)}) collective-permute-start(bf16[128,4096]{1,0:T(8,128)(2,1)S(1)} %constant_dynamic-update-slice_fusion.refs_2_), channel_id=1, source_target_pairs={{0,8},{1,9},{2,10},{3,11},{8,16},{9,17},{10,18},{11,19},{16,24},{1... | collective-permute-start | bytes 3145736 | tf_op jit(solution)/shard_map/ppermute | solution.py:38
  37.0 31.8 %collective-permute-start.5 = (bf16[128,4096]{1,0:T(8,128)(2,1)S(1)}, bf16[128,4096]{1,0:T(8,128)(2,1)S(1)}, u32[]{:S(2)}, u32[]{:S(2)}) collective-permute-start(bf16[128,4096]{1,0:T(8,128)(2,1)S(1)} %constant_dynamic-update-slice_fusion.refs_2_), channel_id=1, source_target_pairs={{0,24},{1,25},{2,26},{3,27},{8,0},{9,1},{10,2},{11,3},{16,8},{17,9... | collective-permute-start | bytes 3145736 | tf_op jit(solution)/shard_map/ppermute | solution.py:38
  39.6 29.2 %collective-permute-start.11 = (bf16[128,4096]{1,0:T(8,128)(2,1)}, bf16[128,4096]{1,0:T(8,128)(2,1)}, u32[]{:S(2)}, u32[]{:S(2)}) collective-permute-start(bf16[128,4096]{1,0:T(8,128)(2,1)} %constant_dynamic-update-slice_fusion.4.refs_4_), channel_id=1, source_target_pairs={{0,24},{1,25},{2,26},{3,27},{8,0},{9,1},{10,2},{11,3},{16,8},{17,9... | collective-permute-start | bytes 3145736 | tf_op jit(solution)/shard_map/ppermute | solution.py:38
  41.7 27.1 %collective-permute-start.8 = (bf16[128,4096]{1,0:T(8,128)(2,1)S(1)}, bf16[128,4096]{1,0:T(8,128)(2,1)S(1)}, u32[]{:S(2)}, u32[]{:S(2)}) collective-permute-start(bf16[128,4096]{1,0:T(8,128)(2,1)S(1)} %constant_dynamic-update-slice_fusion.2.refs_3_), channel_id=1, source_target_pairs={{0,8},{1,9},{2,10},{3,11},{8,16},{9,17},{10,18},{11,19},{16,24},{1... | collective-permute-start | bytes 3145736 | tf_op jit(solution)/shard_map/ppermute | solution.py:38
  44.8 14.9 %collective-permute-start.2 = (bf16[64,4096]{1,0:T(8,128)(2,1)S(1)}, bf16[64,4096]{1,0:T(8,128)(2,1)S(1)}, u32[]{:S(2)}, u32[]{:S(2)}) collective-permute-start(bf16[64,4096]{1,0:T(8,128)(2,1)S(1)} %collective-permute-done.1), channel_id=1, source_target_pairs={{0,3},{1,0},{2,1},{3,2},{8,11},{9,8},{10,9},{11,10},{16,19},{17,16... | collective-permute-start | bytes 1572872 | tf_op jit(solution)/shard_map/ppermute | solution.py:38
  57.8 12.7 %copy-start = (f32[640,1536]{1,0:T(8,128)}, f32[640,1536]{1,0:T(8,128)S(1)}, u32[]{:S(2)}) copy-start(f32[640,1536]{1,0:T(8,128)S(1)} %shard_map.37.refs_0_) | copy-start | bytes 11796484
  59.7 27.2 %collective-permute-start.14 = (bf16[128,4096]{1,0:T(8,128)(2,1)}, bf16[128,4096]{1,0:T(8,128)(2,1)}, u32[]{:S(2)}, u32[]{:S(2)}) collective-permute-start(bf16[128,4096]{1,0:T(8,128)(2,1)} %constant_dynamic-update-slice_fusion.4.refs_4_), channel_id=1, source_target_pairs={{0,8},{1,9},{2,10},{3,11},{8,16},{9,17},{10,18},{11,19},{16,24},{1... | collective-permute-start | bytes 3145736 | tf_op jit(solution)/shard_map/ppermute | solution.py:38
  70.5 16.4 %collective-permute-start.16 = (bf16[128,4096]{1,0:T(8,128)(2,1)}, bf16[128,4096]{1,0:T(8,128)(2,1)}, u32[]{:S(2)}, u32[]{:S(2)}) collective-permute-start(bf16[128,4096]{1,0:T(8,128)(2,1)} %get-tuple-element.84), channel_id=1, source_target_pairs={{0,24},{1,25},{2,26},{3,27},{8,0},{9,1},{10,2},{11,3},{16,8},{17,9... | collective-permute-start | bytes 3145736 | tf_op jit(solution)/shard_map/ppermute | solution.py:38
  88.0 16.5 %copy-start.8 = (f32[256,1536]{1,0:T(8,128)}, f32[256,1536]{1,0:T(8,128)S(1)}, u32[]{:S(2)}) copy-start(f32[256,1536]{1,0:T(8,128)S(1)} %get-tuple-element.51.kept) | copy-start | bytes 4718596
  88.1 16.5 %collective-permute-start.19 = (f32[256,1536]{1,0:T(8,128)S(1)}, f32[256,1536]{1,0:T(8,128)S(1)}, u32[]{:S(2)}, u32[]{:S(2)}) collective-permute-start(f32[256,1536]{1,0:T(8,128)S(1)} %get-tuple-element.52), channel_id=1, source_target_pairs={{0,32},{1,33},{2,34},{3,35},{8,40},{9,41},{10,42},{11,43},{16,48},... | collective-permute-start | bytes 4718600 | tf_op jit(solution)/shard_map/ppermute | solution.py:38
  88.2 16.4 %collective-permute-start.17 = (bf16[128,4096]{1,0:T(8,128)(2,1)S(1)}, bf16[128,4096]{1,0:T(8,128)(2,1)S(1)}, u32[]{:S(2)}, u32[]{:S(2)}) collective-permute-start(bf16[128,4096]{1,0:T(8,128)(2,1)S(1)} %constant_dynamic-update-slice_fusion.6.refs_1_.refs_2_), channel_id=1, source_target_pairs={{0,8},{1,9},{2,10},{3,11},{8,16},{9,17},{10,18},{11,19},{16,24},{1... | collective-permute-start | bytes 3145736 | tf_op jit(solution)/shard_map/ppermute | solution.py:38
  88.2 16.3 %collective-permute-start.18 = (bf16[128,4096]{1,0:T(8,128)(2,1)}, bf16[128,4096]{1,0:T(8,128)(2,1)S(1)}, u32[]{:S(2)}, u32[]{:S(2)}) collective-permute-start(bf16[128,4096]{1,0:T(8,128)(2,1)} %collective-permute-done.11.refs_4_), channel_id=1, source_target_pairs={{0,24},{1,25},{2,26},{3,27},{8,0},{9,1},{10,2},{11,3},{16,8},{17,9... | collective-permute-start | bytes 3145736 | tf_op jit(solution)/shard_map/ppermute | solution.py:38
  105.7 20.2 %copy-start.4 = (f32[256,1536]{1,0:T(8,128)}, f32[256,1536]{1,0:T(8,128)S(1)}, u32[]{:S(2)}) copy-start(f32[256,1536]{1,0:T(8,128)S(1)} %get-tuple-element.63.kept) | copy-start | bytes 4718596
  105.7 20.2 %collective-permute-start.22 = (f32[256,1536]{1,0:T(8,128)S(1)}, f32[256,1536]{1,0:T(8,128)S(1)}, u32[]{:S(2)}, u32[]{:S(2)}) collective-permute-start(f32[256,1536]{1,0:T(8,128)S(1)} %get-tuple-element.59), channel_id=1, source_target_pairs={{0,32},{1,33},{2,34},{3,35},{8,40},{9,41},{10,42},{11,43},{16,48},... | collective-permute-start | bytes 4718600 | tf_op jit(solution)/shard_map/ppermute | solution.py:38
  106.4 15.8 %collective-permute-start.21 = (bf16[128,4096]{1,0:T(8,128)(2,1)S(1)}, bf16[128,4096]{1,0:T(8,128)(2,1)S(1)}, u32[]{:S(2)}, u32[]{:S(2)}) collective-permute-start(bf16[128,4096]{1,0:T(8,128)(2,1)S(1)} %copy-done.21), channel_id=1, source_target_pairs={{0,24},{1,25},{2,26},{3,27},{8,0},{9,1},{10,2},{11,3},{16,8},{17,9... | collective-permute-start | bytes 3145736 | tf_op jit(solution)/shard_map/ppermute | solution.py:38
  109.9 16.0 %collective-permute-start.20 = (bf16[128,4096]{1,0:T(8,128)(2,1)S(1)}, bf16[128,4096]{1,0:T(8,128)(2,1)S(1)}, u32[]{:S(2)}, u32[]{:S(2)}) collective-permute-start(bf16[128,4096]{1,0:T(8,128)(2,1)S(1)} %collective-permute-done.17.refs_1_), channel_id=1, source_target_pairs={{0,8},{1,9},{2,10},{3,11},{8,16},{9,17},{10,18},{11,19},{16,24},{1... | collective-permute-start | bytes 3145736 | tf_op jit(solution)/shard_map/ppermute | solution.py:38
  109.9 12.3 %collective-permute-start.23 = (s16[144,1536]{1,0:T(8,128)(2,1)S(1)}, s16[144,1536]{1,0:T(8,128)(2,1)S(1)}, u32[]{:S(2)}, u32[]{:S(2)}) collective-permute-start(s16[144,1536]{1,0:T(8,128)(2,1)S(1)} %shard_map.41), channel_id=1, source_target_pairs={{0,64},{1,65},{2,66},{3,67},{8,72},{9,73},{10,74},{11,75},{16,80},... | collective-permute-start | bytes 1327112 | tf_op jit(solution)/shard_map/ppermute | solution.py:38
  130.1 3.8 %collective-permute-start.24 = (f32[256,1536]{1,0:T(8,128)}, f32[256,1536]{1,0:T(8,128)}, u32[]{:S(2)}, u32[]{:S(2)}) collective-permute-start(f32[256,1536]{1,0:T(8,128)} %get-tuple-element.68), channel_id=1, source_target_pairs={{0,32},{1,33},{2,34},{3,35},{8,40},{9,41},{10,42},{11,43},{16,48},... | collective-permute-start | bytes 4718600 | tf_op jit(solution)/shard_map/ppermute | solution.py:38
  135.2 14.5 %collective-permute-start.25 = (s16[144,1536]{1,0:T(8,128)(2,1)S(1)}, s16[144,1536]{1,0:T(8,128)(2,1)S(1)}, u32[]{:S(2)}, u32[]{:S(2)}) collective-permute-start(s16[144,1536]{1,0:T(8,128)(2,1)S(1)} %copy-done.17), channel_id=1, source_target_pairs={{0,64},{1,65},{2,66},{3,67},{8,72},{9,73},{10,74},{11,75},{16,80},... | collective-permute-start | bytes 1327112 | tf_op jit(solution)/shard_map/ppermute | solution.py:38
  137.3 21.6 %collective-permute-start.27 = (s16[144,1536]{1,0:T(8,128)(2,1)S(1)}, s16[144,1536]{1,0:T(8,128)(2,1)S(1)}, u32[]{:S(2)}, u32[]{:S(2)}) collective-permute-start(s16[144,1536]{1,0:T(8,128)(2,1)S(1)} %shard_map.46), channel_id=1, source_target_pairs={{0,64},{1,65},{2,66},{3,67},{8,72},{9,73},{10,74},{11,75},{16,80},... | collective-permute-start | bytes 1327112 | tf_op jit(solution)/shard_map/ppermute | solution.py:38
  150.7 8.5 %collective-permute-start.26 = (f32[256,1536]{1,0:T(8,128)S(1)}, f32[256,1536]{1,0:T(8,128)S(1)}, u32[]{:S(2)}, u32[]{:S(2)}) collective-permute-start(f32[256,1536]{1,0:T(8,128)S(1)} %get-tuple-element.79), channel_id=1, source_target_pairs={{0,32},{1,33},{2,34},{3,35},{8,40},{9,41},{10,42},{11,43},{16,48},... | collective-permute-start | bytes 4718600 | tf_op jit(solution)/shard_map/ppermute | solution.py:38
  159.4 13.4 %collective-permute-start.28 = (s16[144,1536]{1,0:T(8,128)(2,1)S(1)}, s16[144,1536]{1,0:T(8,128)(2,1)S(1)}, u32[]{:S(2)}, u32[]{:S(2)}) collective-permute-start(s16[144,1536]{1,0:T(8,128)(2,1)S(1)} %shard_map.49), channel_id=1, source_target_pairs={{0,64},{1,65},{2,66},{3,67},{8,72},{9,73},{10,74},{11,75},{16,80},... | collective-permute-start | bytes 1327112 | tf_op jit(solution)/shard_map/ppermute | solution.py:38
  (20 other events, 99.8 us)

commit v4 on v3

--- a/solution.py
+++ b/solution.py
@@ -198,19 +198,19 @@
 
     message_1, order = join(narrow(keep_1, got_1), order)
     away_3, keep_3 = pick(order, [part_a, part_b, part_c, part_d], [(0, 4), (1, 3), (3, 0), (2, 1)])
+    message_1, away_3 = join(message_1, away_3)
     got_3 = send(away_3, CORE)
-    message_1, got_3 = join(message_1, got_3)
     far_1 = send(message_1, ACROSS)
     message_3 = narrow(keep_3, got_3)
     down_6, up_6, message_3 = join(down_6, up_6, message_3)
     far_3 = send(message_3, ACROSS)
     part_e = products(core, [(down_6, down_6), (up_6, up_6)], train)
-    far_1, part_e = join(far_1, part_e)
+    far_1, part_e, far_0 = join(far_1, part_e, far_0)
     away_2, keep_2 = pick(order, [part_c, part_d, part_e], [(0, 2), (2, 0), (2, 1), (1, 1)])
     got_2 = send(away_2, CORE)
     message_2 = narrow(keep_2, got_2)
-    keep_3, message_2 = join(keep_3, message_2)
     far_2 = send(message_2, ACROSS)
+    keep_3, far_2 = join(keep_3, far_2)
 
     out = jnp.zeros((2, 4, 64, train.shape[0]), jnp.float32)
     for dy, keep, got, message in ((0, keep_0, got_0, far_0), (1, keep_1, got_1, far_1), (3, keep_3, got_3, far_3), (2, keep_2, got_2, far_2)):

time: 175 us -> 174 us (level)
  waiting for transfers between devices: 59.9 us -> 55.3 us
  local copies, waits for them, and re-layouts: 8.28 us -> 12.4 us
    ppermute x29, waiting for transfers between devices: 59.9 us -> 55.3 us  [send(): return lax.ppermute(value, BOTH, pairs)]
    unnamed x50 -> x60, local copies, waits for them, and re-layouts: 6.71 us -> 10.8 us
  transfers between devices with their start and end apart: 29 -> 29, of which waited for: 15 -> 16; matrix products, arithmetic and copies ran while one was open for 5% -> 4% of each run, Pallas kernels for 29% -> 28%
where the time goes in v4:
time: 174 us; the launch traced here: 173 us
  waiting for transfers between devices  55.3 us (32%)
  Pallas kernels  55.1 us (32%)
  starting transfers between devices  41.3 us (24%)
  local copies, waits for them, and re-layouts  12.4 us (7%)
  other arithmetic  8.54 us (5%)
    ppermute x29, waiting for transfers between devices, send(): return lax.ppermute(value, BOTH, pairs)  55.3 us
    pallas_call x5, Pallas kernels, products(): pl.pallas_call(functools.partial(product_kernel, choices, len(blocks)), g...  47.6 us
    ppermute x29, starting transfers between devices, send(): return lax.ppermute(value, BOTH, pairs)  41.3 us
    unnamed x60, local copies, waits for them, and re-layouts  10.8 us
    pallas_call x4, Pallas kernels, pick(): pl.pallas_call(functools.partial(pick_kernel, spots, len(parts)), in_spec...  4.68 us
  transfers between devices with their start and end apart: 29, of which 16 were waited for; matrix products, arithmetic and copies ran while one was open for 4% of the time, Pallas kernels for 28%

profile of v4, /device:TPU:2, one launch (start us, length us, event | category | flops | bytes accessed | tf_op | source)
XLA Modules:
  0.0 173.2 jit_solution(43136576954073224)
XLA Ops:
  2.4 3.1 %collective-permute-start.3 = (bf16[64,4096]{1,0:T(8,128)(2,1)S(1)}, bf16[64,4096]{1,0:T(8,128)(2,1)S(1)}, u32[]{:S(2)}, u32[]{:S(2)}) collective-permute-start(bf16[64,4096]{1,0:T(8,128)(2,1)S(1)} %fusion), channel_id=1, source_target_pairs={{0,3},{1,0},{2,1},{3,2},{8,11},{9,8},{10,9},{11,10},{16,19},{17,16... | collective-permute-start | bytes 1572872 | tf_op jit(solution)/shard_map/ppermute | solution.py:38
  5.5 1.9 %collective-permute-start.6 = (bf16[64,4096]{1,0:T(8,128)(2,1)S(1)}, bf16[64,4096]{1,0:T(8,128)(2,1)S(1)}, u32[]{:S(2)}, u32[]{:S(2)}) collective-permute-start(bf16[64,4096]{1,0:T(8,128)(2,1)S(1)} %fusion), channel_id=1, source_target_pairs={{0,8},{1,9},{2,10},{3,11},{8,16},{9,17},{10,18},{11,19},{16,24},{1... | collective-permute-start | bytes 1572872 | tf_op jit(solution)/shard_map/ppermute | solution.py:38
  7.4 2.1 %collective-permute-start.12 = (bf16[64,4096]{1,0:T(8,128)(2,1)S(1)}, bf16[64,4096]{1,0:T(8,128)(2,1)}, u32[]{:S(2)}, u32[]{:S(2)}) collective-permute-start(bf16[64,4096]{1,0:T(8,128)(2,1)S(1)} %fusion), channel_id=1, source_target_pairs={{0,24},{1,25},{2,26},{3,27},{8,0},{9,1},{10,2},{11,3},{16,8},{17,9... | collective-permute-start | bytes 1572872 | tf_op jit(solution)/shard_map/ppermute | solution.py:38
  9.5 6.1 %collective-permute-done = bf16[64,4096]{1,0:T(8,128)(2,1)S(1)} collective-permute-done((bf16[64,4096]{1,0:T(8,128)(2,1)S(1)}, bf16[64,4096]{1,0:T(8,128)(2,1)S(1)}, u32[]{:S(2)}, u32[]{:S(2)}) %collective-permute-start) | collective-permute-done | bytes 524320 | tf_op jit(solution)/shard_map/ppermute | solution.py:38
  15.6 3.0 %collective-permute-start.1 = (bf16[64,4096]{1,0:T(8,128)(2,1)S(1)}, bf16[64,4096]{1,0:T(8,128)(2,1)S(1)}, u32[]{:S(2)}, u32[]{:S(2)}) collective-permute-start(bf16[64,4096]{1,0:T(8,128)(2,1)S(1)} %collective-permute-done), channel_id=1, source_target_pairs={{0,3},{1,0},{2,1},{3,2},{8,11},{9,8},{10,9},{11,10},{16,19},{17,16... | collective-permute-start | bytes 1572872 | tf_op jit(solution)/shard_map/ppermute | solution.py:38
  18.8 2.1 %collective-permute-done.9 = bf16[64,4096]{1,0:T(8,128)(2,1)S(1)} collective-permute-done((bf16[64,4096]{1,0:T(8,128)(2,1)S(1)}, bf16[64,4096]{1,0:T(8,128)(2,1)S(1)}, u32[]{:S(2)}, u32[]{:S(2)}) %collective-permute-start.9) | collective-permute-done | bytes 524320 | tf_op jit(solution)/shard_map/ppermute | solution.py:38
  21.7 3.2 %collective-permute-start.13 = (bf16[64,4096]{1,0:T(8,128)(2,1)S(1)}, bf16[64,4096]{1,0:T(8,128)(2,1)S(1)}, u32[]{:S(2)}, u32[]{:S(2)}) collective-permute-start(bf16[64,4096]{1,0:T(8,128)(2,1)S(1)} %collective-permute-done), channel_id=1, source_target_pairs={{0,24},{1,25},{2,26},{3,27},{8,0},{9,1},{10,2},{11,3},{16,8},{17,9... | collective-permute-start | bytes 1572872 | tf_op jit(solution)/shard_map/ppermute | solution.py:38
  25.0 2.3 %collective-permute-done.1 = bf16[64,4096]{1,0:T(8,128)(2,1)S(1)} collective-permute-done((bf16[64,4096]{1,0:T(8,128)(2,1)S(1)}, bf16[64,4096]{1,0:T(8,128)(2,1)S(1)}, u32[]{:S(2)}, u32[]{:S(2)}) %collective-permute-start.1) | collective-permute-done | bytes 524320 | tf_op jit(solution)/shard_map/ppermute | solution.py:38
  27.3 7.1 %collective-permute-done.10 = bf16[64,4096]{1,0:T(8,128)(2,1)S(1)} collective-permute-done((bf16[64,4096]{1,0:T(8,128)(2,1)S(1)}, bf16[64,4096]{1,0:T(8,128)(2,1)S(1)}, u32[]{:S(2)}, u32[]{:S(2)}) %collective-permute-start.10) | collective-permute-done | bytes 524320 | tf_op jit(solution)/shard_map/ppermute | solution.py:38
  37.0 2.6 %collective-permute-start.5 = (bf16[128,4096]{1,0:T(8,128)(2,1)S(1)}, bf16[128,4096]{1,0:T(8,128)(2,1)S(1)}, u32[]{:S(2)}, u32[]{:S(2)}) collective-permute-start(bf16[128,4096]{1,0:T(8,128)(2,1)S(1)} %constant_dynamic-update-slice_fusion.refs_2_), channel_id=1, source_target_pairs={{0,24},{1,25},{2,26},{3,27},{8,0},{9,1},{10,2},{11,3},{16,8},{17,9... | collective-permute-start | bytes 3145736 | tf_op jit(solution)/shard_map/ppermute | solution.py:38
  39.6 2.1 %collective-permute-start.11 = (bf16[128,4096]{1,0:T(8,128)(2,1)}, bf16[128,4096]{1,0:T(8,128)(2,1)S(1)}, u32[]{:S(2)}, u32[]{:S(2)}) collective-permute-start(bf16[128,4096]{1,0:T(8,128)(2,1)} %constant_dynamic-update-slice_fusion.4.refs_4_), channel_id=1, source_target_pairs={{0,24},{1,25},{2,26},{3,27},{8,0},{9,1},{10,2},{11,3},{16,8},{17,9... | collective-permute-start | bytes 3145736 | tf_op jit(solution)/shard_map/ppermute | solution.py:38
  42.8 2.0 %collective-permute-done.15 = bf16[64,4096]{1,0:T(8,128)(2,1)S(1)} collective-permute-done((bf16[64,4096]{1,0:T(8,128)(2,1)S(1)}, bf16[64,4096]{1,0:T(8,128)(2,1)S(1)}, u32[]{:S(2)}, u32[]{:S(2)}) %collective-permute-start.15) | collective-permute-done | bytes 524320 | tf_op jit(solution)/shard_map/ppermute | solution.py:38
  44.8 13.0 %shard_map.37.refs_0_ = f32[640,1536]{1,0:T(8,128)S(1)} custom-call(s32[1]{0:T(128)} %bitcast.6.core, bf16[128,4096]{1,0:T(8,128)(2,1)S(1)} %pad_maximum_fusion.refs_0_, bf16[128,4096]{1,0:T(8,128)(2,1)S(1)} %pad_maximum_fusion.1.refs_1_, bf16[128,4096]{1,0:T(8,128)(2,1)S(1)} %constant_dynamic-update-slice_fusion.refs_2_, ...), custom_call_target="tpu_custom_call" | custom-call | flops 8053063680 | bytes 21757952 | tf_op jit(solution)/shard_map/pallas_call | solution.py:74
  57.8 1.8 %collective-permute-done.2 = bf16[64,4096]{1,0:T(8,128)(2,1)S(1)} collective-permute-done((bf16[64,4096]{1,0:T(8,128)(2,1)S(1)}, bf16[64,4096]{1,0:T(8,128)(2,1)S(1)}, u32[]{:S(2)}, u32[]{:S(2)}) %collective-permute-start.2) | collective-permute-done | bytes 524320 | tf_op jit(solution)/shard_map/ppermute | solution.py:38
  59.7 4.0 %collective-permute-start.14 = (bf16[128,4096]{1,0:T(8,128)(2,1)}, bf16[128,4096]{1,0:T(8,128)(2,1)}, u32[]{:S(2)}, u32[]{:S(2)}) collective-permute-start(bf16[128,4096]{1,0:T(8,128)(2,1)} %constant_dynamic-update-slice_fusion.4.refs_4_), channel_id=1, source_target_pairs={{0,8},{1,9},{2,10},{3,11},{8,16},{9,17},{10,18},{11,19},{16,24},{1... | collective-permute-start | bytes 3145736 | tf_op jit(solution)/shard_map/ppermute | solution.py:38
  63.7 5.1 %collective-permute-done.11.refs_4_ = bf16[128,4096]{1,0:T(8,128)(2,1)S(1)} collective-permute-done((bf16[128,4096]{1,0:T(8,128)(2,1)}, bf16[128,4096]{1,0:T(8,128)(2,1)S(1)}, u32[]{:S(2)}, u32[]{:S(2)}) %collective-permute-start.11) | collective-permute-done | bytes 1048608 | tf_op jit(solution)/shard_map/ppermute | solution.py:38
  71.5 3.6 %collective-permute-start.16 = (bf16[128,4096]{1,0:T(8,128)(2,1)}, bf16[128,4096]{1,0:T(8,128)(2,1)}, u32[]{:S(2)}, u32[]{:S(2)}) collective-permute-start(bf16[128,4096]{1,0:T(8,128)(2,1)} %get-tuple-element.86), channel_id=1, source_target_pairs={{0,24},{1,25},{2,26},{3,27},{8,0},{9,1},{10,2},{11,3},{16,8},{17,9... | collective-permute-start | bytes 3145736 | tf_op jit(solution)/shard_map/ppermute | solution.py:38
  77.7 10.0 %shard_map.38.refs_1_ = f32[512,1536]{1,0:T(8,128)S(1)} custom-call(s32[1]{0:T(128)} %bitcast.6.core, bf16[128,4096]{1,0:T(8,128)(2,1)S(1)} %collective-permute-done.8.refs_0_.refs_3_, bf16[128,4096]{1,0:T(8,128)(2,1)S(1)} %constant_dynamic-update-slice_fusion.6.refs_1_.refs_2_, bf16[128,4096]{1,0:T(8,128)(2,1)S(1)} %collective-permute-done.5.refs_2_, ...), custom_call_target="tpu_custom_call" | custom-call | flops 6442450944 | bytes 19922944 | tf_op jit(solution)/shard_map/pallas_call | solution.py:74
  89.1 3.8 %collective-permute-start.18 = (bf16[128,4096]{1,0:T(8,128)(2,1)S(1)}, bf16[128,4096]{1,0:T(8,128)(2,1)S(1)}, u32[]{:S(2)}, u32[]{:S(2)}) collective-permute-start(bf16[128,4096]{1,0:T(8,128)(2,1)S(1)} %copy-done.21), channel_id=1, source_target_pairs={{0,24},{1,25},{2,26},{3,27},{8,0},{9,1},{10,2},{11,3},{16,8},{17,9... | collective-permute-start | bytes 3145736 | tf_op jit(solution)/shard_map/ppermute | solution.py:38
  92.8 10.1 %shard_map.40.refs_2_.refs_0_ = f32[384,1536]{1,0:T(8,128)S(1)} custom-call(s32[1]{0:T(128)} %bitcast.6.core, bf16[128,4096]{1,0:T(8,128)(2,1)} %collective-permute-done.16.refs_0_, bf16[128,4096]{1,0:T(8,128)(2,1)} %collective-permute-done.14.refs_1_, bf16[128,4096]{1,0:T(8,128)(2,1)S(1)} %constant_dynamic-update-slice_fusion.6.refs_1_.refs_2_, ...), custom_call_target="tpu_custom_call" | custom-call | flops 4831838208 | bytes 18087936 | tf_op jit(solution)/shard_map/pallas_call | solution.py:74
  103.0 2.5 %collective-permute-done.17.refs_1_ = bf16[128,4096]{1,0:T(8,128)(2,1)S(1)} collective-permute-done((bf16[128,4096]{1,0:T(8,128)(2,1)S(1)}, bf16[128,4096]{1,0:T(8,128)(2,1)S(1)}, u32[]{:S(2)}, u32[]{:S(2)}) %collective-permute-start.17) | collective-permute-done | bytes 1048608 | tf_op jit(solution)/shard_map/ppermute | solution.py:38
  107.3 3.3 %collective-permute-start.21 = (bf16[128,4096]{1,0:T(8,128)(2,1)S(1)}, bf16[128,4096]{1,0:T(8,128)(2,1)S(1)}, u32[]{:S(2)}, u32[]{:S(2)}) collective-permute-start(bf16[128,4096]{1,0:T(8,128)(2,1)S(1)} %copy-done.25), channel_id=1, source_target_pairs={{0,24},{1,25},{2,26},{3,27},{8,0},{9,1},{10,2},{11,3},{16,8},{17,9... | collective-permute-start | bytes 3145736 | tf_op jit(solution)/shard_map/ppermute | solution.py:38
  110.6 2.0 %collective-permute-start.23 = (s16[144,1536]{1,0:T(8,128)(2,1)S(1)}, s16[144,1536]{1,0:T(8,128)(2,1)S(1)}, u32[]{:S(2)}, u32[]{:S(2)}) collective-permute-start(s16[144,1536]{1,0:T(8,128)(2,1)S(1)} %shard_map.41), channel_id=1, source_target_pairs={{0,64},{1,65},{2,66},{3,67},{8,72},{9,73},{10,74},{11,75},{16,80},... | collective-permute-start | bytes 1327112 | tf_op jit(solution)/shard_map/ppermute | solution.py:38
  112.6 7.2 %shard_map.43.refs_3_.refs_1_ = f32[256,1536]{1,0:T(8,128)S(1)} custom-call(s32[1]{0:T(128)} %bitcast.6.core, bf16[128,4096]{1,0:T(8,128)(2,1)S(1)} %collective-permute-done.18.refs_0_, bf16[128,4096]{1,0:T(8,128)(2,1)S(1)} %collective-permute-done.17.refs_1_, bf16[1536,4096]{1,0:T(8,128)(2,1)} %bitcast.47), custom_call_target="tpu_custom_call" | custom-call | flops 3221225472 | bytes 16252928 | tf_op jit(solution)/shard_map/pallas_call | solution.py:74
  119.8 3.1 %collective-permute-done.21.refs_0_ = bf16[128,4096]{1,0:T(8,128)(2,1)S(1)} collective-permute-done((bf16[128,4096]{1,0:T(8,128)(2,1)S(1)}, bf16[128,4096]{1,0:T(8,128)(2,1)S(1)}, u32[]{:S(2)}, u32[]{:S(2)}) %collective-permute-start.21) | collective-permute-done | bytes 1048608 | tf_op jit(solution)/shard_map/ppermute | solution.py:38
  123.0 3.7 %collective-permute-done.20.refs_1_ = bf16[128,4096]{1,0:T(8,128)(2,1)S(1)} collective-permute-done((bf16[128,4096]{1,0:T(8,128)(2,1)S(1)}, bf16[128,4096]{1,0:T(8,128)(2,1)S(1)}, u32[]{:S(2)}, u32[]{:S(2)}) %collective-permute-start.20) | collective-permute-done | bytes 1048608 | tf_op jit(solution)/shard_map/ppermute | solution.py:38
  130.8 2.0 %collective-permute-start.24 = (s16[144,1536]{1,0:T(8,128)(2,1)}, s16[144,1536]{1,0:T(8,128)(2,1)}, u32[]{:S(2)}, u32[]{:S(2)}) collective-permute-start(s16[144,1536]{1,0:T(8,128)(2,1)} %shard_map.44), channel_id=1, source_target_pairs={{0,64},{1,65},{2,66},{3,67},{8,72},{9,73},{10,74},{11,75},{16,80},... | collective-permute-start | bytes 1327112 | tf_op jit(solution)/shard_map/ppermute | solution.py:38
  132.7 1.8 %collective-permute-done.25.got = f32[256,1536]{1,0:T(8,128)} collective-permute-done((f32[256,1536]{1,0:T(8,128)}, f32[256,1536]{1,0:T(8,128)}, u32[]{:S(2)}, u32[]{:S(2)}) %collective-permute-start.25) | collective-permute-done | bytes 1572896 | tf_op jit(solution)/shard_map/ppermute | solution.py:38
  137.4 7.3 %shard_map.47.refs_2_ = f32[256,1536]{1,0:T(8,128)S(1)} custom-call(s32[1]{0:T(128)} %bitcast.6.core, bf16[128,4096]{1,0:T(8,128)(2,1)S(1)} %collective-permute-done.21.refs_0_, bf16[128,4096]{1,0:T(8,128)(2,1)S(1)} %copy-done.16, bf16[1536,4096]{1,0:T(8,128)(2,1)} %bitcast.48), custom_call_target="tpu_custom_call" | custom-call | flops 3221225472 | bytes 16252928 | tf_op jit(solution)/shard_map/pallas_call | solution.py:74
  146.2 2.1 %collective-permute-start.28 = (s16[144,1536]{1,0:T(8,128)(2,1)S(1)}, s16[144,1536]{1,0:T(8,128)(2,1)S(1)}, u32[]{:S(2)}, u32[]{:S(2)}) collective-permute-start(s16[144,1536]{1,0:T(8,128)(2,1)S(1)} %shard_map.46), channel_id=1, source_target_pairs={{0,64},{1,65},{2,66},{3,67},{8,72},{9,73},{10,74},{11,75},{16,80},... | collective-permute-start | bytes 1327112 | tf_op jit(solution)/shard_map/ppermute | solution.py:38
  154.2 6.5 %collective-permute-done.28 = s16[144,1536]{1,0:T(8,128)(2,1)S(1)} collective-permute-done((s16[144,1536]{1,0:T(8,128)(2,1)S(1)}, s16[144,1536]{1,0:T(8,128)(2,1)S(1)}, u32[]{:S(2)}, u32[]{:S(2)}) %collective-permute-start.28) | collective-permute-done | bytes 442400 | tf_op jit(solution)/shard_map/ppermute | solution.py:38
  160.8 9.0 %collective-permute-done.27 = s16[144,1536]{1,0:T(8,128)(2,1)S(1)} collective-permute-done((s16[144,1536]{1,0:T(8,128)(2,1)S(1)}, s16[144,1536]{1,0:T(8,128)(2,1)S(1)}, u32[]{:S(2)}, u32[]{:S(2)}) %collective-permute-start.27) | collective-permute-done | bytes 442400 | tf_op jit(solution)/shard_map/ppermute | solution.py:38
  (125 shorter events, 33.2 us)
Async XLA Ops:
  1.9 13.7 %collective-permute-start = (bf16[64,4096]{1,0:T(8,128)(2,1)S(1)}, bf16[64,4096]{1,0:T(8,128)(2,1)S(1)}, u32[]{:S(2)}, u32[]{:S(2)}) collective-permute-start(bf16[64,4096]{1,0:T(8,128)(2,1)S(1)} %fusion), channel_id=1, source_target_pairs={{0,4},{1,5},{2,6},{3,7},{8,12},{9,13},{10,14},{11,15},{16,20},{17,... | collective-permute-start | bytes 1572872 | tf_op jit(solution)/shard_map/ppermute | solution.py:38
  2.4 16.3 %collective-permute-start.3 = (bf16[64,4096]{1,0:T(8,128)(2,1)S(1)}, bf16[64,4096]{1,0:T(8,128)(2,1)S(1)}, u32[]{:S(2)}, u32[]{:S(2)}) collective-permute-start(bf16[64,4096]{1,0:T(8,128)(2,1)S(1)} %fusion), channel_id=1, source_target_pairs={{0,3},{1,0},{2,1},{3,2},{8,11},{9,8},{10,9},{11,10},{16,19},{17,16... | collective-permute-start | bytes 1572872 | tf_op jit(solution)/shard_map/ppermute | solution.py:38
  5.5 15.4 %collective-permute-start.9 = (bf16[64,4096]{1,0:T(8,128)(2,1)S(1)}, bf16[64,4096]{1,0:T(8,128)(2,1)S(1)}, u32[]{:S(2)}, u32[]{:S(2)}) collective-permute-start(bf16[64,4096]{1,0:T(8,128)(2,1)S(1)} %fusion), channel_id=1, source_target_pairs={{0,1},{1,2},{2,3},{3,0},{8,9},{9,10},{10,11},{11,8},{16,17},{17,18... | collective-permute-start | bytes 1572872 | tf_op jit(solution)/shard_map/ppermute | solution.py:38
  5.5 16.2 %collective-permute-start.6 = (bf16[64,4096]{1,0:T(8,128)(2,1)S(1)}, bf16[64,4096]{1,0:T(8,128)(2,1)S(1)}, u32[]{:S(2)}, u32[]{:S(2)}) collective-permute-start(bf16[64,4096]{1,0:T(8,128)(2,1)S(1)} %fusion), channel_id=1, source_target_pairs={{0,8},{1,9},{2,10},{3,11},{8,16},{9,17},{10,18},{11,19},{16,24},{1... | collective-permute-start | bytes 1572872 | tf_op jit(solution)/shard_map/ppermute | solution.py:38
  7.4 32.1 %collective-permute-start.12 = (bf16[64,4096]{1,0:T(8,128)(2,1)S(1)}, bf16[64,4096]{1,0:T(8,128)(2,1)}, u32[]{:S(2)}, u32[]{:S(2)}) collective-permute-start(bf16[64,4096]{1,0:T(8,128)(2,1)S(1)} %fusion), channel_id=1, source_target_pairs={{0,24},{1,25},{2,26},{3,27},{8,0},{9,1},{10,2},{11,3},{16,8},{17,9... | collective-permute-start | bytes 1572872 | tf_op jit(solution)/shard_map/ppermute | solution.py:38
  15.6 11.7 %collective-permute-start.1 = (bf16[64,4096]{1,0:T(8,128)(2,1)S(1)}, bf16[64,4096]{1,0:T(8,128)(2,1)S(1)}, u32[]{:S(2)}, u32[]{:S(2)}) collective-permute-start(bf16[64,4096]{1,0:T(8,128)(2,1)S(1)} %collective-permute-done), channel_id=1, source_target_pairs={{0,3},{1,0},{2,1},{3,2},{8,11},{9,8},{10,9},{11,10},{16,19},{17,16... | collective-permute-start | bytes 1572872 | tf_op jit(solution)/shard_map/ppermute | solution.py:38
  18.7 15.7 %collective-permute-start.10 = (bf16[64,4096]{1,0:T(8,128)(2,1)S(1)}, bf16[64,4096]{1,0:T(8,128)(2,1)S(1)}, u32[]{:S(2)}, u32[]{:S(2)}) collective-permute-start(bf16[64,4096]{1,0:T(8,128)(2,1)S(1)} %collective-permute-done), channel_id=1, source_target_pairs={{0,1},{1,2},{2,3},{3,0},{8,9},{9,10},{10,11},{11,8},{16,17},{17,18... | collective-permute-start | bytes 1572872 | tf_op jit(solution)/shard_map/ppermute | solution.py:38
  20.9 16.1 %collective-permute-start.7 = (bf16[64,4096]{1,0:T(8,128)(2,1)S(1)}, bf16[64,4096]{1,0:T(8,128)(2,1)S(1)}, u32[]{:S(2)}, u32[]{:S(2)}) collective-permute-start(bf16[64,4096]{1,0:T(8,128)(2,1)S(1)} %collective-permute-done), channel_id=1, source_target_pairs={{0,8},{1,9},{2,10},{3,11},{8,16},{9,17},{10,18},{11,19},{16,24},{1... | collective-permute-start | bytes 1572872 | tf_op jit(solution)/shard_map/ppermute | solution.py:38
  21.7 19.9 %collective-permute-start.13 = (bf16[64,4096]{1,0:T(8,128)(2,1)S(1)}, bf16[64,4096]{1,0:T(8,128)(2,1)S(1)}, u32[]{:S(2)}, u32[]{:S(2)}) collective-permute-start(bf16[64,4096]{1,0:T(8,128)(2,1)S(1)} %collective-permute-done), channel_id=1, source_target_pairs={{0,24},{1,25},{2,26},{3,27},{8,0},{9,1},{10,2},{11,3},{16,8},{17,9... | collective-permute-start | bytes 1572872 | tf_op jit(solution)/shard_map/ppermute | solution.py:38
  27.3 17.5 %collective-permute-start.15 = (bf16[64,4096]{1,0:T(8,128)(2,1)S(1)}, bf16[64,4096]{1,0:T(8,128)(2,1)S(1)}, u32[]{:S(2)}, u32[]{:S(2)}) collective-permute-start(bf16[64,4096]{1,0:T(8,128)(2,1)S(1)} %collective-permute-done.9), channel_id=1, source_target_pairs={{0,1},{1,2},{2,3},{3,0},{8,9},{9,10},{10,11},{11,8},{16,17},{17,18... | collective-permute-start | bytes 1572872 | tf_op jit(solution)/shard_map/ppermute | solution.py:38
  34.4 34.4 %collective-permute-start.4 = (bf16[128,4096]{1,0:T(8,128)(2,1)S(1)}, bf16[128,4096]{1,0:T(8,128)(2,1)S(1)}, u32[]{:S(2)}, u32[]{:S(2)}) collective-permute-start(bf16[128,4096]{1,0:T(8,128)(2,1)S(1)} %constant_dynamic-update-slice_fusion.refs_2_), channel_id=1, source_target_pairs={{0,8},{1,9},{2,10},{3,11},{8,16},{9,17},{10,18},{11,19},{16,24},{1... | collective-permute-start | bytes 3145736 | tf_op jit(solution)/shard_map/ppermute | solution.py:38
  37.0 32.9 %collective-permute-start.5 = (bf16[128,4096]{1,0:T(8,128)(2,1)S(1)}, bf16[128,4096]{1,0:T(8,128)(2,1)S(1)}, u32[]{:S(2)}, u32[]{:S(2)}) collective-permute-start(bf16[128,4096]{1,0:T(8,128)(2,1)S(1)} %constant_dynamic-update-slice_fusion.refs_2_), channel_id=1, source_target_pairs={{0,24},{1,25},{2,26},{3,27},{8,0},{9,1},{10,2},{11,3},{16,8},{17,9... | collective-permute-start | bytes 3145736 | tf_op jit(solution)/shard_map/ppermute | solution.py:38
  39.6 29.2 %collective-permute-start.11 = (bf16[128,4096]{1,0:T(8,128)(2,1)}, bf16[128,4096]{1,0:T(8,128)(2,1)S(1)}, u32[]{:S(2)}, u32[]{:S(2)}) collective-permute-start(bf16[128,4096]{1,0:T(8,128)(2,1)} %constant_dynamic-update-slice_fusion.4.refs_4_), channel_id=1, source_target_pairs={{0,24},{1,25},{2,26},{3,27},{8,0},{9,1},{10,2},{11,3},{16,8},{17,9... | collective-permute-start | bytes 3145736 | tf_op jit(solution)/shard_map/ppermute | solution.py:38
  41.7 28.2 %collective-permute-start.8 = (bf16[128,4096]{1,0:T(8,128)(2,1)S(1)}, bf16[128,4096]{1,0:T(8,128)(2,1)S(1)}, u32[]{:S(2)}, u32[]{:S(2)}) collective-permute-start(bf16[128,4096]{1,0:T(8,128)(2,1)S(1)} %constant_dynamic-update-slice_fusion.2.refs_3_), channel_id=1, source_target_pairs={{0,8},{1,9},{2,10},{3,11},{8,16},{9,17},{10,18},{11,19},{16,24},{1... | collective-permute-start | bytes 3145736 | tf_op jit(solution)/shard_map/ppermute | solution.py:38
  44.8 14.9 %collective-permute-start.2 = (bf16[64,4096]{1,0:T(8,128)(2,1)S(1)}, bf16[64,4096]{1,0:T(8,128)(2,1)S(1)}, u32[]{:S(2)}, u32[]{:S(2)}) collective-permute-start(bf16[64,4096]{1,0:T(8,128)(2,1)S(1)} %collective-permute-done.1), channel_id=1, source_target_pairs={{0,3},{1,0},{2,1},{3,2},{8,11},{9,8},{10,9},{11,10},{16,19},{17,16... | collective-permute-start | bytes 1572872 | tf_op jit(solution)/shard_map/ppermute | solution.py:38
  59.7 28.0 %collective-permute-start.14 = (bf16[128,4096]{1,0:T(8,128)(2,1)}, bf16[128,4096]{1,0:T(8,128)(2,1)}, u32[]{:S(2)}, u32[]{:S(2)}) collective-permute-start(bf16[128,4096]{1,0:T(8,128)(2,1)} %constant_dynamic-update-slice_fusion.4.refs_4_), channel_id=1, source_target_pairs={{0,8},{1,9},{2,10},{3,11},{8,16},{9,17},{10,18},{11,19},{16,24},{1... | collective-permute-start | bytes 3145736 | tf_op jit(solution)/shard_map/ppermute | solution.py:38
  71.5 16.2 %collective-permute-start.16 = (bf16[128,4096]{1,0:T(8,128)(2,1)}, bf16[128,4096]{1,0:T(8,128)(2,1)}, u32[]{:S(2)}, u32[]{:S(2)}) collective-permute-start(bf16[128,4096]{1,0:T(8,128)(2,1)} %get-tuple-element.86), channel_id=1, source_target_pairs={{0,24},{1,25},{2,26},{3,27},{8,0},{9,1},{10,2},{11,3},{16,8},{17,9... | collective-permute-start | bytes 3145736 | tf_op jit(solution)/shard_map/ppermute | solution.py:38
  88.9 16.7 %copy-start.4 = (f32[256,1536]{1,0:T(8,128)}, f32[256,1536]{1,0:T(8,128)S(1)}, u32[]{:S(2)}) copy-start(f32[256,1536]{1,0:T(8,128)S(1)} %get-tuple-element.52.kept) | copy-start | bytes 4718596
  88.9 16.6 %collective-permute-start.19 = (f32[256,1536]{1,0:T(8,128)S(1)}, f32[256,1536]{1,0:T(8,128)S(1)}, u32[]{:S(2)}, u32[]{:S(2)}) collective-permute-start(f32[256,1536]{1,0:T(8,128)S(1)} %get-tuple-element.53), channel_id=1, source_target_pairs={{0,32},{1,33},{2,34},{3,35},{8,40},{9,41},{10,42},{11,43},{16,48},... | collective-permute-start | bytes 4718600 | tf_op jit(solution)/shard_map/ppermute | solution.py:38
  89.0 16.5 %collective-permute-start.17 = (bf16[128,4096]{1,0:T(8,128)(2,1)S(1)}, bf16[128,4096]{1,0:T(8,128)(2,1)S(1)}, u32[]{:S(2)}, u32[]{:S(2)}) collective-permute-start(bf16[128,4096]{1,0:T(8,128)(2,1)S(1)} %constant_dynamic-update-slice_fusion.6.refs_1_.refs_2_), channel_id=1, source_target_pairs={{0,8},{1,9},{2,10},{3,11},{8,16},{9,17},{10,18},{11,19},{16,24},{1... | collective-permute-start | bytes 3145736 | tf_op jit(solution)/shard_map/ppermute | solution.py:38
  89.1 16.4 %collective-permute-start.18 = (bf16[128,4096]{1,0:T(8,128)(2,1)S(1)}, bf16[128,4096]{1,0:T(8,128)(2,1)S(1)}, u32[]{:S(2)}, u32[]{:S(2)}) collective-permute-start(bf16[128,4096]{1,0:T(8,128)(2,1)S(1)} %copy-done.21), channel_id=1, source_target_pairs={{0,24},{1,25},{2,26},{3,27},{8,0},{9,1},{10,2},{11,3},{16,8},{17,9... | collective-permute-start | bytes 3145736 | tf_op jit(solution)/shard_map/ppermute | solution.py:38
  106.7 20.0 %copy-start.8 = (f32[256,1536]{1,0:T(8,128)}, f32[256,1536]{1,0:T(8,128)S(1)}, u32[]{:S(2)}) copy-start(f32[256,1536]{1,0:T(8,128)S(1)} %get-tuple-element.59.kept) | copy-start | bytes 4718596
  106.7 20.0 %collective-permute-start.22 = (f32[256,1536]{1,0:T(8,128)S(1)}, f32[256,1536]{1,0:T(8,128)S(1)}, u32[]{:S(2)}, u32[]{:S(2)}) collective-permute-start(f32[256,1536]{1,0:T(8,128)S(1)} %get-tuple-element.61), channel_id=1, source_target_pairs={{0,32},{1,33},{2,34},{3,35},{8,40},{9,41},{10,42},{11,43},{16,48},... | collective-permute-start | bytes 4718600 | tf_op jit(solution)/shard_map/ppermute | solution.py:38
  107.3 15.6 %collective-permute-start.21 = (bf16[128,4096]{1,0:T(8,128)(2,1)S(1)}, bf16[128,4096]{1,0:T(8,128)(2,1)S(1)}, u32[]{:S(2)}, u32[]{:S(2)}) collective-permute-start(bf16[128,4096]{1,0:T(8,128)(2,1)S(1)} %copy-done.25), channel_id=1, source_target_pairs={{0,24},{1,25},{2,26},{3,27},{8,0},{9,1},{10,2},{11,3},{16,8},{17,9... | collective-permute-start | bytes 3145736 | tf_op jit(solution)/shard_map/ppermute | solution.py:38
  110.6 16.0 %collective-permute-start.20 = (bf16[128,4096]{1,0:T(8,128)(2,1)S(1)}, bf16[128,4096]{1,0:T(8,128)(2,1)S(1)}, u32[]{:S(2)}, u32[]{:S(2)}) collective-permute-start(bf16[128,4096]{1,0:T(8,128)(2,1)S(1)} %collective-permute-done.17.refs_1_), channel_id=1, source_target_pairs={{0,8},{1,9},{2,10},{3,11},{8,16},{9,17},{10,18},{11,19},{16,24},{1... | collective-permute-start | bytes 3145736 | tf_op jit(solution)/shard_map/ppermute | solution.py:38
  110.6 12.3 %collective-permute-start.23 = (s16[144,1536]{1,0:T(8,128)(2,1)S(1)}, s16[144,1536]{1,0:T(8,128)(2,1)S(1)}, u32[]{:S(2)}, u32[]{:S(2)}) collective-permute-start(s16[144,1536]{1,0:T(8,128)(2,1)S(1)} %shard_map.41), channel_id=1, source_target_pairs={{0,64},{1,65},{2,66},{3,67},{8,72},{9,73},{10,74},{11,75},{16,80},... | collective-permute-start | bytes 1327112 | tf_op jit(solution)/shard_map/ppermute | solution.py:38
  130.8 3.8 %collective-permute-start.25 = (f32[256,1536]{1,0:T(8,128)}, f32[256,1536]{1,0:T(8,128)}, u32[]{:S(2)}, u32[]{:S(2)}) collective-permute-start(f32[256,1536]{1,0:T(8,128)} %get-tuple-element.73), channel_id=1, source_target_pairs={{0,32},{1,33},{2,34},{3,35},{8,40},{9,41},{10,42},{11,43},{16,48},... | collective-permute-start | bytes 4718600 | tf_op jit(solution)/shard_map/ppermute | solution.py:38
  130.8 14.4 %collective-permute-start.24 = (s16[144,1536]{1,0:T(8,128)(2,1)}, s16[144,1536]{1,0:T(8,128)(2,1)}, u32[]{:S(2)}, u32[]{:S(2)}) collective-permute-start(s16[144,1536]{1,0:T(8,128)(2,1)} %shard_map.44), channel_id=1, source_target_pairs={{0,64},{1,65},{2,66},{3,67},{8,72},{9,73},{10,74},{11,75},{16,80},... | collective-permute-start | bytes 1327112 | tf_op jit(solution)/shard_map/ppermute | solution.py:38
  146.1 6.3 %collective-permute-start.26 = (f32[256,1536]{1,0:T(8,128)S(1)}, f32[256,1536]{1,0:T(8,128)S(1)}, u32[]{:S(2)}, u32[]{:S(2)}) collective-permute-start(f32[256,1536]{1,0:T(8,128)S(1)} %get-tuple-element.81), channel_id=1, source_target_pairs={{0,32},{1,33},{2,34},{3,35},{8,40},{9,41},{10,42},{11,43},{16,48},... | collective-permute-start | bytes 4718600 | tf_op jit(solution)/shard_map/ppermute | solution.py:38
  146.2 14.6 %collective-permute-start.28 = (s16[144,1536]{1,0:T(8,128)(2,1)S(1)}, s16[144,1536]{1,0:T(8,128)(2,1)S(1)}, u32[]{:S(2)}, u32[]{:S(2)}) collective-permute-start(s16[144,1536]{1,0:T(8,128)(2,1)S(1)} %shard_map.46), channel_id=1, source_target_pairs={{0,64},{1,65},{2,66},{3,67},{8,72},{9,73},{10,74},{11,75},{16,80},... | collective-permute-start | bytes 1327112 | tf_op jit(solution)/shard_map/ppermute | solution.py:38
  152.4 17.4 %copy-start.14 = (f32[256,1536]{1,0:T(8,128)S(1)}, f32[256,1536]{1,0:T(8,128)}, u32[]{:S(2)}) copy-start(f32[256,1536]{1,0:T(8,128)} %copy-done.12) | copy-start | bytes 4718596
  152.5 17.2 %collective-permute-start.27 = (s16[144,1536]{1,0:T(8,128)(2,1)S(1)}, s16[144,1536]{1,0:T(8,128)(2,1)S(1)}, u32[]{:S(2)}, u32[]{:S(2)}) collective-permute-start(s16[144,1536]{1,0:T(8,128)(2,1)S(1)} %shard_map.49), channel_id=1, source_target_pairs={{0,64},{1,65},{2,66},{3,67},{8,72},{9,73},{10,74},{11,75},{16,80},... | collective-permute-start | bytes 1327112 | tf_op jit(solution)/shard_map/ppermute | solution.py:38
  (25 other events, 95.7 us)

commit v5 on v4

--- a/solution.py
+++ b/solution.py
@@ -38,7 +38,7 @@
     return lax.ppermute(value, BOTH, pairs)
 
 
-TILE = 512
+TILE = 768
 
 
 def product_kernel(choices, count, core, *refs):

time: 174 us -> 174 us (level)
  transfers between devices with their start and end apart: 29 -> 29, of which waited for: 16 -> 15; matrix products, arithmetic and copies ran while one was open for 4% -> 4% of each run, Pallas kernels for 28% -> 29%
where the time goes in v5:
time: 174 us; the launch traced here: 173 us
  Pallas kernels  55.9 us (32%)
  waiting for transfers between devices  53.8 us (31%)
  starting transfers between devices  41.8 us (24%)
  local copies, waits for them, and re-layouts  12.4 us (7%)
  other arithmetic  8.54 us (5%)
    ppermute x29, waiting for transfers between devices, send(): return lax.ppermute(value, BOTH, pairs)  53.8 us
    pallas_call x5, Pallas kernels, products(): pl.pallas_call(functools.partial(product_kernel, choices, len(blocks)), g...  48.6 us
    ppermute x29, starting transfers between devices, send(): return lax.ppermute(value, BOTH, pairs)  41.8 us
    unnamed x60, local copies, waits for them, and re-layouts  10.9 us
    pallas_call x4, Pallas kernels, pick(): pl.pallas_call(functools.partial(pick_kernel, spots, len(parts)), in_spec...  4.5 us
  transfers between devices with their start and end apart: 29, of which 15 were waited for; matrix products, arithmetic and copies ran while one was open for 4% of the time, Pallas kernels for 29%

profile of v5, /device:TPU:2, one launch (start us, length us, event | category | flops | bytes accessed | tf_op | source)
XLA Modules:
  0.0 173.0 jit_solution(10967267652555424272)
XLA Ops:
  2.4 3.1 %collective-permute-start.3 = (bf16[64,4096]{1,0:T(8,128)(2,1)S(1)}, bf16[64,4096]{1,0:T(8,128)(2,1)S(1)}, u32[]{:S(2)}, u32[]{:S(2)}) collective-permute-start(bf16[64,4096]{1,0:T(8,128)(2,1)S(1)} %fusion), channel_id=1, source_target_pairs={{0,3},{1,0},{2,1},{3,2},{8,11},{9,8},{10,9},{11,10},{16,19},{17,16... | collective-permute-start | bytes 1572872 | tf_op jit(solution)/shard_map/ppermute | solution.py:38
  5.5 1.9 %collective-permute-start.6 = (bf16[64,4096]{1,0:T(8,128)(2,1)S(1)}, bf16[64,4096]{1,0:T(8,128)(2,1)S(1)}, u32[]{:S(2)}, u32[]{:S(2)}) collective-permute-start(bf16[64,4096]{1,0:T(8,128)(2,1)S(1)} %fusion), channel_id=1, source_target_pairs={{0,8},{1,9},{2,10},{3,11},{8,16},{9,17},{10,18},{11,19},{16,24},{1... | collective-permute-start | bytes 1572872 | tf_op jit(solution)/shard_map/ppermute | solution.py:38
  7.4 2.1 %collective-permute-start.12 = (bf16[64,4096]{1,0:T(8,128)(2,1)S(1)}, bf16[64,4096]{1,0:T(8,128)(2,1)}, u32[]{:S(2)}, u32[]{:S(2)}) collective-permute-start(bf16[64,4096]{1,0:T(8,128)(2,1)S(1)} %fusion), channel_id=1, source_target_pairs={{0,24},{1,25},{2,26},{3,27},{8,0},{9,1},{10,2},{11,3},{16,8},{17,9... | collective-permute-start | bytes 1572872 | tf_op jit(solution)/shard_map/ppermute | solution.py:38
  9.5 6.1 %collective-permute-done = bf16[64,4096]{1,0:T(8,128)(2,1)S(1)} collective-permute-done((bf16[64,4096]{1,0:T(8,128)(2,1)S(1)}, bf16[64,4096]{1,0:T(8,128)(2,1)S(1)}, u32[]{:S(2)}, u32[]{:S(2)}) %collective-permute-start) | collective-permute-done | bytes 524320 | tf_op jit(solution)/shard_map/ppermute | solution.py:38
  15.6 3.0 %collective-permute-start.1 = (bf16[64,4096]{1,0:T(8,128)(2,1)S(1)}, bf16[64,4096]{1,0:T(8,128)(2,1)S(1)}, u32[]{:S(2)}, u32[]{:S(2)}) collective-permute-start(bf16[64,4096]{1,0:T(8,128)(2,1)S(1)} %collective-permute-done), channel_id=1, source_target_pairs={{0,3},{1,0},{2,1},{3,2},{8,11},{9,8},{10,9},{11,10},{16,19},{17,16... | collective-permute-start | bytes 1572872 | tf_op jit(solution)/shard_map/ppermute | solution.py:38
  18.8 2.1 %collective-permute-done.9 = bf16[64,4096]{1,0:T(8,128)(2,1)S(1)} collective-permute-done((bf16[64,4096]{1,0:T(8,128)(2,1)S(1)}, bf16[64,4096]{1,0:T(8,128)(2,1)S(1)}, u32[]{:S(2)}, u32[]{:S(2)}) %collective-permute-start.9) | collective-permute-done | bytes 524320 | tf_op jit(solution)/shard_map/ppermute | solution.py:38
  21.7 3.2 %collective-permute-start.13 = (bf16[64,4096]{1,0:T(8,128)(2,1)S(1)}, bf16[64,4096]{1,0:T(8,128)(2,1)S(1)}, u32[]{:S(2)}, u32[]{:S(2)}) collective-permute-start(bf16[64,4096]{1,0:T(8,128)(2,1)S(1)} %collective-permute-done), channel_id=1, source_target_pairs={{0,24},{1,25},{2,26},{3,27},{8,0},{9,1},{10,2},{11,3},{16,8},{17,9... | collective-permute-start | bytes 1572872 | tf_op jit(solution)/shard_map/ppermute | solution.py:38
  25.0 2.3 %collective-permute-done.1 = bf16[64,4096]{1,0:T(8,128)(2,1)S(1)} collective-permute-done((bf16[64,4096]{1,0:T(8,128)(2,1)S(1)}, bf16[64,4096]{1,0:T(8,128)(2,1)S(1)}, u32[]{:S(2)}, u32[]{:S(2)}) %collective-permute-start.1) | collective-permute-done | bytes 524320 | tf_op jit(solution)/shard_map/ppermute | solution.py:38
  27.3 7.1 %collective-permute-done.10 = bf16[64,4096]{1,0:T(8,128)(2,1)S(1)} collective-permute-done((bf16[64,4096]{1,0:T(8,128)(2,1)S(1)}, bf16[64,4096]{1,0:T(8,128)(2,1)S(1)}, u32[]{:S(2)}, u32[]{:S(2)}) %collective-permute-start.10) | collective-permute-done | bytes 524320 | tf_op jit(solution)/shard_map/ppermute | solution.py:38
  37.0 2.6 %collective-permute-start.5 = (bf16[128,4096]{1,0:T(8,128)(2,1)S(1)}, bf16[128,4096]{1,0:T(8,128)(2,1)S(1)}, u32[]{:S(2)}, u32[]{:S(2)}) collective-permute-start(bf16[128,4096]{1,0:T(8,128)(2,1)S(1)} %constant_dynamic-update-slice_fusion.refs_2_), channel_id=1, source_target_pairs={{0,24},{1,25},{2,26},{3,27},{8,0},{9,1},{10,2},{11,3},{16,8},{17,9... | collective-permute-start | bytes 3145736 | tf_op jit(solution)/shard_map/ppermute | solution.py:38
  39.6 2.1 %collective-permute-start.11 = (bf16[128,4096]{1,0:T(8,128)(2,1)}, bf16[128,4096]{1,0:T(8,128)(2,1)S(1)}, u32[]{:S(2)}, u32[]{:S(2)}) collective-permute-start(bf16[128,4096]{1,0:T(8,128)(2,1)} %constant_dynamic-update-slice_fusion.4.refs_4_), channel_id=1, source_target_pairs={{0,24},{1,25},{2,26},{3,27},{8,0},{9,1},{10,2},{11,3},{16,8},{17,9... | collective-permute-start | bytes 3145736 | tf_op jit(solution)/shard_map/ppermute | solution.py:38
  42.8 2.0 %collective-permute-done.15 = bf16[64,4096]{1,0:T(8,128)(2,1)S(1)} collective-permute-done((bf16[64,4096]{1,0:T(8,128)(2,1)S(1)}, bf16[64,4096]{1,0:T(8,128)(2,1)S(1)}, u32[]{:S(2)}, u32[]{:S(2)}) %collective-permute-start.15) | collective-permute-done | bytes 524320 | tf_op jit(solution)/shard_map/ppermute | solution.py:38
  44.8 13.9 %shard_map.37.refs_0_ = f32[640,1536]{1,0:T(8,128)S(1)} custom-call(s32[1]{0:T(128)} %bitcast.6.core, bf16[128,4096]{1,0:T(8,128)(2,1)S(1)} %pad_maximum_fusion.refs_0_, bf16[128,4096]{1,0:T(8,128)(2,1)S(1)} %pad_maximum_fusion.1.refs_1_, bf16[128,4096]{1,0:T(8,128)(2,1)S(1)} %constant_dynamic-update-slice_fusion.refs_2_, ...), custom_call_target="tpu_custom_call" | custom-call | flops 8053063680 | bytes 21757952 | tf_op jit(solution)/shard_map/pallas_call | solution.py:74
  59.7 4.9 %collective-permute-start.14 = (bf16[128,4096]{1,0:T(8,128)(2,1)}, bf16[128,4096]{1,0:T(8,128)(2,1)}, u32[]{:S(2)}, u32[]{:S(2)}) collective-permute-start(bf16[128,4096]{1,0:T(8,128)(2,1)} %constant_dynamic-update-slice_fusion.4.refs_4_), channel_id=1, source_target_pairs={{0,8},{1,9},{2,10},{3,11},{8,16},{9,17},{10,18},{11,19},{16,24},{1... | collective-permute-start | bytes 3145736 | tf_op jit(solution)/shard_map/ppermute | solution.py:38
  64.6 4.2 %collective-permute-done.11.refs_4_ = bf16[128,4096]{1,0:T(8,128)(2,1)S(1)} collective-permute-done((bf16[128,4096]{1,0:T(8,128)(2,1)}, bf16[128,4096]{1,0:T(8,128)(2,1)S(1)}, u32[]{:S(2)}, u32[]{:S(2)}) %collective-permute-start.11) | collective-permute-done | bytes 1048608 | tf_op jit(solution)/shard_map/ppermute | solution.py:38
  71.5 3.6 %collective-permute-start.16 = (bf16[128,4096]{1,0:T(8,128)(2,1)}, bf16[128,4096]{1,0:T(8,128)(2,1)}, u32[]{:S(2)}, u32[]{:S(2)}) collective-permute-start(bf16[128,4096]{1,0:T(8,128)(2,1)} %get-tuple-element.86), channel_id=1, source_target_pairs={{0,24},{1,25},{2,26},{3,27},{8,0},{9,1},{10,2},{11,3},{16,8},{17,9... | collective-permute-start | bytes 3145736 | tf_op jit(solution)/shard_map/ppermute | solution.py:38
  77.7 10.4 %shard_map.38.refs_1_ = f32[512,1536]{1,0:T(8,128)S(1)} custom-call(s32[1]{0:T(128)} %bitcast.6.core, bf16[128,4096]{1,0:T(8,128)(2,1)S(1)} %collective-permute-done.8.refs_0_.refs_3_, bf16[128,4096]{1,0:T(8,128)(2,1)S(1)} %constant_dynamic-update-slice_fusion.6.refs_1_.refs_2_, bf16[128,4096]{1,0:T(8,128)(2,1)S(1)} %collective-permute-done.5.refs_2_, ...), custom_call_target="tpu_custom_call" | custom-call | flops 6442450944 | bytes 19922944 | tf_op jit(solution)/shard_map/pallas_call | solution.py:74
  89.3 3.3 %collective-permute-start.18 = (bf16[128,4096]{1,0:T(8,128)(2,1)S(1)}, bf16[128,4096]{1,0:T(8,128)(2,1)S(1)}, u32[]{:S(2)}, u32[]{:S(2)}) collective-permute-start(bf16[128,4096]{1,0:T(8,128)(2,1)S(1)} %copy-done.21), channel_id=1, source_target_pairs={{0,24},{1,25},{2,26},{3,27},{8,0},{9,1},{10,2},{11,3},{16,8},{17,9... | collective-permute-start | bytes 3145736 | tf_op jit(solution)/shard_map/ppermute | solution.py:38
  92.6 10.8 %shard_map.40.refs_2_.refs_0_ = f32[384,1536]{1,0:T(8,128)S(1)} custom-call(s32[1]{0:T(128)} %bitcast.6.core, bf16[128,4096]{1,0:T(8,128)(2,1)} %collective-permute-done.16.refs_0_, bf16[128,4096]{1,0:T(8,128)(2,1)} %collective-permute-done.14.refs_1_, bf16[128,4096]{1,0:T(8,128)(2,1)S(1)} %constant_dynamic-update-slice_fusion.6.refs_1_.refs_2_, ...), custom_call_target="tpu_custom_call" | custom-call | flops 4831838208 | bytes 18087936 | tf_op jit(solution)/shard_map/pallas_call | solution.py:74
  103.5 1.9 %collective-permute-done.17.refs_1_ = bf16[128,4096]{1,0:T(8,128)(2,1)S(1)} collective-permute-done((bf16[128,4096]{1,0:T(8,128)(2,1)S(1)}, bf16[128,4096]{1,0:T(8,128)(2,1)S(1)}, u32[]{:S(2)}, u32[]{:S(2)}) %collective-permute-start.17) | collective-permute-done | bytes 1048608 | tf_op jit(solution)/shard_map/ppermute | solution.py:38
  107.1 3.3 %collective-permute-start.21 = (bf16[128,4096]{1,0:T(8,128)(2,1)S(1)}, bf16[128,4096]{1,0:T(8,128)(2,1)S(1)}, u32[]{:S(2)}, u32[]{:S(2)}) collective-permute-start(bf16[128,4096]{1,0:T(8,128)(2,1)S(1)} %copy-done.25), channel_id=1, source_target_pairs={{0,24},{1,25},{2,26},{3,27},{8,0},{9,1},{10,2},{11,3},{16,8},{17,9... | collective-permute-start | bytes 3145736 | tf_op jit(solution)/shard_map/ppermute | solution.py:38
  110.5 2.0 %collective-permute-start.23 = (s16[144,1536]{1,0:T(8,128)(2,1)S(1)}, s16[144,1536]{1,0:T(8,128)(2,1)S(1)}, u32[]{:S(2)}, u32[]{:S(2)}) collective-permute-start(s16[144,1536]{1,0:T(8,128)(2,1)S(1)} %shard_map.41), channel_id=1, source_target_pairs={{0,64},{1,65},{2,66},{3,67},{8,72},{9,73},{10,74},{11,75},{16,80},... | collective-permute-start | bytes 1327112 | tf_op jit(solution)/shard_map/ppermute | solution.py:38
  112.4 6.7 %shard_map.43.refs_3_.refs_1_ = f32[256,1536]{1,0:T(8,128)S(1)} custom-call(s32[1]{0:T(128)} %bitcast.6.core, bf16[128,4096]{1,0:T(8,128)(2,1)S(1)} %collective-permute-done.18.refs_0_, bf16[128,4096]{1,0:T(8,128)(2,1)S(1)} %collective-permute-done.17.refs_1_, bf16[1536,4096]{1,0:T(8,128)(2,1)} %bitcast.47), custom_call_target="tpu_custom_call" | custom-call | flops 3221225472 | bytes 16252928 | tf_op jit(solution)/shard_map/pallas_call | solution.py:74
  119.2 3.6 %collective-permute-done.21.refs_0_ = bf16[128,4096]{1,0:T(8,128)(2,1)S(1)} collective-permute-done((bf16[128,4096]{1,0:T(8,128)(2,1)S(1)}, bf16[128,4096]{1,0:T(8,128)(2,1)S(1)}, u32[]{:S(2)}, u32[]{:S(2)}) %collective-permute-start.21) | collective-permute-done | bytes 1048608 | tf_op jit(solution)/shard_map/ppermute | solution.py:38
  122.8 3.7 %collective-permute-done.20.refs_1_ = bf16[128,4096]{1,0:T(8,128)(2,1)S(1)} collective-permute-done((bf16[128,4096]{1,0:T(8,128)(2,1)S(1)}, bf16[128,4096]{1,0:T(8,128)(2,1)S(1)}, u32[]{:S(2)}, u32[]{:S(2)}) %collective-permute-start.20) | collective-permute-done | bytes 1048608 | tf_op jit(solution)/shard_map/ppermute | solution.py:38
  127.6 1.7 %shard_map.45 = (f32[256,1536]{1,0:T(8,128)}, f32[256,1536]{1,0:T(8,128)S(1)}) custom-call(s32[4]{0:T(128)S(1)} %and_select_fusion.order, f32[640,1536]{1,0:T(8,128)S(1)} %copy-done.1, f32[512,1536]{1,0:T(8,128)S(1)} %shard_map.38.refs_1_, f32[384,1536]{1,0:T(8,128)S(1)} %shard_map.40.refs_2_.refs_0_, f32[256,1536]{1,0:T(8,128)S(1)} %shard_map.43.refs_3_.refs_1_), custom_call_target="tpu_custom_call" | custom-call | bytes 6291456 | tf_op jit(solution)/shard_map/pallas_call | solution.py:108
  130.6 2.0 %collective-permute-start.24 = (s16[144,1536]{1,0:T(8,128)(2,1)}, s16[144,1536]{1,0:T(8,128)(2,1)}, u32[]{:S(2)}, u32[]{:S(2)}) collective-permute-start(s16[144,1536]{1,0:T(8,128)(2,1)} %shard_map.44), channel_id=1, source_target_pairs={{0,64},{1,65},{2,66},{3,67},{8,72},{9,73},{10,74},{11,75},{16,80},... | collective-permute-start | bytes 1327112 | tf_op jit(solution)/shard_map/ppermute | solution.py:38
  132.6 1.8 %collective-permute-done.25.got = f32[256,1536]{1,0:T(8,128)} collective-permute-done((f32[256,1536]{1,0:T(8,128)}, f32[256,1536]{1,0:T(8,128)}, u32[]{:S(2)}, u32[]{:S(2)}) %collective-permute-start.25) | collective-permute-done | bytes 1572896 | tf_op jit(solution)/shard_map/ppermute | solution.py:38
  137.2 6.8 %shard_map.47.refs_2_ = f32[256,1536]{1,0:T(8,128)S(1)} custom-call(s32[1]{0:T(128)} %bitcast.6.core, bf16[128,4096]{1,0:T(8,128)(2,1)S(1)} %collective-permute-done.21.refs_0_, bf16[128,4096]{1,0:T(8,128)(2,1)S(1)} %copy-done.16, bf16[1536,4096]{1,0:T(8,128)(2,1)} %bitcast.48), custom_call_target="tpu_custom_call" | custom-call | flops 3221225472 | bytes 16252928 | tf_op jit(solution)/shard_map/pallas_call | solution.py:74
  146.0 2.1 %collective-permute-start.28 = (s16[144,1536]{1,0:T(8,128)(2,1)S(1)}, s16[144,1536]{1,0:T(8,128)(2,1)S(1)}, u32[]{:S(2)}, u32[]{:S(2)}) collective-permute-start(s16[144,1536]{1,0:T(8,128)(2,1)S(1)} %shard_map.46), channel_id=1, source_target_pairs={{0,64},{1,65},{2,66},{3,67},{8,72},{9,73},{10,74},{11,75},{16,80},... | collective-permute-start | bytes 1327112 | tf_op jit(solution)/shard_map/ppermute | solution.py:38
  154.0 6.5 %collective-permute-done.28 = s16[144,1536]{1,0:T(8,128)(2,1)S(1)} collective-permute-done((s16[144,1536]{1,0:T(8,128)(2,1)S(1)}, s16[144,1536]{1,0:T(8,128)(2,1)S(1)}, u32[]{:S(2)}, u32[]{:S(2)}) %collective-permute-start.28) | collective-permute-done | bytes 442400 | tf_op jit(solution)/shard_map/ppermute | solution.py:38
  160.6 9.0 %collective-permute-done.27 = s16[144,1536]{1,0:T(8,128)(2,1)S(1)} collective-permute-done((s16[144,1536]{1,0:T(8,128)(2,1)S(1)}, s16[144,1536]{1,0:T(8,128)(2,1)S(1)}, u32[]{:S(2)}, u32[]{:S(2)}) %collective-permute-start.27) | collective-permute-done | bytes 442400 | tf_op jit(solution)/shard_map/ppermute | solution.py:38
  (125 shorter events, 32.7 us)
Async XLA Ops:
  1.9 13.7 %collective-permute-start = (bf16[64,4096]{1,0:T(8,128)(2,1)S(1)}, bf16[64,4096]{1,0:T(8,128)(2,1)S(1)}, u32[]{:S(2)}, u32[]{:S(2)}) collective-permute-start(bf16[64,4096]{1,0:T(8,128)(2,1)S(1)} %fusion), channel_id=1, source_target_pairs={{0,4},{1,5},{2,6},{3,7},{8,12},{9,13},{10,14},{11,15},{16,20},{17,... | collective-permute-start | bytes 1572872 | tf_op jit(solution)/shard_map/ppermute | solution.py:38
  2.4 16.3 %collective-permute-start.3 = (bf16[64,4096]{1,0:T(8,128)(2,1)S(1)}, bf16[64,4096]{1,0:T(8,128)(2,1)S(1)}, u32[]{:S(2)}, u32[]{:S(2)}) collective-permute-start(bf16[64,4096]{1,0:T(8,128)(2,1)S(1)} %fusion), channel_id=1, source_target_pairs={{0,3},{1,0},{2,1},{3,2},{8,11},{9,8},{10,9},{11,10},{16,19},{17,16... | collective-permute-start | bytes 1572872 | tf_op jit(solution)/shard_map/ppermute | solution.py:38
  5.5 15.4 %collective-permute-start.9 = (bf16[64,4096]{1,0:T(8,128)(2,1)S(1)}, bf16[64,4096]{1,0:T(8,128)(2,1)S(1)}, u32[]{:S(2)}, u32[]{:S(2)}) collective-permute-start(bf16[64,4096]{1,0:T(8,128)(2,1)S(1)} %fusion), channel_id=1, source_target_pairs={{0,1},{1,2},{2,3},{3,0},{8,9},{9,10},{10,11},{11,8},{16,17},{17,18... | collective-permute-start | bytes 1572872 | tf_op jit(solution)/shard_map/ppermute | solution.py:38
  5.5 16.2 %collective-permute-start.6 = (bf16[64,4096]{1,0:T(8,128)(2,1)S(1)}, bf16[64,4096]{1,0:T(8,128)(2,1)S(1)}, u32[]{:S(2)}, u32[]{:S(2)}) collective-permute-start(bf16[64,4096]{1,0:T(8,128)(2,1)S(1)} %fusion), channel_id=1, source_target_pairs={{0,8},{1,9},{2,10},{3,11},{8,16},{9,17},{10,18},{11,19},{16,24},{1... | collective-permute-start | bytes 1572872 | tf_op jit(solution)/shard_map/ppermute | solution.py:38
  7.4 32.1 %collective-permute-start.12 = (bf16[64,4096]{1,0:T(8,128)(2,1)S(1)}, bf16[64,4096]{1,0:T(8,128)(2,1)}, u32[]{:S(2)}, u32[]{:S(2)}) collective-permute-start(bf16[64,4096]{1,0:T(8,128)(2,1)S(1)} %fusion), channel_id=1, source_target_pairs={{0,24},{1,25},{2,26},{3,27},{8,0},{9,1},{10,2},{11,3},{16,8},{17,9... | collective-permute-start | bytes 1572872 | tf_op jit(solution)/shard_map/ppermute | solution.py:38
  15.6 11.7 %collective-permute-start.1 = (bf16[64,4096]{1,0:T(8,128)(2,1)S(1)}, bf16[64,4096]{1,0:T(8,128)(2,1)S(1)}, u32[]{:S(2)}, u32[]{:S(2)}) collective-permute-start(bf16[64,4096]{1,0:T(8,128)(2,1)S(1)} %collective-permute-done), channel_id=1, source_target_pairs={{0,3},{1,0},{2,1},{3,2},{8,11},{9,8},{10,9},{11,10},{16,19},{17,16... | collective-permute-start | bytes 1572872 | tf_op jit(solution)/shard_map/ppermute | solution.py:38
  18.7 15.7 %collective-permute-start.10 = (bf16[64,4096]{1,0:T(8,128)(2,1)S(1)}, bf16[64,4096]{1,0:T(8,128)(2,1)S(1)}, u32[]{:S(2)}, u32[]{:S(2)}) collective-permute-start(bf16[64,4096]{1,0:T(8,128)(2,1)S(1)} %collective-permute-done), channel_id=1, source_target_pairs={{0,1},{1,2},{2,3},{3,0},{8,9},{9,10},{10,11},{11,8},{16,17},{17,18... | collective-permute-start | bytes 1572872 | tf_op jit(solution)/shard_map/ppermute | solution.py:38
  20.9 16.1 %collective-permute-start.7 = (bf16[64,4096]{1,0:T(8,128)(2,1)S(1)}, bf16[64,4096]{1,0:T(8,128)(2,1)S(1)}, u32[]{:S(2)}, u32[]{:S(2)}) collective-permute-start(bf16[64,4096]{1,0:T(8,128)(2,1)S(1)} %collective-permute-done), channel_id=1, source_target_pairs={{0,8},{1,9},{2,10},{3,11},{8,16},{9,17},{10,18},{11,19},{16,24},{1... | collective-permute-start | bytes 1572872 | tf_op jit(solution)/shard_map/ppermute | solution.py:38
  21.7 19.9 %collective-permute-start.13 = (bf16[64,4096]{1,0:T(8,128)(2,1)S(1)}, bf16[64,4096]{1,0:T(8,128)(2,1)S(1)}, u32[]{:S(2)}, u32[]{:S(2)}) collective-permute-start(bf16[64,4096]{1,0:T(8,128)(2,1)S(1)} %collective-permute-done), channel_id=1, source_target_pairs={{0,24},{1,25},{2,26},{3,27},{8,0},{9,1},{10,2},{11,3},{16,8},{17,9... | collective-permute-start | bytes 1572872 | tf_op jit(solution)/shard_map/ppermute | solution.py:38
  27.3 17.5 %collective-permute-start.15 = (bf16[64,4096]{1,0:T(8,128)(2,1)S(1)}, bf16[64,4096]{1,0:T(8,128)(2,1)S(1)}, u32[]{:S(2)}, u32[]{:S(2)}) collective-permute-start(bf16[64,4096]{1,0:T(8,128)(2,1)S(1)} %collective-permute-done.9), channel_id=1, source_target_pairs={{0,1},{1,2},{2,3},{3,0},{8,9},{9,10},{10,11},{11,8},{16,17},{17,18... | collective-permute-start | bytes 1572872 | tf_op jit(solution)/shard_map/ppermute | solution.py:38
  34.4 34.4 %collective-permute-start.4 = (bf16[128,4096]{1,0:T(8,128)(2,1)S(1)}, bf16[128,4096]{1,0:T(8,128)(2,1)S(1)}, u32[]{:S(2)}, u32[]{:S(2)}) collective-permute-start(bf16[128,4096]{1,0:T(8,128)(2,1)S(1)} %constant_dynamic-update-slice_fusion.refs_2_), channel_id=1, source_target_pairs={{0,8},{1,9},{2,10},{3,11},{8,16},{9,17},{10,18},{11,19},{16,24},{1... | collective-permute-start | bytes 3145736 | tf_op jit(solution)/shard_map/ppermute | solution.py:38
  37.0 32.9 %collective-permute-start.5 = (bf16[128,4096]{1,0:T(8,128)(2,1)S(1)}, bf16[128,4096]{1,0:T(8,128)(2,1)S(1)}, u32[]{:S(2)}, u32[]{:S(2)}) collective-permute-start(bf16[128,4096]{1,0:T(8,128)(2,1)S(1)} %constant_dynamic-update-slice_fusion.refs_2_), channel_id=1, source_target_pairs={{0,24},{1,25},{2,26},{3,27},{8,0},{9,1},{10,2},{11,3},{16,8},{17,9... | collective-permute-start | bytes 3145736 | tf_op jit(solution)/shard_map/ppermute | solution.py:38
  39.6 29.2 %collective-permute-start.11 = (bf16[128,4096]{1,0:T(8,128)(2,1)}, bf16[128,4096]{1,0:T(8,128)(2,1)S(1)}, u32[]{:S(2)}, u32[]{:S(2)}) collective-permute-start(bf16[128,4096]{1,0:T(8,128)(2,1)} %constant_dynamic-update-slice_fusion.4.refs_4_), channel_id=1, source_target_pairs={{0,24},{1,25},{2,26},{3,27},{8,0},{9,1},{10,2},{11,3},{16,8},{17,9... | collective-permute-start | bytes 3145736 | tf_op jit(solution)/shard_map/ppermute | solution.py:38
  41.7 28.2 %collective-permute-start.8 = (bf16[128,4096]{1,0:T(8,128)(2,1)S(1)}, bf16[128,4096]{1,0:T(8,128)(2,1)S(1)}, u32[]{:S(2)}, u32[]{:S(2)}) collective-permute-start(bf16[128,4096]{1,0:T(8,128)(2,1)S(1)} %constant_dynamic-update-slice_fusion.2.refs_3_), channel_id=1, source_target_pairs={{0,8},{1,9},{2,10},{3,11},{8,16},{9,17},{10,18},{11,19},{16,24},{1... | collective-permute-start | bytes 3145736 | tf_op jit(solution)/shard_map/ppermute | solution.py:38
  44.8 14.9 %collective-permute-start.2 = (bf16[64,4096]{1,0:T(8,128)(2,1)S(1)}, bf16[64,4096]{1,0:T(8,128)(2,1)S(1)}, u32[]{:S(2)}, u32[]{:S(2)}) collective-permute-start(bf16[64,4096]{1,0:T(8,128)(2,1)S(1)} %collective-permute-done.1), channel_id=1, source_target_pairs={{0,3},{1,0},{2,1},{3,2},{8,11},{9,8},{10,9},{11,10},{16,19},{17,16... | collective-permute-start | bytes 1572872 | tf_op jit(solution)/shard_map/ppermute | solution.py:38
  59.7 28.4 %collective-permute-start.14 = (bf16[128,4096]{1,0:T(8,128)(2,1)}, bf16[128,4096]{1,0:T(8,128)(2,1)}, u32[]{:S(2)}, u32[]{:S(2)}) collective-permute-start(bf16[128,4096]{1,0:T(8,128)(2,1)} %constant_dynamic-update-slice_fusion.4.refs_4_), channel_id=1, source_target_pairs={{0,8},{1,9},{2,10},{3,11},{8,16},{9,17},{10,18},{11,19},{16,24},{1... | collective-permute-start | bytes 3145736 | tf_op jit(solution)/shard_map/ppermute | solution.py:38
  71.5 16.6 %collective-permute-start.16 = (bf16[128,4096]{1,0:T(8,128)(2,1)}, bf16[128,4096]{1,0:T(8,128)(2,1)}, u32[]{:S(2)}, u32[]{:S(2)}) collective-permute-start(bf16[128,4096]{1,0:T(8,128)(2,1)} %get-tuple-element.86), channel_id=1, source_target_pairs={{0,24},{1,25},{2,26},{3,27},{8,0},{9,1},{10,2},{11,3},{16,8},{17,9... | collective-permute-start | bytes 3145736 | tf_op jit(solution)/shard_map/ppermute | solution.py:38
  89.0 16.3 %copy-start.4 = (f32[256,1536]{1,0:T(8,128)}, f32[256,1536]{1,0:T(8,128)S(1)}, u32[]{:S(2)}) copy-start(f32[256,1536]{1,0:T(8,128)S(1)} %get-tuple-element.52.kept) | copy-start | bytes 4718596
  89.1 16.3 %collective-permute-start.19 = (f32[256,1536]{1,0:T(8,128)S(1)}, f32[256,1536]{1,0:T(8,128)S(1)}, u32[]{:S(2)}, u32[]{:S(2)}) collective-permute-start(f32[256,1536]{1,0:T(8,128)S(1)} %get-tuple-element.53), channel_id=1, source_target_pairs={{0,32},{1,33},{2,34},{3,35},{8,40},{9,41},{10,42},{11,43},{16,48},... | collective-permute-start | bytes 4718600 | tf_op jit(solution)/shard_map/ppermute | solution.py:38
  89.1 16.2 %collective-permute-start.17 = (bf16[128,4096]{1,0:T(8,128)(2,1)S(1)}, bf16[128,4096]{1,0:T(8,128)(2,1)S(1)}, u32[]{:S(2)}, u32[]{:S(2)}) collective-permute-start(bf16[128,4096]{1,0:T(8,128)(2,1)S(1)} %constant_dynamic-update-slice_fusion.6.refs_1_.refs_2_), channel_id=1, source_target_pairs={{0,8},{1,9},{2,10},{3,11},{8,16},{9,17},{10,18},{11,19},{16,24},{1... | collective-permute-start | bytes 3145736 | tf_op jit(solution)/shard_map/ppermute | solution.py:38
  89.3 16.0 %collective-permute-start.18 = (bf16[128,4096]{1,0:T(8,128)(2,1)S(1)}, bf16[128,4096]{1,0:T(8,128)(2,1)S(1)}, u32[]{:S(2)}, u32[]{:S(2)}) collective-permute-start(bf16[128,4096]{1,0:T(8,128)(2,1)S(1)} %copy-done.21), channel_id=1, source_target_pairs={{0,24},{1,25},{2,26},{3,27},{8,0},{9,1},{10,2},{11,3},{16,8},{17,9... | collective-permute-start | bytes 3145736 | tf_op jit(solution)/shard_map/ppermute | solution.py:38
  106.5 20.0 %copy-start.8 = (f32[256,1536]{1,0:T(8,128)}, f32[256,1536]{1,0:T(8,128)S(1)}, u32[]{:S(2)}) copy-start(f32[256,1536]{1,0:T(8,128)S(1)} %get-tuple-element.59.kept) | copy-start | bytes 4718596
  106.5 20.0 %collective-permute-start.22 = (f32[256,1536]{1,0:T(8,128)S(1)}, f32[256,1536]{1,0:T(8,128)S(1)}, u32[]{:S(2)}, u32[]{:S(2)}) collective-permute-start(f32[256,1536]{1,0:T(8,128)S(1)} %get-tuple-element.61), channel_id=1, source_target_pairs={{0,32},{1,33},{2,34},{3,35},{8,40},{9,41},{10,42},{11,43},{16,48},... | collective-permute-start | bytes 4718600 | tf_op jit(solution)/shard_map/ppermute | solution.py:38
  107.1 15.6 %collective-permute-start.21 = (bf16[128,4096]{1,0:T(8,128)(2,1)S(1)}, bf16[128,4096]{1,0:T(8,128)(2,1)S(1)}, u32[]{:S(2)}, u32[]{:S(2)}) collective-permute-start(bf16[128,4096]{1,0:T(8,128)(2,1)S(1)} %copy-done.25), channel_id=1, source_target_pairs={{0,24},{1,25},{2,26},{3,27},{8,0},{9,1},{10,2},{11,3},{16,8},{17,9... | collective-permute-start | bytes 3145736 | tf_op jit(solution)/shard_map/ppermute | solution.py:38
  110.5 16.0 %collective-permute-start.20 = (bf16[128,4096]{1,0:T(8,128)(2,1)S(1)}, bf16[128,4096]{1,0:T(8,128)(2,1)S(1)}, u32[]{:S(2)}, u32[]{:S(2)}) collective-permute-start(bf16[128,4096]{1,0:T(8,128)(2,1)S(1)} %collective-permute-done.17.refs_1_), channel_id=1, source_target_pairs={{0,8},{1,9},{2,10},{3,11},{8,16},{9,17},{10,18},{11,19},{16,24},{1... | collective-permute-start | bytes 3145736 | tf_op jit(solution)/shard_map/ppermute | solution.py:38
  110.5 12.3 %collective-permute-start.23 = (s16[144,1536]{1,0:T(8,128)(2,1)S(1)}, s16[144,1536]{1,0:T(8,128)(2,1)S(1)}, u32[]{:S(2)}, u32[]{:S(2)}) collective-permute-start(s16[144,1536]{1,0:T(8,128)(2,1)S(1)} %shard_map.41), channel_id=1, source_target_pairs={{0,64},{1,65},{2,66},{3,67},{8,72},{9,73},{10,74},{11,75},{16,80},... | collective-permute-start | bytes 1327112 | tf_op jit(solution)/shard_map/ppermute | solution.py:38
  130.6 3.8 %collective-permute-start.25 = (f32[256,1536]{1,0:T(8,128)}, f32[256,1536]{1,0:T(8,128)}, u32[]{:S(2)}, u32[]{:S(2)}) collective-permute-start(f32[256,1536]{1,0:T(8,128)} %get-tuple-element.73), channel_id=1, source_target_pairs={{0,32},{1,33},{2,34},{3,35},{8,40},{9,41},{10,42},{11,43},{16,48},... | collective-permute-start | bytes 4718600 | tf_op jit(solution)/shard_map/ppermute | solution.py:38
  130.6 14.4 %collective-permute-start.24 = (s16[144,1536]{1,0:T(8,128)(2,1)}, s16[144,1536]{1,0:T(8,128)(2,1)}, u32[]{:S(2)}, u32[]{:S(2)}) collective-permute-start(s16[144,1536]{1,0:T(8,128)(2,1)} %shard_map.44), channel_id=1, source_target_pairs={{0,64},{1,65},{2,66},{3,67},{8,72},{9,73},{10,74},{11,75},{16,80},... | collective-permute-start | bytes 1327112 | tf_op jit(solution)/shard_map/ppermute | solution.py:38
  145.9 6.3 %collective-permute-start.26 = (f32[256,1536]{1,0:T(8,128)S(1)}, f32[256,1536]{1,0:T(8,128)S(1)}, u32[]{:S(2)}, u32[]{:S(2)}) collective-permute-start(f32[256,1536]{1,0:T(8,128)S(1)} %get-tuple-element.81), channel_id=1, source_target_pairs={{0,32},{1,33},{2,34},{3,35},{8,40},{9,41},{10,42},{11,43},{16,48},... | collective-permute-start | bytes 4718600 | tf_op jit(solution)/shard_map/ppermute | solution.py:38
  146.0 14.6 %collective-permute-start.28 = (s16[144,1536]{1,0:T(8,128)(2,1)S(1)}, s16[144,1536]{1,0:T(8,128)(2,1)S(1)}, u32[]{:S(2)}, u32[]{:S(2)}) collective-permute-start(s16[144,1536]{1,0:T(8,128)(2,1)S(1)} %shard_map.46), channel_id=1, source_target_pairs={{0,64},{1,65},{2,66},{3,67},{8,72},{9,73},{10,74},{11,75},{16,80},... | collective-permute-start | bytes 1327112 | tf_op jit(solution)/shard_map/ppermute | solution.py:38
  152.2 17.4 %copy-start.14 = (f32[256,1536]{1,0:T(8,128)S(1)}, f32[256,1536]{1,0:T(8,128)}, u32[]{:S(2)}) copy-start(f32[256,1536]{1,0:T(8,128)} %copy-done.12) | copy-start | bytes 4718596
  152.4 17.2 %collective-permute-start.27 = (s16[144,1536]{1,0:T(8,128)(2,1)S(1)}, s16[144,1536]{1,0:T(8,128)(2,1)S(1)}, u32[]{:S(2)}, u32[]{:S(2)}) collective-permute-start(s16[144,1536]{1,0:T(8,128)(2,1)S(1)} %shard_map.49), channel_id=1, source_target_pairs={{0,64},{1,65},{2,66},{3,67},{8,72},{9,73},{10,74},{11,75},{16,80},... | collective-permute-start | bytes 1327112 | tf_op jit(solution)/shard_map/ppermute | solution.py:38
  (25 other events, 96.4 us)
